TPU v7x, 32 devices: a whole 2x2x4 slice. The times are simulated.
32 devices in a mesh: dp: 8 (over z, x), fsdp: 4 (over y, core).
Axes of the slice: x: 2, y: 2, z: 4, core: 2. Of those that a mesh axis runs over, the one named last changes fastest.
Arguments:
- tokens: bfloat16 [32, 256, 2048], P(('dp', 'fsdp')), may hold values from -6 to 6
- group_ids: int32 [32], P(('dp', 'fsdp')), may hold values from 0 to 7
- seq_weights: int32 [32], P(('dp', 'fsdp')), may hold values from 1 to 4
- cotangent: bfloat16 [32, 256, 2048], P(('dp', 'fsdp')), may hold values from -6 to 6
- attn_gain: bfloat16 [2048], P(('dp', 'fsdp')), may hold values from 0.5 to 1.5
- w_query: bfloat16 [2048, 2048], P(('dp', 'fsdp')), may hold values from -0.125 to 0.125
- w_key: bfloat16 [2048, 2048], P(('dp', 'fsdp')), may hold values from -0.125 to 0.125
- w_value: bfloat16 [2048, 2048], P(('dp', 'fsdp')), may hold values from -0.125 to 0.125
- w_gate: bfloat16 [2048, 2048], P(('dp', 'fsdp')), may hold values from -0.125 to 0.125
- w_beta: bfloat16 [2048, 16], P(('dp', 'fsdp')), may hold values from -0.125 to 0.125
- conv_query: bfloat16 [4, 2048], P(None, ('dp', 'fsdp')), may hold values from -3 to 3
- conv_key: bfloat16 [4, 2048], P(None, ('dp', 'fsdp')), may hold values from -3 to 3
- conv_value: bfloat16 [4, 2048], P(None, ('dp', 'fsdp')), may hold values from -3 to 3
- head_gain: bfloat16 [128], P(('dp', 'fsdp')), may hold values from 0.5 to 1.5
- w_out: bfloat16 [2048, 2048], P(('dp', 'fsdp')), may hold values from -0.1875 to 0.1875
- mlp_gain: bfloat16 [2048], P(('dp', 'fsdp')), may hold values from 0.5 to 1.5
- w_ffgate: bfloat16 [2048, 5632], P(('dp', 'fsdp')), may hold values from -0.125 to 0.125
- w_ffup: bfloat16 [2048, 5632], P(('dp', 'fsdp')), may hold values from -0.125 to 0.125
- w_ffdown: bfloat16 [5632, 2048], P(('dp', 'fsdp')), may hold values from -0.078125 to 0.078125
Outputs:
- mixed: bfloat16 [32, 256, 2048], P(('dp', 'fsdp'))
- input_grad: float32 [32, 256, 2048], P(('dp', 'fsdp'))
- grad_attn_gain: float32 [2048], P(('dp', 'fsdp'))
- grad_query: float32 [2048, 2048], P(('dp', 'fsdp'))
- grad_key: float32 [2048, 2048], P(('dp', 'fsdp'))
- grad_value: float32 [2048, 2048], P(('dp', 'fsdp'))
- grad_gate: float32 [2048, 2048], P(('dp', 'fsdp'))
- grad_beta: float32 [2048, 16], P(('dp', 'fsdp'))
- grad_conv_query: float32 [4, 2048], P(None, ('dp', 'fsdp'))
- grad_conv_key: float32 [4, 2048], P(None, ('dp', 'fsdp'))
- grad_conv_value: float32 [4, 2048], P(None, ('dp', 'fsdp'))
- grad_head_gain: float32 [128], P(('dp', 'fsdp'))
- grad_out: float32 [2048, 2048], P(('dp', 'fsdp'))
- grad_mlp_gain: float32 [2048], P(('dp', 'fsdp'))
- grad_ffgate: float32 [2048, 5632], P(('dp', 'fsdp'))
- grad_ffup: float32 [2048, 5632], P(('dp', 'fsdp'))
- grad_ffdown: float32 [5632, 2048], P(('dp', 'fsdp'))
All inputs are finite; a program needn't handle non-finite values.
Results may differ from a plain program's by a relative error of at most 0.012.
Values may be sent and summed in bfloat16 or wider, within the bound.
No kernel may reach another device: no remote copies, remote signals or barrier semaphores. Data moves between devices by JAX's collectives and lax.ppermute only.
A program may use at most 512 MiB of HBM per device.

v0:
```python
import jax
import jax.numpy as jnp
from jax import lax
from jax.sharding import PartitionSpec as P

BLOCK = 64
GROUPS = 8


EPS = 1e-06
HIGHEST = lax.Precision.HIGHEST


def rounded(value):
    shortened = lax.optimization_barrier(value.astype(jnp.bfloat16)).astype(jnp.float32)
    return value + lax.stop_gradient(shortened - value)


def rms_scale(value, gain):
    return value * lax.rsqrt(jnp.mean(value * value, axis=-1, keepdims=True) + EPS) * gain


def short_conv(projected, taps):
    total = taps[0] * projected
    for offset in range(1, taps.shape[0]):
        moved = jnp.pad(projected, ((offset, 0), (0, 0)))[:-offset]
        total = total + taps[offset] * moved
    return jax.nn.silu(total)


def unit_inverse(strict):
    count = strict.shape[-1]
    power = -strict
    result = jnp.eye(count, dtype=strict.dtype) + power
    for repeat in range(count.bit_length() - 2):
        power = jnp.einsum("hij,hjk->hik", power, power, precision=HIGHEST)
        result = result + jnp.einsum("hij,hjk->hik", result, power, precision=HIGHEST)
    return result


def block_step(state, pieces):
    query_blk, key_blk, value_blk, beta_blk = pieces
    count = query_blk.shape[1]
    row_ids = jnp.arange(count)
    strictly = row_ids[:, None] > row_ids[None, :]
    inclusive = row_ids[:, None] >= row_ids[None, :]
    key_beta = key_blk * beta_blk[..., None]
    strict = jnp.where(
        strictly, jnp.einsum("hcd,hed->hce", key_beta, key_blk, precision=HIGHEST), 0.0
    )
    inverse = unit_inverse(strict)
    weight_mat = jnp.einsum("hce,hed->hcd", inverse, key_beta, precision=HIGHEST)
    update_mat = jnp.einsum(
        "hce,hed->hcd", inverse, value_blk * beta_blk[..., None], precision=HIGHEST
    )
    fresh = update_mat - jnp.einsum("hcd,hde->hce", weight_mat, state, precision=HIGHEST)
    scores = jnp.where(
        inclusive, jnp.einsum("hcd,hed->hce", query_blk, key_blk, precision=HIGHEST), 0.0
    )
    result = jnp.einsum("hcd,hde->hce", query_blk, state, precision=HIGHEST)
    result = result + jnp.einsum("hce,hev->hcv", scores, fresh, precision=HIGHEST)
    state = state + jnp.einsum("hcd,hcv->hdv", key_blk, fresh, precision=HIGHEST)
    return (state, result)


def delta_rule(query, key, value, beta):
    length, heads, head_size = query.shape
    number = length // BLOCK

    def arrange(item):
        return item.reshape(number, BLOCK, heads, head_size).transpose(0, 2, 1, 3)

    stacked = (
        arrange(query),
        arrange(key),
        arrange(value),
        beta.reshape(number, BLOCK, heads).transpose(0, 2, 1),
    )
    start = jnp.zeros((heads, head_size, head_size), jnp.float32)
    final, results = lax.scan(jax.checkpoint(block_step), start, stacked)
    return results.transpose(0, 2, 1, 3).reshape(length, heads, head_size)


def mix_heads(
    query_pre, key_pre, value_pre, gate_pre, beta_pre, conv_query, conv_key, conv_value, head_gain
):
    length = query_pre.shape[0]
    heads = beta_pre.shape[1]
    head_size = head_gain.shape[0]

    def split(item):
        return item.reshape(length, heads, head_size)

    query = split(short_conv(query_pre, conv_query))
    query = rounded(
        query
        * lax.rsqrt(jnp.sum(query * query, axis=-1, keepdims=True) + EPS)
        * head_size ** (-0.5)
    )
    key = split(short_conv(key_pre, conv_key))
    key = rounded(key * lax.rsqrt(jnp.sum(key * key, axis=-1, keepdims=True) + EPS))
    value = rounded(split(short_conv(value_pre, conv_value)))
    beta = jax.nn.sigmoid(beta_pre)
    mixer = delta_rule(query, key, value, beta)
    gated = rms_scale(mixer, head_gain) * jax.nn.silu(split(gate_pre))
    return gated.reshape(length, heads * head_size)


def matmul(left, right):
    return jnp.dot(left, right, preferred_element_type=jnp.float32)


def weight_grad(left, right):
    return jnp.einsum("ra,rb->ab", left, right, preferred_element_type=jnp.float32)


def back_grad(grad, weight):
    return jnp.einsum("rb,ab->ra", grad, weight, preferred_element_type=jnp.float32)


def on_device(
    tokens,
    group_ids,
    seq_weights,
    cotangent,
    attn_gain,
    w_query,
    w_key,
    w_value,
    w_gate,
    w_beta,
    conv_query,
    conv_key,
    conv_value,
    head_gain,
    w_out,
    mlp_gain,
    w_ffgate,
    w_ffup,
    w_ffdown,
):
    seqs, length, width = tokens.shape
    total_rows = seqs * length
    devices = lax.axis_size(("dp", "fsdp"))
    labels = jnp.arange(GROUPS)
    hits = group_ids[:, None] == labels[None, :]
    local_hits = jnp.sum(hits.astype(jnp.int32), axis=0)
    seq_count = lax.psum(local_hits, ("dp", "fsdp"))
    token_count = length * seq_count
    own_count = jnp.sum(jnp.where(hits, token_count[None, :], 0), axis=1)
    factor = (
        seq_weights.astype(jnp.float32)
        * (devices * seqs * length)
        / (GROUPS * own_count.astype(jnp.float32))
    )
    attn_full = (
        lax.all_gather(attn_gain, ("dp", "fsdp"), axis=0, tiled=True),
        lax.all_gather(w_query, ("dp", "fsdp"), axis=0, tiled=True),
        lax.all_gather(w_key, ("dp", "fsdp"), axis=0, tiled=True),
        lax.all_gather(w_value, ("dp", "fsdp"), axis=0, tiled=True),
        lax.all_gather(w_gate, ("dp", "fsdp"), axis=0, tiled=True),
        lax.all_gather(w_beta, ("dp", "fsdp"), axis=0, tiled=True),
        lax.all_gather(conv_query, ("dp", "fsdp"), axis=1, tiled=True),
        lax.all_gather(conv_key, ("dp", "fsdp"), axis=1, tiled=True),
        lax.all_gather(conv_value, ("dp", "fsdp"), axis=1, tiled=True),
        lax.all_gather(head_gain, ("dp", "fsdp"), axis=0, tiled=True),
        lax.all_gather(w_out, ("dp", "fsdp"), axis=0, tiled=True),
    )
    (
        gain_one,
        query_w,
        key_w,
        value_w,
        gate_w,
        beta_w,
        taps_query,
        taps_key,
        taps_value,
        gain_head,
        out_w,
    ) = attn_full
    small_params = (
        taps_query.astype(jnp.float32),
        taps_key.astype(jnp.float32),
        taps_value.astype(jnp.float32),
        gain_head.astype(jnp.float32),
    )
    gain_first = gain_one.astype(jnp.float32)
    inputs = tokens.reshape(total_rows, width).astype(jnp.float32)
    normed = rms_scale(inputs, gain_first).astype(jnp.bfloat16)
    query_pre = matmul(normed, query_w)
    key_pre = matmul(normed, key_w)
    value_pre = matmul(normed, value_w)
    gate_pre = matmul(normed, gate_w)
    beta_pre = matmul(normed, beta_w)

    def shaped(item):
        return item.reshape(seqs, length, item.shape[-1])

    mixing = jax.vmap(mix_heads, in_axes=(0, 0, 0, 0, 0, None, None, None, None))
    pre_list = (
        shaped(query_pre),
        shaped(key_pre),
        shaped(value_pre),
        shaped(gate_pre),
        shaped(beta_pre),
    )
    gated = mixing(*pre_list, *small_params).reshape(total_rows, width).astype(jnp.bfloat16)
    resid = inputs + matmul(gated, out_w)
    mlp_full = (
        lax.all_gather(mlp_gain, ("dp", "fsdp"), axis=0, tiled=True),
        lax.all_gather(w_ffgate, ("dp", "fsdp"), axis=0, tiled=True),
        lax.all_gather(w_ffup, ("dp", "fsdp"), axis=0, tiled=True),
        lax.all_gather(w_ffdown, ("dp", "fsdp"), axis=0, tiled=True),
    )
    gain_two, ffgate_w, ffup_w, ffdown_w = mlp_full
    gain_second = gain_two.astype(jnp.float32)
    normed2 = rms_scale(resid, gain_second).astype(jnp.bfloat16)
    gate_ff = matmul(normed2, ffgate_w)
    up_ff = matmul(normed2, ffup_w)
    silu_gate = jax.nn.silu(gate_ff)
    hidden = (silu_gate * up_ff).astype(jnp.bfloat16)
    final = resid + matmul(hidden, ffdown_w)
    mixed = final.astype(jnp.bfloat16).reshape(seqs, length, width)
    mlp_back = (
        lax.all_gather(mlp_gain, ("dp", "fsdp"), axis=0, tiled=True),
        lax.all_gather(w_ffgate, ("dp", "fsdp"), axis=0, tiled=True),
        lax.all_gather(w_ffup, ("dp", "fsdp"), axis=0, tiled=True),
        lax.all_gather(w_ffdown, ("dp", "fsdp"), axis=0, tiled=True),
    )
    back_ffgate, back_ffup, back_ffdown = (mlp_back[1], mlp_back[2], mlp_back[3])
    row_factor = jnp.repeat(factor, length)[:, None]
    d_final = cotangent.reshape(total_rows, width).astype(jnp.float32) * row_factor
    d_down = d_final.astype(jnp.bfloat16)
    grad_ffdown = weight_grad(hidden, d_down)
    d_hidden = back_grad(d_down, back_ffdown)
    sigmoid_gate = jax.nn.sigmoid(gate_ff)
    silu_slope = sigmoid_gate + gate_ff * sigmoid_gate * (1.0 - sigmoid_gate)
    d_gate = (d_hidden * up_ff * silu_slope).astype(jnp.bfloat16)
    d_up = (d_hidden * silu_gate).astype(jnp.bfloat16)
    grad_ffgate = weight_grad(normed2, d_gate)
    grad_ffup = weight_grad(normed2, d_up)
    d_normed2 = back_grad(d_gate, back_ffgate) + back_grad(d_up, back_ffup)
    unused_second, norm_pull = jax.vjp(rms_scale, resid, gain_second)
    d_resid_part, grad_mlp_gain = norm_pull(d_normed2)
    d_resid = d_final + d_resid_part
    mlp_sums = (
        lax.psum_scatter(grad_mlp_gain, ("dp", "fsdp"), scatter_dimension=0, tiled=True),
        lax.psum_scatter(grad_ffgate, ("dp", "fsdp"), scatter_dimension=0, tiled=True),
        lax.psum_scatter(grad_ffup, ("dp", "fsdp"), scatter_dimension=0, tiled=True),
        lax.psum_scatter(grad_ffdown, ("dp", "fsdp"), scatter_dimension=0, tiled=True),
    )
    attn_back = (
        lax.all_gather(attn_gain, ("dp", "fsdp"), axis=0, tiled=True),
        lax.all_gather(w_query, ("dp", "fsdp"), axis=0, tiled=True),
        lax.all_gather(w_key, ("dp", "fsdp"), axis=0, tiled=True),
        lax.all_gather(w_value, ("dp", "fsdp"), axis=0, tiled=True),
        lax.all_gather(w_gate, ("dp", "fsdp"), axis=0, tiled=True),
        lax.all_gather(w_beta, ("dp", "fsdp"), axis=0, tiled=True),
        lax.all_gather(conv_query, ("dp", "fsdp"), axis=1, tiled=True),
        lax.all_gather(conv_key, ("dp", "fsdp"), axis=1, tiled=True),
        lax.all_gather(conv_value, ("dp", "fsdp"), axis=1, tiled=True),
        lax.all_gather(head_gain, ("dp", "fsdp"), axis=0, tiled=True),
        lax.all_gather(w_out, ("dp", "fsdp"), axis=0, tiled=True),
    )
    back_query, back_key, back_value, back_gate, back_beta = (
        attn_back[1],
        attn_back[2],
        attn_back[3],
        attn_back[4],
        attn_back[5],
    )
    back_out = attn_back[10]
    d_branch = d_resid.astype(jnp.bfloat16)
    grad_out = weight_grad(gated, d_branch)
    d_gated = back_grad(d_branch, back_out)
    unused_mix, mix_pull = jax.vjp(mixing, *pre_list, *small_params)
    mix_grads = mix_pull(d_gated.reshape(seqs, length, width))
    d_query = mix_grads[0].reshape(total_rows, -1).astype(jnp.bfloat16)
    d_key = mix_grads[1].reshape(total_rows, -1).astype(jnp.bfloat16)
    d_value = mix_grads[2].reshape(total_rows, -1).astype(jnp.bfloat16)
    d_gatepre = mix_grads[3].reshape(total_rows, -1).astype(jnp.bfloat16)
    d_betapre = mix_grads[4].reshape(total_rows, -1).astype(jnp.bfloat16)
    grad_query = weight_grad(normed, d_query)
    grad_key = weight_grad(normed, d_key)
    grad_value = weight_grad(normed, d_value)
    grad_gate = weight_grad(normed, d_gatepre)
    grad_beta = weight_grad(normed, d_betapre)
    d_normed = (
        back_grad(d_query, back_query) + back_grad(d_key, back_key) + back_grad(d_value, back_value)
    )
    d_normed = d_normed + back_grad(d_gatepre, back_gate) + back_grad(d_betapre, back_beta)
    unused_first, first_pull = jax.vjp(rms_scale, inputs, gain_first)
    d_inputs_part, grad_attn_gain = first_pull(d_normed)
    input_grad = (d_resid + d_inputs_part).reshape(seqs, length, width)
    attn_sums = (
        lax.psum_scatter(grad_attn_gain, ("dp", "fsdp"), scatter_dimension=0, tiled=True),
        lax.psum_scatter(grad_query, ("dp", "fsdp"), scatter_dimension=0, tiled=True),
        lax.psum_scatter(grad_key, ("dp", "fsdp"), scatter_dimension=0, tiled=True),
        lax.psum_scatter(grad_value, ("dp", "fsdp"), scatter_dimension=0, tiled=True),
        lax.psum_scatter(grad_gate, ("dp", "fsdp"), scatter_dimension=0, tiled=True),
        lax.psum_scatter(grad_beta, ("dp", "fsdp"), scatter_dimension=0, tiled=True),
        lax.psum_scatter(mix_grads[5], ("dp", "fsdp"), scatter_dimension=1, tiled=True),
        lax.psum_scatter(mix_grads[6], ("dp", "fsdp"), scatter_dimension=1, tiled=True),
        lax.psum_scatter(mix_grads[7], ("dp", "fsdp"), scatter_dimension=1, tiled=True),
        lax.psum_scatter(mix_grads[8], ("dp", "fsdp"), scatter_dimension=0, tiled=True),
        lax.psum_scatter(grad_out, ("dp", "fsdp"), scatter_dimension=0, tiled=True),
    )
    return (
        mixed,
        input_grad,
        attn_sums[0],
        attn_sums[1],
        attn_sums[2],
        attn_sums[3],
        attn_sums[4],
        attn_sums[5],
        attn_sums[6],
        attn_sums[7],
        attn_sums[8],
        attn_sums[9],
        attn_sums[10],
        mlp_sums[0],
        mlp_sums[1],
        mlp_sums[2],
        mlp_sums[3],
    )


def solution(mesh):
    placed = (
        P(("dp", "fsdp"), None, None),
        P(("dp", "fsdp")),
        P(("dp", "fsdp")),
        P(("dp", "fsdp"), None, None),
        P(("dp", "fsdp")),
        P(("dp", "fsdp"), None),
        P(("dp", "fsdp"), None),
        P(("dp", "fsdp"), None),
        P(("dp", "fsdp"), None),
        P(("dp", "fsdp"), None),
        P(None, ("dp", "fsdp")),
        P(None, ("dp", "fsdp")),
        P(None, ("dp", "fsdp")),
        P(("dp", "fsdp")),
        P(("dp", "fsdp"), None),
        P(("dp", "fsdp")),
        P(("dp", "fsdp"), None),
        P(("dp", "fsdp"), None),
        P(("dp", "fsdp"), None),
    )
    return jax.shard_map(
        on_device,
        mesh=mesh,
        in_specs=placed,
        out_specs=(
            P(("dp", "fsdp"), None, None),
            P(("dp", "fsdp"), None, None),
            P(("dp", "fsdp")),
            P(("dp", "fsdp"), None),
            P(("dp", "fsdp"), None),
            P(("dp", "fsdp"), None),
            P(("dp", "fsdp"), None),
            P(("dp", "fsdp"), None),
            P(None, ("dp", "fsdp")),
            P(None, ("dp", "fsdp")),
            P(None, ("dp", "fsdp")),
            P(("dp", "fsdp")),
            P(("dp", "fsdp"), None),
            P(("dp", "fsdp")),
            P(("dp", "fsdp"), None),
            P(("dp", "fsdp"), None),
            P(("dp", "fsdp"), None),
        ),
        check_vma=False,
    )
```

profile of v0, /device:TPU:11, one launch (start us, length us, event | category | flops | bytes accessed | tf_op | source)
XLA Modules:
  0.0 4152.3 jit_solution(5467324617049401751)
XLA Ops:
  13.6 40.2 all-reduce.37
  54.7 32.1 all-gather
  86.9 37.4 all-gather.1
  125.6 38.5 all-gather.2
  164.3 36.8 all-gather.3
  203.2 49.0 %psum.7 = s32[8]{0:T(128)S(1)} all-reduce(s32[8]{0:T(128)S(1)} %compare_convert_fusion), channel_id=1, replica_groups=mesh['dp'=8,'fsdp'=4] {'dp','fsdp'}, use_global_device_ids=true, to_apply=%region_7.8 | all-reduce | flops 8 | bytes 64 | tf_op jit(solution)/shard_map/psum | solution.py:148
  291.6 108.6 %while.53 = (s32[]{:T(128)}, f32[1,16,128,128]{3,2,1,0:T(8,128)}, f32[4,1,16,64,128]{4,3,2,1,0:T(8,128)}, f32[4,1,16,64,128]{4,3,2,1,0:T(8,128)S(1)}, f32[4,1,16...) while((s32[]{:T(128)}, f32[1,16,128,128]{3,2,1,0:T(8,128)}, ...), condition=%wide.region_4.5_spmd.clone, body=%wide.region_3.4_spmd.clone.sunk | while | flops 1612922880 | bytes 31284948 | solution.py:80
  420.4 74.9 %while.54 = (s32[]{:T(128)}, f32[1,16,128,128]{3,2,1,0:T(8,128)S(1)}, f32[4,1,16,64,128]{4,3,2,1,0:T(8,128)}, f32[4,1,16,128,128]{4,3,2,1,0:T(8,128)}, f32[4,1,1...) while((s32[]{:T(128)}, ...), condition=%wide.region_11.12_spmd.clone, body=%wide.region_10.11_spmd.clone.sunk | while | flops 1613176832 | bytes 32325304 | solution.py:80
  514.4 36.3 all-gather.23.cloned.1.call-done
  563.9 132.5 %all-gather.25.cloned.1.call-done = bf16[2048,5632]{1,0:T(8,128)(2,1)} async-done(((bf16[64,5632]{1,0:T(8,128)(2,1)}), bf16[2048,5632]{1,0:T(8,128)(2,1)}) %all-gather.25.cloned.1.call-update) | async-done | bytes 23068688 | tf_op jit(solution)/shard_map/all_gather | solution.py:213
  709.7 132.4 %all-gather.27.cloned.1.call-done = bf16[5632,2048]{1,0:T(8,128)(2,1)} async-done(((bf16[176,2048]{1,0:T(8,128)(2,1)}), bf16[5632,2048]{1,0:T(8,128)(2,1)}) %all-gather.27.cloned.1.call-update) | async-done | bytes 23068688 | tf_op jit(solution)/shard_map/all_gather | solution.py:214
  913.8 254.7 %while.55 = (s32[]{:T(128)}, f32[1,16,128,128]{2,3,1,0:T(8,128)}, f32[4,1,16,64,128]{4,2,3,0,1:T(8,128)}, f32[4,1,16,64,128]{4,2,3,0,1:T(8,128)}, f32[4,1,16,64,...) while((s32[]{:T(128)}, f32[1,16,128,128]{2,3,1,0:T(8,128)}, ...), condition=%wide.region_17.18_spmd.clone, body=%wide.region_14.17_spmd.clone.sunk | while | flops 4333976576 | bytes 82460928 | solution.py:80
  1278.9 19.9 fusion.304
  1360.8 40.5 all-reduce.36
  1441.4 131.6 %reduce-scatter.43.cloned.1.call-done = f32[64,4]{1,0:T(8,128)} async-done(((f32[2048,4]{1,0:T(8,128)}), f32[64,4]{1,0:T(8,128)}) %reduce-scatter.43.cloned.1.call-update) | async-done | bytes 1040
  1574.5 131.5 %reduce-scatter.37.cloned.1.call-done = f32[64,16]{1,0:T(8,128)} async-done(((f32[2048,16]{1,0:T(8,128)}), f32[64,16]{1,0:T(8,128)}) %reduce-scatter.37.cloned.1.call-update) | async-done | bytes 4112
  1707.4 214.5 %reduce-scatter.21.cloned.1.call-done = f32[64,2048]{1,0:T(8,128)} async-done(((f32[2048,2048]{1,0:T(8,128)}), f32[64,2048]{1,0:T(8,128)}) %reduce-scatter.21.cloned.1.call-update) | async-done | bytes 524304 | tf_op jit(solution)/shard_map/reduce_scatter | solution.py:298
  1921.9 186.4 %reduce-scatter.23.cloned.1.call-done = f32[64,2048]{1,0:T(8,128)} async-done(((f32[2048,2048]{1,0:T(8,128)}), f32[64,2048]{1,0:T(8,128)}) %reduce-scatter.23.cloned.1.call-update) | async-done | bytes 524304 | tf_op jit(solution)/shard_map/reduce_scatter | solution.py:299
  2108.3 188.0 %reduce-scatter.25.cloned.1.call-done = f32[64,2048]{1,0:T(8,128)} async-done(((f32[2048,2048]{1,0:T(8,128)}), f32[64,2048]{1,0:T(8,128)}) %reduce-scatter.25.cloned.1.call-update) | async-done | bytes 524304 | tf_op jit(solution)/shard_map/reduce_scatter | solution.py:300
  2296.4 187.3 %reduce-scatter.27.cloned.1.call-done = f32[64,2048]{1,0:T(8,128)} async-done(((f32[2048,2048]{1,0:T(8,128)}), f32[64,2048]{1,0:T(8,128)}) %reduce-scatter.27.cloned.1.call-update) | async-done | bytes 524304 | tf_op jit(solution)/shard_map/reduce_scatter | solution.py:301
  2483.7 187.3 %reduce-scatter.29.cloned.1.call-done = f32[64,2048]{1,0:T(8,128)} async-done(((f32[2048,2048]{1,0:T(8,128)}), f32[64,2048]{1,0:T(8,128)}) %reduce-scatter.29.cloned.1.call-update) | async-done | bytes 524304 | tf_op jit(solution)/shard_map/reduce_scatter | solution.py:307
  2671.0 491.6 %reduce-scatter.31.cloned.1.call-done = f32[64,5632]{1,0:T(8,128)} async-done(((f32[2048,5632]{1,0:T(8,128)}), f32[64,5632]{1,0:T(8,128)}) %reduce-scatter.31.cloned.1.call-update) | async-done | bytes 1441808 | tf_op jit(solution)/shard_map/reduce_scatter | solution.py:249
  3162.6 491.3 %reduce-scatter.33.cloned.1.call-done = f32[64,5632]{1,0:T(8,128)} async-done(((f32[2048,5632]{1,0:T(8,128)}), f32[64,5632]{1,0:T(8,128)}) %reduce-scatter.33.cloned.1.call-update) | async-done | bytes 1441808 | tf_op jit(solution)/shard_map/reduce_scatter | solution.py:250
  3653.9 491.2 %reduce-scatter.35.cloned.1.call-done = f32[176,2048]{1,0:T(8,128)} async-done(((f32[5632,2048]{1,0:T(8,128)}), f32[176,2048]{1,0:T(8,128)}) %reduce-scatter.35.cloned.1.call-update) | async-done | bytes 1441808 | tf_op jit(solution)/shard_map/reduce_scatter | solution.py:251
  (869 shorter events, 811.2 us)
Async XLA Ops:
  7.2 246.3 %all-gather.13.cloned.1.call-start = ((), (), s32[]{:S(2)}) async-start(), calls=%async_computation.12 | async-start | bytes 8650752 | tf_op jit(solution)/shard_map/all_gather | solution.py:159
  8.0 257.5 %all-gather.15.cloned.1.call-start = ((), (), s32[]{:S(2)}) async-start(), calls=%async_computation.13 | async-start | bytes 8650752 | tf_op jit(solution)/shard_map/all_gather | solution.py:160
  8.7 268.2 %all-gather.17.cloned.1.call-start = ((), (), s32[]{:S(2)}) async-start(), calls=%async_computation.14 | async-start | bytes 8650752 | tf_op jit(solution)/shard_map/all_gather | solution.py:158
  9.5 397.3 %all-gather.19.cloned.1.call-start = ((), (), s32[]{:S(2)}) async-start(), calls=%async_computation.15 | async-start | bytes 8650752 | tf_op jit(solution)/shard_map/all_gather | solution.py:161
  10.0 496.6 %all-gather.21.cloned.1.call-start = ((), (), s32[]{:S(2)}) async-start(), calls=%async_computation.16 | async-start | bytes 8650752 | tf_op jit(solution)/shard_map/all_gather | solution.py:167
  10.6 540.1 %all-gather.23.cloned.1.call-start = ((), (), s32[]{:S(2)}) async-start(), calls=%async_computation.17 | async-start | bytes 23789568 | tf_op jit(solution)/shard_map/all_gather | solution.py:212
  11.2 685.2 %all-gather.25.cloned.1.call-start = ((), (), s32[]{:S(2)}) async-start(), calls=%async_computation.18 | async-start | bytes 23789568 | tf_op jit(solution)/shard_map/all_gather | solution.py:213
  12.0 830.2 %all-gather.27.cloned.1.call-start = ((), (), s32[]{:S(2)}) async-start(), calls=%async_computation.19 | async-start | bytes 23789568 | tf_op jit(solution)/shard_map/all_gather | solution.py:214
  12.7 1406.1 %reduce-scatter.39.cloned.1.call-start = ((), (), s32[]{:S(2)}) async-start(), calls=%async_computation.29 | async-start | bytes 1081344
  53.8 353.6 %copy-start.53 = (f32[2048]{0:T(1024)}, f32[2048]{0:T(1024)S(1)}, u32[]{:S(2)}) copy-start(f32[2048]{0:T(1024)S(1)} %convert_element_type.216) | copy-start | bytes 24580
  54.1 353.3 %copy-start.57 = (f32[256]{0:T(256)}, f32[256]{0:T(256)S(1)}, u32[]{:S(2)}) copy-start(f32[256]{0:T(256)S(1)} %fusion.255) | copy-start | bytes 3076
  86.9 172.5 %copy-start.68 = (f32[1,2048]{1,0:T(1,128)}, f32[1,2048]{1,0:T(1,128)S(1)}, u32[]{:S(2)}) copy-start(f32[1,2048]{1,0:T(1,128)S(1)} %get-tuple-element.751) | copy-start | bytes 24580
  514.4 182.0 %copy-start.30 = (bf16[256,2048]{1,0:T(8,128)(2,1)}, bf16[256,2048]{1,0:T(8,128)(2,1)S(1)}, u32[]{:S(2)}) copy-start(bf16[256,2048]{1,0:T(8,128)(2,1)S(1)} %multiply_convert_fusion.3) | copy-start | bytes 3145732
  1205.2 234.8 %reduce-scatter.41.cloned.1.call-start = ((), (), s32[]{:S(2)}) async-start(), calls=%async_computation.30 | async-start | bytes 1081344
  1216.0 357.1 %reduce-scatter.43.cloned.1.call-start = ((), (), s32[]{:S(2)}) async-start(), calls=%async_computation.31 | async-start | bytes 1081344
  1217.5 488.5 %reduce-scatter.37.cloned.1.call-start = ((), (), s32[]{:S(2)}) async-start(), calls=%async_computation.28 | async-start | bytes 1081344
  1219.2 702.7 %reduce-scatter.21.cloned.1.call-start = ((), (), s32[]{:S(2)}) async-start(), calls=%async_computation.20 | async-start | bytes 17301504 | tf_op jit(solution)/shard_map/reduce_scatter | solution.py:298
  1232.9 875.4 %reduce-scatter.23.cloned.1.call-start = ((), (), s32[]{:S(2)}) async-start(), calls=%async_computation.21 | async-start | bytes 17301504 | tf_op jit(solution)/shard_map/reduce_scatter | solution.py:299
  1245.6 1050.8 %reduce-scatter.25.cloned.1.call-start = ((), (), s32[]{:S(2)}) async-start(), calls=%async_computation.22 | async-start | bytes 17301504 | tf_op jit(solution)/shard_map/reduce_scatter | solution.py:300
  1258.3 1225.4 %reduce-scatter.27.cloned.1.call-start = ((), (), s32[]{:S(2)}) async-start(), calls=%async_computation.23 | async-start | bytes 17301504 | tf_op jit(solution)/shard_map/reduce_scatter | solution.py:301
  1267.8 1403.2 %reduce-scatter.29.cloned.1.call-start = ((), (), s32[]{:S(2)}) async-start(), calls=%async_computation.24 | async-start | bytes 17301504 | tf_op jit(solution)/shard_map/reduce_scatter | solution.py:307
  1278.9 1883.7 %reduce-scatter.31.cloned.1.call-start = ((), (), s32[]{:S(2)}) async-start(), calls=%async_computation.25 | async-start | bytes 47579136 | tf_op jit(solution)/shard_map/reduce_scatter | solution.py:249
  1298.9 2355.0 %reduce-scatter.33.cloned.1.call-start = ((), (), s32[]{:S(2)}) async-start(), calls=%async_computation.26 | async-start | bytes 47579136 | tf_op jit(solution)/shard_map/reduce_scatter | solution.py:250
  1318.7 2826.4 %reduce-scatter.35.cloned.1.call-start = ((), (), s32[]{:S(2)}) async-start(), calls=%async_computation.27 | async-start | bytes 47579136 | tf_op jit(solution)/shard_map/reduce_scatter | solution.py:251
  (119 other events, 2226.0 us)
Sparse Core Ops, SparseCore 0:
  10.9 79.3 all-gather.12
  93.2 76.2 all-gather.14
  172.4 76.4 all-gather.16
  251.6 76.2 all-gather.18
  330.5 76.1 all-gather.20
  409.5 141.2 all-gather.22
  553.6 142.7 all-gather.24
  699.3 142.7 all-gather.26
  1205.3 101.6 reduce-scatter.38
  1309.2 130.7 reduce-scatter.40
  1442.3 130.7 reduce-scatter.42
  1575.3 130.6 reduce-scatter.36
  1708.8 213.0 reduce-scatter.20
  1924.6 183.6 reduce-scatter.22
  2111.0 185.2 reduce-scatter.24
  2299.1 184.5 reduce-scatter.26
  2486.4 184.5 reduce-scatter.28
  2673.7 488.7 reduce-scatter.30
  3165.4 488.3 reduce-scatter.32
  3656.6 488.3 reduce-scatter.34
where the time goes:
time: 4160 us; the launch traced here: 4150 us
  waiting for transfers between devices  3030 us (73%)
  matrix products  614 us (15%)
  blocking collectives  274 us (7%)
  local copies, waits for them, and re-layouts  124 us (3%)
  other arithmetic  66.2 us (2%)
    reduce_scatter x1, waiting for transfers between devices, on_device(): lax.psum_scatter(grad_ffgate, ('dp', 'fsdp'), scatter_dimension=0, tiled=...  492 us
    reduce_scatter x1, waiting for transfers between devices, on_device(): lax.psum_scatter(grad_ffup, ('dp', 'fsdp'), scatter_dimension=0, tiled=True)  491 us
    reduce_scatter x1, waiting for transfers between devices, on_device(): lax.psum_scatter(grad_ffdown, ('dp', 'fsdp'), scatter_dimension=0, tiled=...  491 us
    unnamed x24, waiting for transfers between devices  288 us
    reduce_scatter x1, waiting for transfers between devices, on_device(): lax.psum_scatter(grad_query, ('dp', 'fsdp'), scatter_dimension=0, tiled=T...  215 us
    reduce_scatter x1, waiting for transfers between devices, on_device(): lax.psum_scatter(grad_value, ('dp', 'fsdp'), scatter_dimension=0, tiled=T...  188 us
    reduce_scatter x1, waiting for transfers between devices, on_device(): lax.psum_scatter(grad_gate, ('dp', 'fsdp'), scatter_dimension=0, tiled=True)  187 us
    reduce_scatter x1, waiting for transfers between devices, on_device(): lax.psum_scatter(grad_out, ('dp', 'fsdp'), scatter_dimension=0, tiled=True)  187 us
  transfers between devices with their start and end apart: 20, of which 14 were waited for; matrix products, arithmetic and copies ran while one was open for 10% of the time, Pallas kernels for 0%

commit v1 on v0

v1 whole, which is shorter than its diff:
```python
import functools
import jax
import jax.numpy as jnp
from jax import lax
from jax.experimental import pallas as pl
from jax.experimental.pallas import tpu as pltpu
from jax.sharding import PartitionSpec as P

EPS = 1e-06
BF = jnp.bfloat16
F32 = jnp.float32


def mm(left, right, dims):
    return lax.dot_general(left, right, ((dims[0], dims[1]), ((), ())), preferred_element_type=F32)


NN = ((1,), (0,))
NT = ((1,), (1,))
TN = ((0,), (0,))


def halves(value):
    high = value.astype(BF)
    return high, (value - high.astype(F32)).astype(BF)


def mm3(left, right, dims):
    lh, ll = left
    rh, rl = right
    return mm(lh, rh, dims) + (mm(lh, rl, dims) + mm(ll, rh, dims))


def mm2(left, right, dims):
    lh, ll = left
    return mm(lh, right, dims) + mm(ll, right, dims)


def sigmoid(v):
    return 1.0 / (1.0 + jnp.exp(-v))


def shift_down(v, count, rows):
    if count == 0:
        return v
    return jnp.where(rows >= count, pltpu.roll(v, count, 0), 0.0)


def shift_up(v, count, rows):
    if count == 0:
        return v
    length = v.shape[0]
    return jnp.where(rows < length - count, pltpu.roll(v, length - count, 0), 0.0)


def conv_of(pre, taps, rows):
    total = taps[0] * pre
    for j in range(1, len(taps)):
        total = total + taps[j] * shift_down(pre, j, rows)
    return total


def small_inverse(strict):
    size = strict.shape[0]
    ri = lax.broadcasted_iota(jnp.int32, (size, size), 0)
    ci = lax.broadcasted_iota(jnp.int32, (size, size), 1)
    diff = jnp.bitwise_xor(ri, ci)
    result = jnp.where(ri == ci, 1.0, 0.0) - jnp.where(diff == 1, strict, 0.0)
    span = 2
    while span < size:
        part = jnp.where((diff >= span) & (diff < 2 * span), strict, 0.0)
        rs = halves(result)
        inner = mm3(halves(part), rs, NN)
        result = result - mm3(rs, halves(inner), NN)
        span *= 2
    return result


def head_forward(pre_q, pre_k, pre_v, beta_pre, taps, half):
    length, size = pre_q.shape
    rows = lax.broadcasted_iota(jnp.int32, (length, size), 0)
    cq = conv_of(pre_q, taps[0:4], rows)
    ck = conv_of(pre_k, taps[4:8], rows)
    cv = conv_of(pre_v, taps[8:12], rows)
    sq, sk, sv = sigmoid(cq), sigmoid(ck), sigmoid(cv)
    yq, yk, yv = cq * sq, ck * sk, cv * sv
    rq = lax.rsqrt(jnp.sum(yq * yq, axis=-1, keepdims=True) + EPS)
    rk = lax.rsqrt(jnp.sum(yk * yk, axis=-1, keepdims=True) + EPS)
    query = (yq * rq * size ** (-0.5)).astype(BF)
    key = (yk * rk).astype(BF)
    value = yv.astype(BF)
    beta = sigmoid(beta_pre)
    return (cq, ck, cv, sq, sk, sv, yq, yk, rq, rk, query, key, value, beta, rows)


def lower_masks(length):
    ri = lax.broadcasted_iota(jnp.int32, (length, length), 0)
    ci = lax.broadcasted_iota(jnp.int32, (length, length), 1)
    return ri > ci, ri >= ci


def fwd_kernel(place_ref, pre_ref, bpre_ref, taps_ref, gain_ref, gated_ref, inv_ref, *, heads, size):
    length = pre_ref.shape[0]
    half = length // 2
    width = heads * size
    strictly, inclusive = lower_masks(length)
    for h in range(heads):
        at = pl.ds(h * size, size)
        pre = [pre_ref[:, pl.ds(i * width + h * size, size)] for i in range(4)]
        taps = [taps_ref[i : i + 1, at] for i in range(12)]
        (cq, ck, cv, sq, sk, sv, yq, yk, rq, rk, query, key, value, beta, rows) = head_forward(
            pre[0], pre[1], pre[2], bpre_ref[:, h : h + 1], taps, half
        )
        strict = jnp.where(strictly, mm(key, key, NT) * beta, 0.0)
        top = small_inverse(strict[:half, :half])
        low = small_inverse(strict[half:, half:])
        inv_ref[0, h, 0] = top
        inv_ref[0, h, 1] = low
        rhs = value.astype(F32) * beta
        fresh_top = mm3(halves(top), halves(rhs[:half]), NN)
        ft = halves(fresh_top)
        fresh_low = mm3(
            halves(low), halves(rhs[half:] - mm3(halves(strict[half:, :half]), ft, NN)), NN
        )
        fresh = jnp.concatenate([fresh_top, fresh_low], axis=0)
        scores = jnp.where(inclusive, mm(query, key, NT), 0.0)
        mixer = mm3(halves(scores), halves(fresh), NN)
        scale = lax.rsqrt(jnp.mean(mixer * mixer, axis=-1, keepdims=True) + EPS)
        gate = pre[3]
        gated = mixer * scale * gain_ref[0:1, :] * (gate * sigmoid(gate))
        gated_ref[0, :, at] = gated.astype(BF)


def bwd_kernel(
    place_ref, pre_ref, bpre_ref, taps_ref, gain_ref, inv_ref, dgated_ref,
    dpre_ref, dbeta_ref, dtaps_ref, dgain_ref, *, heads, size,
):
    length = pre_ref.shape[0]
    half = length // 2
    width = heads * size

    @pl.when(pl.program_id(0) == 0)
    def _():
        dtaps_ref[...] = jnp.zeros_like(dtaps_ref)
        dgain_ref[...] = jnp.zeros_like(dgain_ref)

    dbeta_ref[...] = jnp.zeros_like(dbeta_ref)
    strictly, inclusive = lower_masks(length)
    for h in range(heads):
        at = pl.ds(h * size, size)
        pre = [pre_ref[:, pl.ds(i * width + h * size, size)] for i in range(4)]
        taps = [taps_ref[i : i + 1, at] for i in range(12)]
        (cq, ck, cv, sq, sk, sv, yq, yk, rq, rk, query, key, value, beta, rows) = head_forward(
            pre[0], pre[1], pre[2], bpre_ref[:, h : h + 1], taps, half
        )
        gram = mm(key, key, NT)
        strict_low = (gram * beta)[half:, :half]
        top, low = halves(inv_ref[0, h, 0]), halves(inv_ref[0, h, 1])
        cross = halves(strict_low)
        val = value.astype(F32)
        rhs = val * beta
        fresh_top = mm3(top, halves(rhs[:half]), NN)
        fresh_low = mm3(low, halves(rhs[half:] - mm3(cross, halves(fresh_top), NN)), NN)
        fresh = halves(jnp.concatenate([fresh_top, fresh_low], axis=0))
        scores = halves(jnp.where(inclusive, mm(query, key, NT), 0.0))
        mixer = mm3(scores, fresh, NN)
        scale = lax.rsqrt(jnp.mean(mixer * mixer, axis=-1, keepdims=True) + EPS)
        gate = pre[3]
        sg = sigmoid(gate)
        dgated = dgated_ref[0, :, at].astype(F32)
        unit = mixer * scale
        gain = gain_ref[0:1, :]
        dgate = dgated * unit * gain * (sg * (1.0 + gate * (1.0 - sg)))
        dnorm = dgated * (gate * sg)
        dgain_ref[0:1, :] += jnp.sum(dnorm * unit, axis=0, keepdims=True)
        dunit = dnorm * gain
        dmixer = scale * (dunit - unit * jnp.mean(dunit * unit, axis=-1, keepdims=True))
        dm = halves(dmixer)
        dscores = halves(jnp.where(inclusive, mm3(dm, fresh, NT), 0.0))
        dfresh = mm3(scores, dm, TN)
        drhs_low = mm3(low, halves(dfresh[half:]), TN)
        drhs_top = mm3(top, halves(dfresh[:half] - mm3(cross, halves(drhs_low), TN)), TN)
        drhs = jnp.concatenate([drhs_top, drhs_low], axis=0)
        dstrict = jnp.where(strictly, -mm3(halves(drhs), fresh, NT), 0.0)
        dgram = halves(dstrict * beta)
        dquery = mm2(dscores, key, NN)
        dkey = mm2(dscores, query, TN) + mm2(dgram, key, NN) + mm2(dgram, key, TN)
        dval = drhs * beta
        dbeta = jnp.sum(dstrict * gram, axis=-1, keepdims=True) + jnp.sum(
            drhs * val, axis=-1, keepdims=True
        )
        dbeta_ref[:, h : h + 1] = (dbeta * beta * (1.0 - beta)).astype(BF)
        sc = size ** (-0.5)
        uq, uk = yq * rq, yk * rk
        dyq = (rq * sc) * (dquery - uq * jnp.sum(dquery * uq, axis=-1, keepdims=True))
        dyk = rk * (dkey - uk * jnp.sum(dkey * uk, axis=-1, keepdims=True))
        for i, (dy, s, c) in enumerate(((dyq, sq, cq), (dyk, sk, ck), (dval, sv, cv))):
            dc = dy * (s * (1.0 + c * (1.0 - s)))
            total = taps[4 * i] * dc
            for j in range(4):
                dtaps_ref[4 * i + j : 4 * i + j + 1, at] += jnp.sum(
                    dc * shift_down(pre[i], j, rows), axis=0, keepdims=True
                )
                if j:
                    total = total + taps[4 * i + j] * shift_up(dc, j, rows)
            dpre_ref[:, pl.ds(i * width + h * size, size)] = total.astype(BF)
        dpre_ref[:, pl.ds(3 * width + h * size, size)] = dgate.astype(BF)


def delta_forward(place, pre, bpre, taps, gain, slots, heads, size):
    rows = pre.shape[0]
    length = rows // slots
    width = heads * size
    return pl.pallas_call(
        functools.partial(fwd_kernel, heads=heads, size=size),
        grid_spec=pltpu.PrefetchScalarGridSpec(
            num_scalar_prefetch=1,
            grid=(slots,),
            in_specs=[
                pl.BlockSpec((length, 4 * width), lambda i, p: (i, 0)),
                pl.BlockSpec((length, 128), lambda i, p: (i, 0)),
                pl.BlockSpec((16, width), lambda i, p: (0, 0)),
                pl.BlockSpec((8, size), lambda i, p: (0, 0)),
            ],
            out_specs=[
                pl.BlockSpec((1, length, width), lambda i, p: (jnp.bitwise_xor(p[0], i), 0, 0)),
                pl.BlockSpec((1, heads, 2, length // 2, length // 2), lambda i, p: (i, 0, 0, 0, 0)),
            ],
        ),
        out_shape=[
            jax.ShapeDtypeStruct((slots, length, width), BF),
            jax.ShapeDtypeStruct((slots, heads, 2, length // 2, length // 2), F32),
        ],
        compiler_params=pltpu.CompilerParams(vmem_limit_bytes=48 * 1024 * 1024),
        cost_estimate=pl.CostEstimate(
            flops=slots * heads * 400_000_000, bytes_accessed=rows * width * 30, transcendentals=0
        ),
        name="delta_forward",
    )(place, pre, bpre, taps, gain)


def delta_backward(place, pre, bpre, taps, gain, inverse, dgated, slots, heads, size):
    rows = pre.shape[0]
    length = rows // slots
    width = heads * size
    return pl.pallas_call(
        functools.partial(bwd_kernel, heads=heads, size=size),
        grid_spec=pltpu.PrefetchScalarGridSpec(
            num_scalar_prefetch=1,
            grid=(slots,),
            in_specs=[
                pl.BlockSpec((length, 4 * width), lambda i, p: (i, 0)),
                pl.BlockSpec((length, 128), lambda i, p: (i, 0)),
                pl.BlockSpec((16, width), lambda i, p: (0, 0)),
                pl.BlockSpec((8, size), lambda i, p: (0, 0)),
                pl.BlockSpec((1, heads, 2, length // 2, length // 2), lambda i, p: (i, 0, 0, 0, 0)),
                pl.BlockSpec((1, length, width), lambda i, p: (jnp.bitwise_xor(p[0], i), 0, 0)),
            ],
            out_specs=[
                pl.BlockSpec((length, 4 * width), lambda i, p: (i, 0)),
                pl.BlockSpec((length, 128), lambda i, p: (i, 0)),
                pl.BlockSpec((16, width), lambda i, p: (0, 0)),
                pl.BlockSpec((8, size), lambda i, p: (0, 0)),
            ],
        ),
        out_shape=[
            jax.ShapeDtypeStruct((rows, 4 * width), BF),
            jax.ShapeDtypeStruct((rows, 128), BF),
            jax.ShapeDtypeStruct((16, width), F32),
            jax.ShapeDtypeStruct((8, size), F32),
        ],
        compiler_params=pltpu.CompilerParams(vmem_limit_bytes=48 * 1024 * 1024),
        cost_estimate=pl.CostEstimate(
            flops=slots * heads * 800_000_000, bytes_accessed=rows * width * 40, transcendentals=0
        ),
        name="delta_backward",
    )(place, pre, bpre, taps, gain, inverse, dgated)


GROUPS = 8
AXES = ("g", "a", "b", "c")
TEAM = ("a", "b", "c")
SWAP = ((0, 1), (1, 0))
CROSS = ((0, 3), (1, 2), (2, 1), (3, 0))


def swap_a(v):
    return lax.ppermute(v, "a", SWAP)


def swap_b(v):
    return lax.ppermute(v, "b", SWAP)


def swap_c(v):
    return lax.ppermute(v, "c", SWAP)


def team_pieces(v):
    rows = v.shape[0] // 2
    from_a, from_b = swap_a(v), swap_b(v)
    from_ab = jnp.concatenate([swap_b(from_a[:rows]), swap_a(from_b[rows:])], axis=0)
    pieces = []
    for near in (v, from_b, from_a, from_ab):
        pieces += [near, swap_c(near)]
    return pieces


def team_sum(pieces):
    own = []
    for i in range(0, 8, 2):
        own.append(pieces[i] + swap_c(pieces[i + 1].astype(BF)).astype(F32))
    from_b = swap_b(own[1].astype(BF))
    from_a = swap_a(own[2].astype(BF))
    from_ab = lax.ppermute(own[3].astype(BF), ("a", "b"), CROSS)
    return own[0] + from_a.astype(F32) + (from_b.astype(F32) + from_ab.astype(F32))


def team_exchange(v):
    return lax.all_to_all(v, TEAM, 0, 0, tiled=True)


def matmul(left, right):
    return jnp.dot(left, right, preferred_element_type=F32)


def weight_grad(left, right):
    return jnp.einsum("ra,rb->ab", left, right, preferred_element_type=F32)


def back_grad(grad, weight):
    return jnp.einsum("rb,ab->ra", grad, weight, preferred_element_type=F32)


def rms_unit(value):
    scale = lax.rsqrt(jnp.mean(value * value, axis=-1, keepdims=True) + EPS)
    return value * scale, scale


def rms_pull(unit, scale, gain, grad):
    inner = grad * gain
    return scale * (inner - unit * jnp.mean(inner * unit, axis=-1, keepdims=True))


def gather_small(v, groups):
    index = [lax.axis_index(k) for k in AXES]
    both = v[None]
    for axis, swap in (("c", swap_c), ("b", swap_b), ("a", swap_a)):
        other = swap(both)
        mine = lax.axis_index(axis) == 0
        both = jnp.concatenate(
            [jnp.where(mine, both, other), jnp.where(mine, other, both)], axis=0
        )
    whole = jnp.zeros((groups,) + both.shape, both.dtype)
    whole = lax.dynamic_update_index_in_dim(whole, both, index[0], 0)
    for step in range(1, groups):
        got = lax.ppermute(both, "g", [(j, (j + step) % groups) for j in range(groups)])
        whole = lax.dynamic_update_index_in_dim(whole, got, (index[0] - step) % groups, 0)
    return whole.reshape(-1, v.shape[0])


def group_sum_small(v, groups):
    me = lax.axis_index("g")
    total = lax.dynamic_index_in_dim(v, me, 0, False)
    for step in range(1, groups):
        send = lax.dynamic_index_in_dim(v, (me + step) % groups, 0, False)
        total = total + lax.ppermute(send, "g", [(j, (j + step) % groups) for j in range(groups)])
    return total


def group_scatter(v):
    return lax.psum_scatter(v, "g", scatter_dimension=0, tiled=True)


def on_device(
    tokens, group_ids, seq_weights, cotangent, attn_gain, w_query, w_key, w_value, w_gate, w_beta,
    conv_query, conv_key, conv_value, head_gain, w_out, mlp_gain, w_ffgate, w_ffup, w_ffdown,
):
    groups = lax.axis_size("g")
    team = 8
    devices = groups * team
    seqs, length, width = tokens.shape
    span = attn_gain.shape[0]
    taps = conv_query.shape[0]
    heads = w_beta.shape[1]
    size = head_gain.shape[0] * devices
    ff = w_ffgate.shape[1]
    cols = width // team
    own_heads = heads // team
    ff_rows = w_ffdown.shape[0]
    ff_cols = groups * ff_rows
    member = lax.axis_index(TEAM)
    group = lax.axis_index("g")

    mixer_w = jnp.concatenate(
        [w.reshape(span, team, cols) for w in (w_query, w_key, w_value, w_gate)], axis=2
    ).transpose(1, 0, 2)
    mixer_w = team_exchange(mixer_w).reshape(team * span, 4 * cols)
    mixer_w = lax.all_gather(mixer_w, "g", axis=0, tiled=True)

    x_own = tokens.reshape(length, width)
    x_pieces = team_pieces(x_own)

    small = jnp.concatenate(
        [
            attn_gain, mlp_gain,
            conv_query.reshape(-1), conv_key.reshape(-1), conv_value.reshape(-1),
            head_gain, w_beta.reshape(-1),
            group_ids.astype(BF), seq_weights.astype(BF),
        ]
    )
    small = jnp.pad(small, (0, -small.shape[0] % 128))
    small = gather_small(small, groups)
    at = 0

    def take(count):
        nonlocal at
        part = small[:, at : at + count]
        at += count
        return part

    gain_one = take(span).reshape(-1).astype(F32)
    gain_two = take(span).reshape(-1).astype(F32)
    all_taps = [
        take(taps * span).reshape(devices, taps, span).transpose(1, 0, 2).reshape(taps, width)
        for _ in range(3)
    ]
    gain_head = take(head_gain.shape[0]).reshape(-1).astype(F32)
    beta_w = take(span * heads).reshape(width, heads)
    ids = take(1).reshape(-1)
    factor_w = take(1).reshape(-1)
    own_taps = lax.dynamic_slice_in_dim(
        jnp.concatenate(all_taps, axis=0).astype(F32), member * cols, cols, 1
    )
    own_taps = jnp.pad(own_taps, ((0, 16 - 3 * taps), (0, 0)))
    head_rows = jnp.pad(gain_head[None], ((0, 7), (0, 0)))
    beta_w = jnp.pad(
        lax.dynamic_slice_in_dim(beta_w, member * own_heads, own_heads, 1),
        ((0, 0), (0, 128 - own_heads)),
    )
    own_id = group_ids.astype(F32)[0]
    count = jnp.sum((ids.astype(F32) == own_id).astype(jnp.int32)) * length
    factor = (
        seq_weights.astype(F32)[0] * (devices * seqs * length) / (GROUPS * count.astype(F32))
    )

    d_final = cotangent.reshape(length, width).astype(F32) * factor
    d_down = jnp.concatenate(team_pieces(d_final.astype(BF)), axis=0)

    out_w = lax.all_gather(w_out, "g", axis=0, tiled=False)
    ff_w = jnp.concatenate(
        [
            w.reshape(span, groups, team, ff_rows).transpose(2, 0, 1, 3).reshape(team, span, ff_cols)
            for w in (w_ffgate, w_ffup)
        ],
        axis=2,
    )
    ff_w = team_exchange(ff_w).reshape(team * span, 2 * ff_cols)
    ff_w = lax.all_gather(ff_w, "g", axis=0, tiled=True)
    down_w = lax.all_gather(w_ffdown, "g", axis=0, tiled=True)
    out_full = jnp.zeros((groups, team, span, width), BF)
    for i, piece in enumerate(team_pieces(out_w.reshape(groups * span, width))):
        out_full = lax.dynamic_update_slice(
            out_full,
            piece.reshape(groups, 1, span, width),
            (0, jnp.bitwise_xor(member, i), 0, 0),
        )
    out_full = out_full.reshape(width, width)

    normed = jnp.concatenate(
        [(rms_unit(p.astype(F32))[0] * gain_one).astype(BF) for p in x_pieces], axis=0
    )
    beta_pre = matmul(normed, beta_w)
    pre = matmul(normed, mixer_w)
    place = member.astype(jnp.int32).reshape(1)
    gated, inverse = delta_forward(
        place, pre, beta_pre, own_taps, head_rows, team, own_heads, size
    )
    gated = team_exchange(gated).transpose(1, 0, 2).reshape(length, width)
    inputs = x_own.astype(F32)
    resid = inputs + matmul(gated, out_full)

    unit_two, scale_two = rms_unit(resid)
    normed_two = jnp.concatenate(team_pieces((unit_two * gain_two).astype(BF)), axis=0)
    gate_w, up_w = ff_w[:, :ff_cols], ff_w[:, ff_cols:]
    gate_ff = matmul(normed_two, gate_w)
    up_ff = matmul(normed_two, up_w)
    d_hidden = back_grad(d_down, down_w)
    sig = jax.nn.sigmoid(gate_ff)
    silu = gate_ff * sig
    hidden = (silu * up_ff).astype(BF)
    d_gate = (d_hidden * up_ff * (sig + silu * (1.0 - sig))).astype(BF)
    d_up = (d_hidden * silu).astype(BF)
    d_normed_two = back_grad(d_gate, gate_w) + back_grad(d_up, up_w)

    def split(v):
        return [v[i * length : (i + 1) * length] for i in range(team)]

    d_normed_two = team_sum(split(d_normed_two))
    final = resid + team_sum(split(matmul(hidden, down_w)))
    mixed = final.astype(BF).reshape(seqs, length, width)
    grad_ffdown = group_scatter(weight_grad(hidden, d_down).astype(BF)).astype(F32)

    def ff_home(v):
        v = group_scatter(v.astype(BF))
        v = team_exchange(v).reshape(team, span, groups, ff_rows)
        return v.transpose(1, 2, 0, 3).reshape(span, ff).astype(F32)

    grad_ffgate = ff_home(weight_grad(normed_two, d_gate))
    grad_ffup = ff_home(weight_grad(normed_two, d_up))
    mlp_part = jnp.sum(d_normed_two * unit_two, axis=0)
    d_resid = d_final + rms_pull(unit_two, scale_two, gain_two, d_normed_two)

    d_branch = d_resid.astype(BF)
    d_gated = back_grad(d_branch, out_full).astype(BF)
    d_gated = team_exchange(
        d_gated.reshape(length, team, cols).transpose(1, 0, 2)
    )
    gated_rows = gated.reshape(length, groups, team, span)
    grad_out = []
    for i in range(team):
        part = lax.dynamic_index_in_dim(gated_rows, jnp.bitwise_xor(member, i), 2, False)
        grad_out.append(weight_grad(part.reshape(length, groups * span), d_branch))
    grad_out = group_scatter(team_sum(grad_out).astype(BF)).astype(F32)
    d_pre, d_beta, d_taps, d_head = delta_backward(
        place, pre, beta_pre, own_taps, head_rows, inverse, d_gated, team, own_heads, size
    )
    grads = weight_grad(normed, d_pre)
    grad_beta = weight_grad(normed, d_beta)[:, :own_heads]
    d_normed = back_grad(d_pre, mixer_w) + back_grad(d_beta, beta_w)
    x_units = jnp.concatenate([rms_unit(p.astype(F32))[0] for p in x_pieces], axis=0)
    attn_part = jnp.sum(d_normed * x_units, axis=0)
    mixer_grads = team_exchange(group_scatter(grads.astype(BF)))
    mixer_grads = mixer_grads.reshape(team, span, 4, cols).transpose(2, 1, 0, 3)
    mixer_grads = mixer_grads.reshape(4, span, width).astype(F32)

    tap_rows = lax.dynamic_update_slice_in_dim(
        jnp.zeros((3 * taps, width), F32), d_taps[: 3 * taps], member * cols, 1
    )
    head_part = jnp.pad(
        d_head[0].reshape(devices, -1), ((0, 0), (0, span - head_gain.shape[0]))
    )
    extra = jnp.concatenate(
        [
            grad_beta, attn_part[:, None], tap_rows.T, head_part.reshape(-1)[:, None],
            mlp_part[:, None],
        ],
        axis=1,
    )
    kinds = extra.shape[1]
    extra = extra.reshape(groups, team, span * kinds)
    extra = jnp.pad(extra, ((0, 0), (0, 0), (0, -extra.shape[2] % 128)))
    extra = team_exchange(group_sum_small(extra, groups))
    extra = extra[:, : span * kinds].reshape(team, span, kinds)
    grad_beta = extra[:, :, :own_heads].transpose(1, 0, 2).reshape(span, heads)
    rest = jnp.sum(extra[:, :, own_heads:], axis=0)
    grad_attn = rest[:, 0]
    grad_taps = rest[:, 1 : 1 + 3 * taps].T.reshape(3, taps, span)
    grad_head = rest[: head_gain.shape[0], 1 + 3 * taps]
    grad_mlp = rest[:, 2 + 3 * taps]

    d_normed = team_sum(split(d_normed))
    unit_one, scale_one = rms_unit(inputs)
    input_grad = d_resid + rms_pull(unit_one, scale_one, gain_one, d_normed)
    return (
        mixed,
        input_grad.reshape(seqs, length, width),
        grad_attn,
        mixer_grads[0],
        mixer_grads[1],
        mixer_grads[2],
        mixer_grads[3],
        grad_beta,
        grad_taps[0],
        grad_taps[1],
        grad_taps[2],
        grad_head,
        grad_out,
        grad_mlp,
        grad_ffgate,
        grad_ffup,
        grad_ffdown,
    )


def solution(mesh):
    dp, fsdp = mesh.shape["dp"], mesh.shape["fsdp"]
    finer = jax.sharding.Mesh(mesh.devices.reshape(dp // 2, 2, fsdp // 2, 2), AXES)
    one, rows, last = P(AXES), P(AXES, None), P(None, AXES)
    seq = P(AXES, None, None)
    return jax.shard_map(
        on_device,
        mesh=finer,
        in_specs=(
            seq, one, one, seq, one, rows, rows, rows, rows, rows, last, last, last, one, rows,
            one, rows, rows, rows,
        ),
        out_specs=(
            seq, seq, one, rows, rows, rows, rows, rows, last, last, last, one, rows, one, rows,
            rows, rows,
        ),
        check_vma=False,
    )
```

time: 4160 us -> 969 us (0.23)
  waiting for transfers between devices: 3030 us -> 231 us
  matrix products: 614 us -> 216 us
  blocking collectives: 274 us -> 59.3 us
  Pallas kernels: 0 us -> 122 us
  starting transfers between devices: 1.59 us -> 97.3 us
    reduce_scatter x8 -> x5, waiting for transfers between devices: 2440 us -> 0.04 us  [group_scatter(): return lax.psum_scatter(v, 'g', scatter_dimension=0, tiled=True)]
    dot_general x374 -> x25, matrix products: 613 us -> 216 us  [the longest x6 89.7 us: back_grad(): return jnp.einsum('rb,ab->ra', grad, weight, preferred_element_type=F32)]
    all_gather x8 -> x4, waiting for transfers between devices: 301 us -> 0.03 us  [the longest x1 0.02 us: on_device(): out_w = lax.all_gather(w_out, 'g', axis=0, tiled=False)]
    unnamed x24 -> x9, waiting for transfers between devices: 288 us -> 0.81 us
    ppermute x0 -> x69, waiting for transfers between devices: none -> 168 us  [the longest x13 74 us: swap_a(): return lax.ppermute(v, 'a', SWAP)]
    all_gather x4 -> x0, blocking collectives: 145 us -> none  [the longest x1 38.5 us: on_device(): lax.all_gather(conv_value, ('dp', 'fsdp'), axis=1, tiled=True)]
    pallas_call x0 -> x2, Pallas kernels: none -> 122 us  [the longest x1 74.8 us: delta_forward(): pl.pallas_call(functools.partial(fwd_kernel, heads=heads, size=size), gri...]
    unnamed x2 -> x0, blocking collectives: 80.7 us -> none
  transfers between devices with their start and end apart: 20 -> 83, of which waited for: 14 -> 26; matrix products, arithmetic and copies ran while one was open for 10% -> 41% of each run, Pallas kernels for 0% -> 13%
where the time goes in v1:
time: 969 us; the launch traced here: 960 us
  waiting for transfers between devices  231 us (24%)
  matrix products  216 us (22%)
  local copies, waits for them, and re-layouts  128 us (13%)
  Pallas kernels  122 us (13%)
  starting transfers between devices  97.3 us (10%)
  other arithmetic  89.7 us (9%)
  blocking collectives  59.3 us (6%)
  between operations  17.3 us (2%)
    dot_general x6, matrix products, back_grad(): return jnp.einsum('rb,ab->ra', grad, weight, preferred_element_type=F32)  89.7 us
    pallas_call x1, Pallas kernels, delta_forward(): pl.pallas_call(functools.partial(fwd_kernel, heads=heads, size=size), gri...  74.8 us
    ppermute x13, waiting for transfers between devices, swap_a(): return lax.ppermute(v, 'a', SWAP)  74 us
    dot_general x13, matrix products, weight_grad(): return jnp.einsum('ra,rb->ab', left, right, preferred_element_type=F32)  63.5 us
    dot_general x6, matrix products, matmul(): return jnp.dot(left, right, preferred_element_type=F32)  62.9 us
    all_to_all x5, waiting for transfers between devices, team_exchange(): return lax.all_to_all(v, TEAM, 0, 0, tiled=True)  61.7 us
    all_to_all x3, blocking collectives, team_exchange(): return lax.all_to_all(v, TEAM, 0, 0, tiled=True)  59.3 us
    ppermute x13, waiting for transfers between devices, swap_b(): return lax.ppermute(v, 'b', SWAP)  55.5 us
  transfers between devices with their start and end apart: 83, of which 26 were waited for; matrix products, arithmetic and copies ran while one was open for 41% of the time, Pallas kernels for 13%

profile of v1, /device:TPU:11, one launch (start us, length us, event | category | flops | bytes accessed | tf_op | source)
XLA Modules:
  0.0 959.7 jit_solution(8249929743333497268)
XLA Ops:
  12.7 18.0 %all_to_all.59 = bf16[8,64,1024]{2,1,0:T(8,128)(2,1)} all-to-all(bf16[8,64,1024]{2,1,0:T(8,128)(2,1)S(1)} %copy.104), channel_id=1, replica_groups=mesh['g'=4,'a'=2,'b'=2,'c'=2] {'a','b','c'}, dimensions={0} | all-to-all | bytes 2097152 | tf_op jit(solution)/shard_map/all_to_all | solution.py:320
  39.0 22.1 %all_to_all.60 = bf16[8,64,1408]{2,1,0:T(8,128)(2,1)} all-to-all(bf16[8,64,1408]{2,1,0:T(8,128)(2,1)S(1)} %pad_maximum_fusion), channel_id=1, replica_groups=mesh['g'=4,'a'=2,'b'=2,'c'=2] {'a','b','c'}, dimensions={0} | all-to-all | bytes 2883584 | tf_op jit(solution)/shard_map/all_to_all | solution.py:320
  67.0 21.6 %collective-permute-done.1 = bf16[2,2048]{1,0:T(2,128)(2,1)S(1)} collective-permute-done((bf16[2,2048]{1,0:T(2,128)(2,1)S(1)}, bf16[2,2048]{1,0:T(2,128)(2,1)S(1)}, u32[]{:S(2)}, u32[]{:S(2)}) %collective-permute-start.1) | collective-permute-done | bytes 8224 | tf_op jit(solution)/shard_map/ppermute | solution.py:292
  129.5 12.7 %collective-permute-done.40 = bf16[256,2048]{1,0:T(8,128)(2,1)} collective-permute-done((bf16[256,2048]{1,0:T(8,128)(2,1)}, bf16[256,2048]{1,0:T(8,128)(2,1)}, u32[]{:S(2)}, u32[]{:S(2)}) %collective-permute-start.40) | collective-permute-done | bytes 1048608 | tf_op jit(solution)/shard_map/ppermute | solution.py:288
  172.6 15.2 %collective-permute-done.17 = bf16[256,2048]{1,0:T(8,128)(2,1)S(1)} collective-permute-done((bf16[256,2048]{1,0:T(8,128)(2,1)S(1)}, bf16[256,2048]{1,0:T(8,128)(2,1)S(1)}, u32[]{:S(2)}, u32[]{:S(2)}) %collective-permute-start.17) | collective-permute-done | bytes 1048608 | tf_op jit(solution)/shard_map/ppermute | solution.py:288
  215.8 14.9 %fusion.102.pre_ref = f32[2048,1024]{1,0:T(8,128)} fusion(bf16[2048,2048]{1,0:T(8,128)(2,1)} %fusion.73, bf16[2048,1024]{1,0:T(8,128)(2,1)} %all-gather.6.cloned.1.call-done), kind=kOutput, calls=%fused_computation.250 | convolution fusion | flops 8589934592 | bytes 20971520 | tf_op jit(solution)/shard_map/dot_general | solution.py:324
  230.7 74.8 %delta_forward.1 = (bf16[8,256,256]{2,1,0:T(8,128)(2,1)}, f32[8,2,2,128,128]{4,3,2,1,0:T(8,128)S(1)}) custom-call(s32[1]{0:T(128)} %bitcast.1.place_ref, f32[2048,1024]{1,0:T(8,128)} %fusion.102.pre_ref, f32[2048,128]{1,0:T(8,128)S(1)} %fusion.77.bpre_ref, f32[16,256]{1,0:T(8,128)S(1)} %pad.28.taps_ref, f32[8,128]{1,0:T(8,128)S(1)} %pad_convert_fusion.gain_ref), custom_call_target="tpu_custom_call" | custom-call | flops 6400000000 | bytes 15728640 | tf_op jit(solution)/shard_map/delta_forward/pallas_call | solution.py:214
  384.1 11.4 %fusion.10 = f32[2048,704]{0,1:T(8,128)} fusion(bf16[2048,2048]{1,0:T(8,128)(2,1)} %constant_dynamic-update-slice_fusion.4, bf16[2048,1408]{1,0:T(8,128)(2,1)} %all-gather.8.cloned.1.call-done), kind=kOutput, calls=%fused_computation.24 | convolution fusion | flops 5905580032 | bytes 17301504 | tf_op jit(solution)/shard_map/dot_general | solution.py:324
  395.5 11.8 %fusion.6 = f32[2048,704]{0,1:T(8,128)} fusion(bf16[2048,2048]{1,0:T(8,128)(2,1)} %constant_dynamic-update-slice_fusion.4, bf16[2048,1408]{1,0:T(8,128)(2,1)S(1)} %copy-done.52), kind=kOutput, calls=%fused_computation.20 | convolution fusion | flops 5905580032 | bytes 17301504 | tf_op jit(solution)/shard_map/dot_general | solution.py:324
  407.3 15.7 %multiply_convert_fusion = (bf16[2048,704]{0,1:T(8,128)(2,1)S(1)}, bf16[2048,704]{0,1:T(8,128)(2,1)}, bf16[2048,704]{0,1:T(8,128)(2,1)}) fusion(f32[2048,704]{0,1:T(8,128)} %fusion.10, f32[2048,704]{0,1:T(8,128)} %fusion.6, bf16[2048,2048]{1,0:T(8,128)(2,1)} %constant_dynamic-update-slice_fusion.13, bf16[704,2048]{1,0:T(8,128)(2,1)} %all-gather.10.cloned.1.call-done), kind=kOutput, calls=%fused_computation.3 | convolution fusion | flops 5925765120 | bytes 31457280 | tf_op jit(solution)/shard_map/rb,ab->ra/dot_general | solution.py:332
  435.6 12.7 %fusion.8 = f32[2048,2048]{1,0:T(8,128)} fusion(bf16[2048,704]{0,1:T(8,128)(2,1)} %get-tuple-element.86, bf16[2048,1408]{1,0:T(8,128)(2,1)} %all-gather.8.cloned.1.call-done), kind=kOutput, calls=%fused_computation.22 | convolution fusion | flops 5905580032 | bytes 22806528 | tf_op jit(solution)/shard_map/rb,ab->ra/dot_general | solution.py:332
  448.4 18.0 %fusion.100 = (bf16[2048,2048]{1,0:T(8,128)(2,1)}, f32[2048,2048]{1,0:T(8,128)}) fusion(f32[2048,2048]{1,0:T(8,128)} %fusion.8, bf16[2048,704]{0,1:T(8,128)(2,1)} %copy-done.57, bf16[2048,1408]{1,0:T(8,128)(2,1)} %all-gather.8.cloned.1.call-done), kind=kOutput, calls=%fused_computation.248 | convolution fusion | flops 5913968640 | bytes 47972352 | tf_op jit(solution)/shard_map/rb,ab->ra/dot_general | solution.py:332
  485.5 10.9 %convolution_convert_fusion.2 = bf16[2048,704]{0,1:T(8,128)(2,1)} fusion(bf16[2048,704]{0,1:T(8,128)(2,1)S(1)} %copy-done.59, bf16[2048,2048]{1,0:T(8,128)(2,1)} %constant_dynamic-update-slice_fusion.4), kind=kOutput, calls=%fused_computation.10 | convolution fusion | flops 5907021824 | bytes 14155776 | tf_op jit(solution)/shard_map/ra,rb->ab/dot_general | solution.py:328
  496.7 11.1 %collective-permute-done.47 = bf16[256,2048]{1,0:T(8,128)(2,1)} collective-permute-done((bf16[256,2048]{1,0:T(8,128)(2,1)}, bf16[256,2048]{1,0:T(8,128)(2,1)}, u32[]{:S(2)}, u32[]{:S(2)}) %collective-permute-start.47) | collective-permute-done | bytes 1048608 | tf_op jit(solution)/shard_map/ppermute | solution.py:288
  507.8 22.6 %collective-permute-done.51 = bf16[256,2048]{1,0:T(8,128)(2,1)} collective-permute-done((bf16[256,2048]{1,0:T(8,128)(2,1)}, bf16[256,2048]{1,0:T(8,128)(2,1)}, u32[]{:S(2)}, u32[]{:S(2)}) %collective-permute-start.51) | collective-permute-done | bytes 1048608 | tf_op jit(solution)/shard_map/ppermute | solution.py:315
  547.7 19.2 %all_to_all.61.dgated_ref = bf16[8,256,256]{2,1,0:T(8,128)(2,1)S(1)} all-to-all(bf16[8,256,256]{2,1,0:T(8,128)(2,1)} %bitcast.187), channel_id=1, replica_groups=mesh['g'=4,'a'=2,'b'=2,'c'=2] {'a','b','c'}, dimensions={0} | all-to-all | bytes 2097152 | tf_op jit(solution)/shard_map/all_to_all | solution.py:320
  568.6 46.7 %delta_backward.1 = (bf16[2048,1024]{1,0:T(8,128)(2,1)}, bf16[2048,128]{1,0:T(8,128)(2,1)S(1)}, f32[16,256]{1,0:T(8,128)S(1)}, f32[8,128]{1,0:T(8,128)S(1)}) custom-call(s32[1]{0:T(128)} %bitcast.1.place_ref, f32[2048,1024]{1,0:T(8,128)} %fusion.102.pre_ref, f32[2048,128]{1,0:T(8,128)S(1)} %copy-done.5, f32[16,256]{1,0:T(8,128)S(1)} %copy-done.1, ...), custom_call_target="tpu_custom_call" | custom-call | flops 12800000000 | bytes 20971520 | tf_op jit(solution)/shard_map/delta_backward/pallas_call | solution.py:246
  615.3 14.0 %convolution_convert_fusion = bf16[2048,1024]{1,0:T(8,128)(2,1)} fusion(bf16[2048,2048]{1,0:T(8,128)(2,1)} %fusion.73, bf16[2048,1024]{1,0:T(8,128)(2,1)} %get-tuple-element.25), kind=kOutput, calls=%fused_computation.8 | convolution fusion | flops 8592031744 | bytes 16777216 | tf_op jit(solution)/shard_map/ra,rb->ab/dot_general | solution.py:328
  649.0 12.8 %fusion.101 = (bf16[2048,2048]{1,0:T(8,128)(2,1)S(1)}, f32[2048,2048]{1,0:T(8,128)}) fusion(bf16[2048,704]{0,1:T(8,128)(2,1)} %get-tuple-element.87, bf16[704,2048]{1,0:T(8,128)(2,1)S(1)} %copy-done.53), kind=kOutput, calls=%fused_computation.249 | convolution fusion | flops 5909774336 | bytes 30932992 | tf_op jit(solution)/shard_map/dot_general | solution.py:324
  690.3 15.5 %fusion.103 = f32[2048,2048]{1,0:T(8,128)} fusion(bf16[2048,1024]{1,0:T(8,128)(2,1)} %get-tuple-element.25, bf16[2048,1024]{1,0:T(8,128)(2,1)} %all-gather.6.cloned.1.call-done), kind=kOutput, calls=%fused_computation.251 | convolution fusion | flops 8589934592 | bytes 25165824 | tf_op jit(solution)/shard_map/rb,ab->ra/dot_general | solution.py:332
  705.8 21.0 %multiply_reduce_fusion = (f32[2048]{0:T(1024)S(1)}, bf16[2048,2048]{1,0:T(8,128)(2,1)}, f32[2048,2048]{1,0:T(8,128)}) fusion(f32[2048,2048]{1,0:T(8,128)} %fusion.24, f32[2048,2048]{1,0:T(8,128)} %fusion.103, bf16[2048,128]{1,0:T(8,128)(2,1)S(1)} %get-tuple-element.26, bf16[2048,2]{1,0:T(8,128)(2,1)S(1)} %copy-done.24), kind=kOutput, calls=%fused_computation | convolution fusion | flops 1090516992 | bytes 59260928 | tf_op jit(solution)/shard_map/rb,ab->ra/dot_general | solution.py:332
  787.8 14.3 %collective-permute-done.66 = bf16[256,2048]{1,0:T(8,128)(2,1)} collective-permute-done((bf16[256,2048]{1,0:T(8,128)(2,1)}, bf16[256,2048]{1,0:T(8,128)(2,1)}, u32[]{:S(2)}, u32[]{:S(2)}) %collective-permute-start.66) | collective-permute-done | bytes 1048608 | tf_op jit(solution)/shard_map/ppermute | solution.py:292
  833.2 21.6 %all-to-all-done.7 = bf16[8,64,704]{2,1,0:T(8,128)(2,1)} async-done(((bf16[8,64,704]{2,1,0:T(8,128)(2,1)}), bf16[8,64,704]{2,1,0:T(8,128)(2,1)}, u32[]{:S(2)}, u32[]{:S(2)}) %all-to-all-start.7) | async-done | bytes 720928 | tf_op jit(solution)/shard_map/all_to_all | solution.py:320
  872.5 36.1 %all-to-all-done.6 = bf16[8,64,704]{2,1,0:T(8,128)(2,1)} async-done(((bf16[8,64,704]{2,1,0:T(8,128)(2,1)}), bf16[8,64,704]{2,1,0:T(8,128)(2,1)}, u32[]{:S(2)}, u32[]{:S(2)}) %all-to-all-start.6) | async-done | bytes 720928 | tf_op jit(solution)/shard_map/all_to_all | solution.py:320
  (492 shorter events, 447.7 us)
Async XLA Ops:
  7.2 147.2 %all-gather.12.cloned.1.call-start = ((), (), s32[]{:S(2)}) async-start(), calls=%async_computation.21 | async-start | bytes 1310720 | tf_op jit(solution)/shard_map/all_gather | solution.py:450
  7.9 207.8 %all-gather.6.cloned.1.call-start = ((), (), s32[]{:S(2)}) async-start(), calls=%async_computation.13 | async-start | bytes 5242880 | tf_op jit(solution)/shard_map/all_gather | solution.py:399
  30.7 353.4 %all-gather.8.cloned.1.call-start = ((), (), s32[]{:S(2)}) async-start(), calls=%async_computation.14 | async-start | bytes 7208960 | tf_op jit(solution)/shard_map/all_gather | solution.py:459
  61.2 346.1 %all-gather.10.cloned.1.call-start = ((), (), s32[]{:S(2)}) async-start(), calls=%async_computation.15 | async-start | bytes 3604480 | tf_op jit(solution)/shard_map/all_gather | solution.py:460
  64.0 56.0 %collective-permute-start.7 = (bf16[256,2048]{1,0:T(8,128)(2,1)S(1)}, bf16[256,2048]{1,0:T(8,128)(2,1)S(1)}, u32[]{:S(2)}, u32[]{:S(2)}) collective-permute-start(bf16[256,2048]{1,0:T(8,128)(2,1)S(1)} %bitcast.174), channel_id=1, source_target_pairs={{0,2},{2,0},{1,3},{3,1},{4,6},{6,4},{5,7},{7,5},{8,10},{10,8},{9,1... | collective-permute-start | bytes 3145736 | tf_op jit(solution)/shard_map/ppermute | solution.py:292
  145.0 189.9 %collective-permute-start.42 = (bf16[128,2048]{1,0:T(8,128)(2,1)}, bf16[128,2048]{1,0:T(8,128)(2,1)}, u32[]{:S(2)}, u32[]{:S(2)}) collective-permute-start(bf16[128,2048]{1,0:T(8,128)(2,1)} %slice.281), channel_id=1, source_target_pairs={{0,2},{2,0},{1,3},{3,1},{4,6},{6,4},{5,7},{7,5},{8,10},{10,8},{9,1... | collective-permute-start | bytes 1572872 | tf_op jit(solution)/shard_map/ppermute | solution.py:292
  150.7 184.3 %collective-permute-start.43 = (bf16[128,2048]{1,0:T(8,128)(2,1)}, bf16[128,2048]{1,0:T(8,128)(2,1)}, u32[]{:S(2)}, u32[]{:S(2)}) collective-permute-start(bf16[128,2048]{1,0:T(8,128)(2,1)} %slice.282), channel_id=1, source_target_pairs={{0,4},{4,0},{1,5},{5,1},{2,6},{6,2},{3,7},{7,3},{8,12},{12,8},{9,1... | collective-permute-start | bytes 1572872 | tf_op jit(solution)/shard_map/ppermute | solution.py:288
  203.0 135.6 %collective-permute-start.39 = (bf16[256,2048]{1,0:T(8,128)(2,1)}, bf16[256,2048]{1,0:T(8,128)(2,1)}, u32[]{:S(2)}, u32[]{:S(2)}) collective-permute-start(bf16[256,2048]{1,0:T(8,128)(2,1)} %collective-permute-done.38), channel_id=1, source_target_pairs={{0,1},{1,0},{2,3},{3,2},{4,5},{5,4},{6,7},{7,6},{8,9},{9,8},{10,11... | collective-permute-start | bytes 3145736 | tf_op jit(solution)/shard_map/ppermute | solution.py:296
  212.8 100.4 %collective-permute-start.18 = (bf16[256,2048]{1,0:T(8,128)(2,1)S(1)}, bf16[256,2048]{1,0:T(8,128)(2,1)}, u32[]{:S(2)}, u32[]{:S(2)}) collective-permute-start(bf16[256,2048]{1,0:T(8,128)(2,1)S(1)} %collective-permute-done.17), channel_id=1, source_target_pairs={{0,1},{1,0},{2,3},{3,2},{4,5},{5,4},{6,7},{7,6},{8,9},{9,8},{10,11... | collective-permute-start | bytes 3145736 | tf_op jit(solution)/shard_map/ppermute | solution.py:296
  214.7 103.7 %collective-permute-start.21 = (bf16[256,2048]{1,0:T(8,128)(2,1)}, bf16[256,2048]{1,0:T(8,128)(2,1)}, u32[]{:S(2)}, u32[]{:S(2)}) collective-permute-start(bf16[256,2048]{1,0:T(8,128)(2,1)} %constant_dynamic-update-slice_fusion.2), channel_id=1, source_target_pairs={{0,1},{1,0},{2,3},{3,2},{4,5},{5,4},{6,7},{7,6},{8,9},{9,8},{10,11... | collective-permute-start | bytes 3145736 | tf_op jit(solution)/shard_map/ppermute | solution.py:296
  312.1 466.8 %reduce-scatter.12.cloned.1.call-start = ((), (), s32[]{:S(2)}) async-start(), calls=%async_computation.19 | async-start | bytes 3604480 | tf_op jit(solution)/shard_map/reduce_scatter | solution.py:372
  435.6 395.4 %reduce-scatter.10.cloned.1.call-start = ((), (), s32[]{:S(2)}) async-start(), calls=%async_computation.18 | async-start | bytes 3604480 | tf_op jit(solution)/shard_map/reduce_scatter | solution.py:372
  496.4 412.2 %reduce-scatter.6.cloned.1.call-start = ((), (), s32[]{:S(2)}) async-start(), calls=%async_computation.16 | async-start | bytes 5242880 | tf_op jit(solution)/shard_map/reduce_scatter | solution.py:372
  629.4 293.4 %reduce-scatter.14.cloned.1.call-start = ((), (), s32[]{:S(2)}) async-start(), calls=%async_computation.20 | async-start | bytes 3604480 | tf_op jit(solution)/shard_map/reduce_scatter | solution.py:372
  681.9 64.4 %collective-permute-start.63 = (bf16[256,2048]{1,0:T(8,128)(2,1)}, bf16[256,2048]{1,0:T(8,128)(2,1)}, u32[]{:S(2)}, u32[]{:S(2)}) collective-permute-start(bf16[256,2048]{1,0:T(8,128)(2,1)} %convolution_convert_fusion.6), channel_id=1, source_target_pairs={{0,1},{1,0},{2,3},{3,2},{4,5},{5,4},{6,7},{7,6},{8,9},{9,8},{10,11... | collective-permute-start | bytes 3145736 | tf_op jit(solution)/shard_map/ppermute | solution.py:296
  684.0 65.5 %collective-permute-start.65 = (bf16[256,2048]{1,0:T(8,128)(2,1)}, bf16[256,2048]{1,0:T(8,128)(2,1)}, u32[]{:S(2)}, u32[]{:S(2)}) collective-permute-start(bf16[256,2048]{1,0:T(8,128)(2,1)} %convolution_convert_fusion.5), channel_id=1, source_target_pairs={{0,1},{1,0},{2,3},{3,2},{4,5},{5,4},{6,7},{7,6},{8,9},{9,8},{10,11... | collective-permute-start | bytes 3145736 | tf_op jit(solution)/shard_map/ppermute | solution.py:296
  766.8 55.1 %collective-permute-start.54 = (bf16[256,2048]{1,0:T(8,128)(2,1)}, bf16[256,2048]{1,0:T(8,128)(2,1)}, u32[]{:S(2)}, u32[]{:S(2)}) collective-permute-start(bf16[256,2048]{1,0:T(8,128)(2,1)} %get-tuple-element.76), channel_id=1, source_target_pairs={{0,4},{4,0},{1,5},{5,1},{2,6},{6,2},{3,7},{7,3},{8,12},{12,8},{9,1... | collective-permute-start | bytes 3145736 | tf_op jit(solution)/shard_map/ppermute | solution.py:288
  781.2 73.7 %all-to-all-start.7 = ((bf16[8,64,704]{2,1,0:T(8,128)(2,1)}), bf16[8,64,704]{2,1,0:T(8,128)(2,1)}, u32[]{:S(2)}, u32[]{:S(2)}) async-start(bf16[8,64,704]{2,1,0:T(8,128)(2,1)} %bitcast.188), calls=%async_computation.11 | async-start | bytes 1572864 | tf_op jit(solution)/shard_map/all_to_all | solution.py:320
  787.8 137.3 %reduce-scatter.8.cloned.1.call-start = ((), (), s32[]{:S(2)}) async-start(), calls=%async_computation.17 | async-start | bytes 1310720 | tf_op jit(solution)/shard_map/reduce_scatter | solution.py:372
  802.1 113.8 %collective-permute-start.30 = (bf16[256,2048]{1,0:T(8,128)(2,1)}, bf16[256,2048]{1,0:T(8,128)(2,1)}, u32[]{:S(2)}, u32[]{:S(2)}) collective-permute-start(bf16[256,2048]{1,0:T(8,128)(2,1)} %get-tuple-element.96), channel_id=1, source_target_pairs={{0,1},{1,0},{2,3},{3,2},{4,5},{5,4},{6,7},{7,6},{8,9},{9,8},{10,11... | collective-permute-start | bytes 3145736 | tf_op jit(solution)/shard_map/ppermute | solution.py:296
  804.3 63.1 %collective-permute-start.58 = (bf16[256,2048]{1,0:T(8,128)(2,1)}, bf16[256,2048]{1,0:T(8,128)(2,1)}, u32[]{:S(2)}, u32[]{:S(2)}) collective-permute-start(bf16[256,2048]{1,0:T(8,128)(2,1)} %get-tuple-element.77), channel_id=1, source_target_pairs={{0,6},{2,4},{4,2},{6,0},{1,7},{3,5},{5,3},{7,1},{8,14},{10,12},{12... | collective-permute-start | bytes 3145736 | tf_op jit(solution)/shard_map/ppermute | solution.py:315
  811.0 104.9 %collective-permute-start.32 = (bf16[256,2048]{1,0:T(8,128)(2,1)}, bf16[256,2048]{1,0:T(8,128)(2,1)}, u32[]{:S(2)}, u32[]{:S(2)}) collective-permute-start(bf16[256,2048]{1,0:T(8,128)(2,1)} %get-tuple-element.82), channel_id=1, source_target_pairs={{0,4},{4,0},{1,5},{5,1},{2,6},{6,2},{3,7},{7,3},{8,12},{12,8},{9,1... | collective-permute-start | bytes 3145736 | tf_op jit(solution)/shard_map/ppermute | solution.py:288
  822.0 93.9 %collective-permute-start.34 = (bf16[256,2048]{1,0:T(8,128)(2,1)}, bf16[256,2048]{1,0:T(8,128)(2,1)}, u32[]{:S(2)}, u32[]{:S(2)}) collective-permute-start(bf16[256,2048]{1,0:T(8,128)(2,1)} %get-tuple-element.84), channel_id=1, source_target_pairs={{0,2},{2,0},{1,3},{3,1},{4,6},{6,4},{5,7},{7,5},{8,10},{10,8},{9,1... | collective-permute-start | bytes 3145736 | tf_op jit(solution)/shard_map/ppermute | solution.py:292
  827.6 88.3 %collective-permute-start.36 = (bf16[256,2048]{1,0:T(8,128)(2,1)}, bf16[256,2048]{1,0:T(8,128)(2,1)}, u32[]{:S(2)}, u32[]{:S(2)}) collective-permute-start(bf16[256,2048]{1,0:T(8,128)(2,1)} %get-tuple-element.83), channel_id=1, source_target_pairs={{0,6},{2,4},{4,2},{6,0},{1,7},{3,5},{5,3},{7,1},{8,14},{10,12},{12... | collective-permute-start | bytes 3145736 | tf_op jit(solution)/shard_map/ppermute | solution.py:315
  (121 other events, 2760.9 us)
Sparse Core Ops, SparseCore 0:
  9.6 28.8 all-gather.11
  40.0 80.1 all-gather.5
  121.7 105.5 all-gather.7
  228.8 57.8 all-gather.9
  435.7 53.9 reduce-scatter.11
  496.5 54.8 reduce-scatter.9
  629.5 75.9 reduce-scatter.5
  707.8 59.1 reduce-scatter.13
  811.1 22.8 reduce-scatter.7

commit v2 on v1

v2 whole, which is shorter than its diff:
```python
import collections
import functools
import jax
import jax.numpy as jnp
from jax import lax
from jax.experimental import pallas as pl
from jax.experimental.pallas import tpu as pltpu
from jax.sharding import PartitionSpec as P

EPS = 1e-06
BF = jnp.bfloat16
F32 = jnp.float32


def mm(left, right, dims):
    return lax.dot_general(left, right, ((dims[0], dims[1]), ((), ())), preferred_element_type=F32)


NN = ((1,), (0,))
NT = ((1,), (1,))
TN = ((0,), (0,))


def halves(value):
    high = value.astype(BF)
    return high, (value - high.astype(F32)).astype(BF)


def mm3(left, right, dims):
    lh, ll = left
    rh, rl = right
    return mm(lh, rh, dims) + (mm(lh, rl, dims) + mm(ll, rh, dims))


def mm2(left, right, dims):
    lh, ll = left
    return mm(lh, right, dims) + mm(ll, right, dims)


def sigmoid(v):
    return 1.0 / (1.0 + jnp.exp(-v))


def shift_down(v, count, rows):
    if count == 0:
        return v
    return jnp.where(rows >= count, pltpu.roll(v, count, 0), 0.0)


def shift_up(v, count, rows):
    if count == 0:
        return v
    length = v.shape[0]
    return jnp.where(rows < length - count, pltpu.roll(v, length - count, 0), 0.0)


def conv_of(pre, taps, rows):
    total = taps[0] * pre
    for j in range(1, len(taps)):
        total = total + taps[j] * shift_down(pre, j, rows)
    return total


def unit_inverses(stricts):
    size = stricts[0].shape[0]
    ri = lax.broadcasted_iota(jnp.int32, (size, size), 0)
    ci = lax.broadcasted_iota(jnp.int32, (size, size), 1)
    diff = jnp.bitwise_xor(ri, ci)
    eye = jnp.where(ri == ci, 1.0, 0.0)
    results = [eye - jnp.where(diff == 1, strict, 0.0) for strict in stricts]
    span = 2
    while span < size:
        here = (diff >= span) & (diff < 2 * span)
        split = [halves(result) for result in results]
        inner = [mm3(halves(jnp.where(here, s, 0.0)), r, NN) for s, r in zip(stricts, split)]
        inner = [halves(i) for i in inner]
        results = [t - mm3(r, i, NN) for t, r, i in zip(results, split, inner)]
        span *= 2
    return results


def head_forward(pre_q, pre_k, pre_v, beta_pre, taps):
    length, size = pre_q.shape
    rows = lax.broadcasted_iota(jnp.int32, (length, size), 0)
    cq = conv_of(pre_q, taps[0:4], rows)
    ck = conv_of(pre_k, taps[4:8], rows)
    cv = conv_of(pre_v, taps[8:12], rows)
    sq, sk, sv = sigmoid(cq), sigmoid(ck), sigmoid(cv)
    yq, yk, yv = cq * sq, ck * sk, cv * sv
    rq = lax.rsqrt(jnp.sum(yq * yq, axis=-1, keepdims=True) + EPS)
    rk = lax.rsqrt(jnp.sum(yk * yk, axis=-1, keepdims=True) + EPS)
    query = (yq * rq * size ** (-0.5)).astype(BF)
    key = (yk * rk).astype(BF)
    value = yv.astype(BF)
    beta = sigmoid(beta_pre)
    return (cq, ck, cv, sq, sk, sv, yq, yk, rq, rk, query, key, value, beta, rows)


def lower_masks(length):
    ri = lax.broadcasted_iota(jnp.int32, (length, length), 0)
    ci = lax.broadcasted_iota(jnp.int32, (length, length), 1)
    return ri > ci, ri >= ci


def fwd_kernel(
    place_ref, pre_ref, bpre_ref, taps_ref, gain_ref, gated_ref, inv_ref, *, heads, size, length
):
    half = length // 2
    width = heads * size
    flip = place_ref[0] & (gated_ref.shape[0] - 1)
    strictly, inclusive = lower_masks(length)
    work = []
    blocks = []
    chains = [(b, h) for b in range(pre_ref.shape[0] // length) for h in range(heads)]
    for b, h in chains:
        at = pl.ds(h * size, size)
        rows = pl.ds(b * length, length)
        pre = [pre_ref[rows, pl.ds(i * width + h * size, size)] for i in range(3)]
        taps = [taps_ref[i : i + 1, at] for i in range(12)]
        made = head_forward(*pre, bpre_ref[rows, h : h + 1], taps)
        query, key, value, beta = made[10:14]
        strict = jnp.where(strictly, mm(key, key, NT) * beta, 0.0)
        blocks += [strict[:half, :half], strict[half:, half:]]
        scores = jnp.where(inclusive, mm(query, key, NT), 0.0)
        work.append((halves(strict[half:, :half]), value.astype(F32) * beta, halves(scores)))
    inverses = unit_inverses(blocks)
    for n, (b, h) in enumerate(chains):
        inv_ref[b, h, 0] = inverses[2 * n]
        inv_ref[b, h, 1] = inverses[2 * n + 1]
    tops = [mm3(halves(inverses[2 * n]), halves(w[1][:half]), NN) for n, w in enumerate(work)]
    lows = [w[1][half:] - mm3(w[0], halves(top), NN) for w, top in zip(work, tops)]
    lows = [mm3(halves(inverses[2 * n + 1]), halves(low), NN) for n, low in enumerate(lows)]
    mixers = [
        mm3(w[2], halves(jnp.concatenate([top, low], axis=0)), NN)
        for w, top, low in zip(work, tops, lows)
    ]
    for (b, h), mixer in zip(chains, mixers):
        at = pl.ds(h * size, size)
        rows = pl.ds(b * length, length)
        scale = lax.rsqrt(jnp.mean(mixer * mixer, axis=-1, keepdims=True) + EPS)
        gate = pre_ref[rows, pl.ds(3 * width + h * size, size)]
        gated = mixer * scale * gain_ref[0:1, :] * (gate * sigmoid(gate))
        gated_ref[b ^ flip, :, at] = gated.astype(BF)


def bwd_chain(refs, b, h, heads, size, length, masks, sums):
    pre_ref, bpre_ref, taps_ref, gain_ref, inv_ref, dgated_ref, dpre_ref, dbeta_ref, flip = refs
    strictly, inclusive = masks
    half = length // 2
    width = heads * size
    at = pl.ds(h * size, size)
    line = pl.ds(b * length, length)
    cols = [pl.ds(i * width + h * size, size) for i in range(4)]
    taps = [taps_ref[i : i + 1, at] for i in range(12)]
    made = head_forward(
        *[pre_ref[line, c] for c in cols[:3]], bpre_ref[line, h : h + 1], taps
    )
    (cq, ck, cv, sq, sk, sv, yq, yk, rq, rk, query, key, value, beta, rows) = made
    yield
    gram = mm(key, key, NT)
    cross = halves((gram * beta)[half:, :half])
    scores = halves(jnp.where(inclusive, mm(query, key, NT), 0.0))
    top, low = halves(inv_ref[b, h, 0]), halves(inv_ref[b, h, 1])
    val = value.astype(F32)
    rhs = val * beta
    yield
    fresh_top = mm3(top, halves(rhs[:half]), NN)
    yield
    fresh_low = rhs[half:] - mm3(cross, halves(fresh_top), NN)
    yield
    fresh_low = mm3(low, halves(fresh_low), NN)
    fresh = halves(jnp.concatenate([fresh_top, fresh_low], axis=0))
    yield
    mixer = mm3(scores, fresh, NN)
    yield
    scale = lax.rsqrt(jnp.mean(mixer * mixer, axis=-1, keepdims=True) + EPS)
    gate = pre_ref[line, cols[3]]
    sg = sigmoid(gate)
    dgated = dgated_ref[b ^ flip, :, at].astype(F32)
    unit = mixer * scale
    gain = gain_ref[0:1, :]
    dgate = dgated * unit * gain * (sg * (1.0 + gate * (1.0 - sg)))
    dnorm = dgated * (gate * sg)
    sums["gain"].append(jnp.sum(dnorm * unit, axis=0, keepdims=True))
    dunit = dnorm * gain
    dmixer = scale * (dunit - unit * jnp.mean(dunit * unit, axis=-1, keepdims=True))
    dm = halves(dmixer)
    dpre_ref[line, cols[3]] = dgate.astype(BF)
    yield
    dscores = halves(jnp.where(inclusive, mm3(dm, fresh, NT), 0.0))
    dfresh = mm3(scores, dm, TN)
    yield
    drhs_low = mm3(low, halves(dfresh[half:]), TN)
    yield
    drhs_top = dfresh[:half] - mm3(cross, halves(drhs_low), TN)
    yield
    drhs_top = mm3(top, halves(drhs_top), TN)
    drhs = jnp.concatenate([drhs_top, drhs_low], axis=0)
    yield
    dstrict = jnp.where(strictly, -mm3(halves(drhs), fresh, NT), 0.0)
    dgram = halves(dstrict * beta)
    dval = drhs * beta
    dbeta = jnp.sum(dstrict * gram, axis=-1, keepdims=True) + jnp.sum(
        drhs * val, axis=-1, keepdims=True
    )
    dbeta_ref[line, h : h + 1] = (dbeta * beta * (1.0 - beta)).astype(BF)
    yield
    dquery = mm2(dscores, key, NN)
    dkey = mm2(dscores, query, TN) + mm2(dgram, key, NN) + mm2(dgram, key, TN)
    yield
    sc = size ** (-0.5)
    uq, uk = yq * rq, yk * rk
    dyq = (rq * sc) * (dquery - uq * jnp.sum(dquery * uq, axis=-1, keepdims=True))
    dyk = rk * (dkey - uk * jnp.sum(dkey * uk, axis=-1, keepdims=True))
    for i, (dy, s, c) in enumerate(((dyq, sq, cq), (dyk, sk, ck), (dval, sv, cv))):
        dc = dy * (s * (1.0 + c * (1.0 - s)))
        total = taps[4 * i] * dc
        for j in range(4):
            moved = shift_down(pre_ref[line, cols[i]], j, rows)
            sums[4 * i + j, h].append(jnp.sum(dc * moved, axis=0, keepdims=True))
            if j:
                total = total + taps[4 * i + j] * shift_up(dc, j, rows)
        dpre_ref[line, cols[i]] = total.astype(BF)
        yield


def bwd_kernel(
    place_ref, pre_ref, bpre_ref, taps_ref, gain_ref, inv_ref, dgated_ref,
    dpre_ref, dbeta_ref, dtaps_ref, dgain_ref, *, heads, size, length,
):
    @pl.when(pl.program_id(0) == 0)
    def _():
        dtaps_ref[...] = jnp.zeros_like(dtaps_ref)
        dgain_ref[...] = jnp.zeros_like(dgain_ref)

    dbeta_ref[...] = jnp.zeros_like(dbeta_ref)
    masks = lower_masks(length)
    sums = collections.defaultdict(list)
    flip = place_ref[0] & (dgated_ref.shape[0] - 1)
    refs = (
        pre_ref, bpre_ref, taps_ref, gain_ref, inv_ref, dgated_ref, dpre_ref, dbeta_ref, flip
    )
    chains = [
        bwd_chain(refs, b, h, heads, size, length, masks, sums)
        for b in range(dgated_ref.shape[0])
        for h in range(heads)
    ]
    while chains:
        chains = [chain for chain in chains if next(chain, True) is None]
    dgain_ref[0:1, :] += sum(sums.pop("gain"))
    for (row, h), parts in sums.items():
        dtaps_ref[row : row + 1, pl.ds(h * size, size)] += sum(parts)


PAIR = 2


def team_block(i, p):
    return (jnp.bitwise_xor(p[0] // PAIR, i), 0, 0)


def delta_forward(place, pre, bpre, taps, gain, slots, heads, size):
    rows = pre.shape[0]
    length = rows // slots
    width = heads * size
    return pl.pallas_call(
        functools.partial(fwd_kernel, heads=heads, size=size, length=length),
        grid_spec=pltpu.PrefetchScalarGridSpec(
            num_scalar_prefetch=1,
            grid=(slots // PAIR,),
            in_specs=[
                pl.BlockSpec((PAIR * length, 4 * width), lambda i, p: (i, 0)),
                pl.BlockSpec((PAIR * length, 128), lambda i, p: (i, 0)),
                pl.BlockSpec((16, width), lambda i, p: (0, 0)),
                pl.BlockSpec((8, size), lambda i, p: (0, 0)),
            ],
            out_specs=[
                pl.BlockSpec((PAIR, length, width), team_block),
                pl.BlockSpec((PAIR, heads, 2, length // 2, length // 2), lambda i, p: (i, 0, 0, 0, 0)),
            ],
        ),
        out_shape=[
            jax.ShapeDtypeStruct((slots, length, width), BF),
            jax.ShapeDtypeStruct((slots, heads, 2, length // 2, length // 2), F32),
        ],
        compiler_params=pltpu.CompilerParams(vmem_limit_bytes=48 * 1024 * 1024),
        cost_estimate=pl.CostEstimate(
            flops=slots * heads * 100_000_000, bytes_accessed=rows * width * 4, transcendentals=0
        ),
        name="delta_forward",
    )(place, pre, bpre, taps, gain)


def delta_backward(place, pre, bpre, taps, gain, inverse, dgated, slots, heads, size):
    rows = pre.shape[0]
    length = rows // slots
    width = heads * size
    return pl.pallas_call(
        functools.partial(bwd_kernel, heads=heads, size=size, length=length),
        grid_spec=pltpu.PrefetchScalarGridSpec(
            num_scalar_prefetch=1,
            grid=(slots // PAIR,),
            in_specs=[
                pl.BlockSpec((PAIR * length, 4 * width), lambda i, p: (i, 0)),
                pl.BlockSpec((PAIR * length, 128), lambda i, p: (i, 0)),
                pl.BlockSpec((16, width), lambda i, p: (0, 0)),
                pl.BlockSpec((8, size), lambda i, p: (0, 0)),
                pl.BlockSpec((PAIR, heads, 2, length // 2, length // 2), lambda i, p: (i, 0, 0, 0, 0)),
                pl.BlockSpec((PAIR, length, width), team_block),
            ],
            out_specs=[
                pl.BlockSpec((PAIR * length, 4 * width), lambda i, p: (i, 0)),
                pl.BlockSpec((PAIR * length, 128), lambda i, p: (i, 0)),
                pl.BlockSpec((16, width), lambda i, p: (0, 0)),
                pl.BlockSpec((8, size), lambda i, p: (0, 0)),
            ],
        ),
        out_shape=[
            jax.ShapeDtypeStruct((rows, 4 * width), BF),
            jax.ShapeDtypeStruct((rows, 128), BF),
            jax.ShapeDtypeStruct((16, width), F32),
            jax.ShapeDtypeStruct((8, size), F32),
        ],
        compiler_params=pltpu.CompilerParams(vmem_limit_bytes=48 * 1024 * 1024),
        cost_estimate=pl.CostEstimate(
            flops=slots * heads * 100_000_000, bytes_accessed=rows * width * 4, transcendentals=0
        ),
        name="delta_backward",
    )(place, pre, bpre, taps, gain, inverse, dgated)


def load_piece(step, pieces, buf, sem):
    def start(which):
        for n, piece in enumerate(pieces):

            @pl.when(which == n)
            def _():
                pltpu.make_async_copy(piece, buf.at[n % 2], sem.at[n % 2]).start()

    @pl.when(step == 0)
    def _():
        start(0)

    start(step + 1)
    slot = lax.rem(step, 2)
    pltpu.make_async_copy(pieces[0], buf.at[slot], sem.at[slot]).wait()
    return buf[slot]


def piece_scratch(piece):
    return [pltpu.VMEM((2,) + piece.shape, piece.dtype), pltpu.SemaphoreType.DMA((2,))]


ANY = pl.BlockSpec(memory_space=pl.ANY)


def assemble_kernel(place_ref, *refs):
    *pieces, out_ref, buf, sem = refs
    out_ref[:, 0] = load_piece(pl.program_id(0), pieces, buf, sem)


def assemble(place, pieces):
    groups, rows, width = pieces[0].shape
    count = len(pieces)
    return pl.pallas_call(
        assemble_kernel,
        grid_spec=pltpu.PrefetchScalarGridSpec(
            num_scalar_prefetch=1,
            grid=(count,),
            in_specs=[ANY] * count,
            out_specs=pl.BlockSpec(
                (groups, 1, rows, width), lambda i, p: (0, jnp.bitwise_xor(p[0], i), 0, 0)
            ),
            scratch_shapes=piece_scratch(pieces[0]),
        ),
        out_shape=jax.ShapeDtypeStruct((groups, count, rows, width), BF),
        cost_estimate=pl.CostEstimate(
            flops=0, bytes_accessed=4 * count * groups * rows * width, transcendentals=0
        ),
        name="assemble",
    )(place, *pieces)


def ff_tile(n, d, gu_ref, down_ref, hid_ref, dgu_ref):
    cols = hid_ref.shape[1]
    main = cols // 128 * 128
    gu_w = gu_ref[...]
    gu = mm(n, gu_w, NN)
    dh = mm(d, down_ref[...], NT)
    spans = [(0, main, main, 0)]
    if main < cols:
        spans.append((2 * main, main + cols, cols - main, main))
    for gate_at, up_at, count, at in spans:
        gate, up = gu[:, gate_at : gate_at + count], gu[:, up_at : up_at + count]
        grad = dh[:, at : at + count]
        sig = sigmoid(gate)
        silu = gate * sig
        hid_ref[:, at : at + count] = (silu * up).astype(BF)
        dgu_ref[:, gate_at : gate_at + count] = (grad * up * (sig + silu * (1.0 - sig))).astype(BF)
        dgu_ref[:, up_at : up_at + count] = (grad * silu).astype(BF)
    return mm(dgu_ref[...], gu_w, NT), mm(hid_ref[...], down_ref[...], NN)


def ff_first_kernel(gu_ref, down_ref, *refs):
    ns, ds = refs[:8], refs[8:16]
    n_ref, d_ref, hid_ref, dgu_ref, dn_ref, out_ref, n_buf, n_sem, d_buf, d_sem = refs[16:]
    step = pl.program_id(0)
    n = load_piece(step, ns, n_buf, n_sem)
    d = load_piece(step, ds, d_buf, d_sem)
    n_ref[...] = n
    d_ref[...] = d
    dn, out = ff_tile(n, d, gu_ref, down_ref, hid_ref, dgu_ref)
    dn_ref[...] = dn.astype(BF)
    out_ref[...] = out.astype(BF)


def put_pair(step, value, even_ref, odd_ref):
    value = value.astype(BF)

    @pl.when(lax.rem(step, 2) == 0)
    def _():
        even_ref[...] = value

    @pl.when(lax.rem(step, 2) == 1)
    def _():
        odd_ref[...] = value


def ff_more_kernel(
    gu_ref, down_ref, n_ref, d_ref, dn_in, out_in,
    hid_ref, dgu_ref, dn_even, dn_odd, out_even, out_odd,
):
    dn, out = ff_tile(n_ref[...], d_ref[...], gu_ref, down_ref, hid_ref, dgu_ref)
    step = pl.program_id(0)
    put_pair(step, dn + dn_in[...].astype(F32), dn_even, dn_odd)
    put_pair(step, out + out_in[...].astype(F32), out_even, out_odd)


def feed_forward(gu, down, ns=None, ds=None, more=None):
    cols, width = down.shape
    tile = ns[0].shape[0] if more is None else more[0].shape[0] // 8
    rows = 8 * tile

    def row(count):
        return pl.BlockSpec((tile, count), lambda i: (i, 0))

    pair = pl.BlockSpec((tile, width), lambda i: (i // 2, 0))
    if more is None:
        outs = [width, width, cols, 2 * cols, width, width]
        out_specs = [row(k) for k in outs]
        shapes = [(rows, k) for k in outs]
    else:
        out_specs = [row(cols), row(2 * cols)] + [pair] * 4
        shapes = [(rows, cols), (rows, 2 * cols)] + [(rows // 2, width)] * 4
    return pl.pallas_call(
        ff_first_kernel if more is None else ff_more_kernel,
        grid=(8,),
        in_specs=[
            pl.BlockSpec((width, 2 * cols), lambda i: (0, 0)),
            pl.BlockSpec((cols, width), lambda i: (0, 0)),
        ]
        + ([ANY] * 16 if more is None else [row(width)] * 4),
        out_specs=out_specs,
        out_shape=[jax.ShapeDtypeStruct(k, BF) for k in shapes],
        scratch_shapes=piece_scratch(ns[0]) + piece_scratch(ds[0]) if more is None else [],
        compiler_params=pltpu.CompilerParams(vmem_limit_bytes=56 * 1024 * 1024),
        cost_estimate=pl.CostEstimate(
            flops=rows * width * cols, bytes_accessed=2 * rows * width, transcendentals=0
        ),
        name="feed_forward",
    )(gu, down, *(tuple(ns) + tuple(ds) if more is None else more))


def pull_kernel(dpre_ref, dbeta_ref, w_ref, beta_ref, *refs):
    even_ref, odd_ref, part_ref, buf, sem = refs[8:]

    @pl.when(pl.program_id(0) == 0)
    def _():
        part_ref[...] = jnp.zeros_like(part_ref)

    x = load_piece(pl.program_id(0), refs[:8], buf, sem).astype(F32)
    unit = x * lax.rsqrt(jnp.mean(x * x, axis=-1, keepdims=True) + EPS)
    w = w_ref[...].reshape(-1, w_ref.shape[-1])
    dn = mm(dpre_ref[...], w, NT) + mm(dbeta_ref[...], beta_ref[...], NT)
    part_ref[...] += jnp.sum((dn * unit).reshape(-1, 8, dn.shape[1]), axis=0)
    put_pair(pl.program_id(0), dn, even_ref, odd_ref)


def pull_projections(dpre, dbeta, x, w, beta_w):
    tile, width = x[0].shape
    rows, cols = dpre.shape
    groups = w.shape[0]

    def row(count):
        return pl.BlockSpec((tile, count), lambda i: (i, 0))

    return pl.pallas_call(
        pull_kernel,
        grid=(rows // tile,),
        in_specs=[
            row(cols),
            row(dbeta.shape[1]),
            pl.BlockSpec((groups, width // groups, cols), lambda i: (0, 0, 0)),
            pl.BlockSpec(beta_w.shape, lambda i: (0, 0)),
        ]
        + [ANY] * 8,
        scratch_shapes=piece_scratch(x[0]),
        out_specs=[pl.BlockSpec((tile, width), lambda i: (i // 2, 0))] * 2
        + [pl.BlockSpec((8, width), lambda i: (0, 0))],
        out_shape=[
            jax.ShapeDtypeStruct((rows // 2, width), BF),
            jax.ShapeDtypeStruct((rows // 2, width), BF),
            jax.ShapeDtypeStruct((8, width), F32),
        ],
        compiler_params=pltpu.CompilerParams(vmem_limit_bytes=48 * 1024 * 1024),
        cost_estimate=pl.CostEstimate(
            flops=rows * width * cols // 4, bytes_accessed=rows * width, transcendentals=0
        ),
        name="pull_projections",
    )(dpre, dbeta, w, beta_w, *x)


def project_kernel(gain_ref, w_ref, beta_ref, *refs):
    n_ref, pre_ref, bpre_ref, buf, sem = refs[8:]
    x = load_piece(pl.program_id(0), refs[:8], buf, sem).astype(F32)
    unit = x * lax.rsqrt(jnp.mean(x * x, axis=-1, keepdims=True) + EPS)
    n = (unit * gain_ref[0:1, :]).astype(BF)
    n_ref[...] = n
    pre_ref[...] = mm(n, w_ref[...].reshape(-1, w_ref.shape[-1]), NN)
    bpre_ref[...] = mm(n, beta_ref[...], NN)


def project(x, gain, w, beta_w):
    tile, width = x[0].shape
    rows = 8 * tile
    groups, _, cols = w.shape

    def row(count):
        return pl.BlockSpec((tile, count), lambda i: (i, 0))

    return pl.pallas_call(
        project_kernel,
        grid=(rows // tile,),
        in_specs=[
            pl.BlockSpec((8, width), lambda i: (0, 0)),
            pl.BlockSpec((groups, width // groups, cols), lambda i: (0, 0, 0)),
            pl.BlockSpec(beta_w.shape, lambda i: (0, 0)),
        ]
        + [ANY] * 8,
        scratch_shapes=piece_scratch(x[0]),
        out_specs=[row(width), row(cols), row(beta_w.shape[1])],
        out_shape=[
            jax.ShapeDtypeStruct((rows, width), BF),
            jax.ShapeDtypeStruct((rows, cols), F32),
            jax.ShapeDtypeStruct((rows, beta_w.shape[1]), F32),
        ],
        compiler_params=pltpu.CompilerParams(vmem_limit_bytes=48 * 1024 * 1024),
        cost_estimate=pl.CostEstimate(
            flops=rows * width * cols // 4, bytes_accessed=rows * width, transcendentals=0
        ),
        name="project",
    )(gain, w, beta_w, *x)


GROUPS = 8
AXES = ("g", "a", "b", "c")
TEAM = ("a", "b", "c")
SWAP = ((0, 1), (1, 0))
CROSS = ((0, 3), (1, 2), (2, 1), (3, 0))


def swap_a(v):
    return lax.ppermute(v, "a", SWAP)


def swap_b(v):
    return lax.ppermute(v, "b", SWAP)


def swap_c(v):
    return lax.ppermute(v, "c", SWAP)


def after(v, *others):
    if not others:
        return lax.optimization_barrier(v)
    return lax.optimization_barrier((v,) + others)[0]


def plus(left, right):
    return (left.astype(F32) + right.astype(F32)).astype(BF)


def near_pieces(v):
    return v, swap_b(v), swap_a(v)


def far_piece(near):
    _, from_b, from_a = near
    rows = from_a.shape[0] // 2
    return jnp.concatenate([swap_b(from_a[:rows]), swap_a(from_b[rows:])], axis=0)


def team_pieces(near, far=None):
    pieces = []
    for v in (*near, far_piece(near) if far is None else far):
        pieces += [v, swap_c(v)]
    return pieces


def team_terms(even, odd):
    length = even.shape[0] // 4
    got = swap_c(odd)
    parts = [[v[i * length : (i + 1) * length] for v in (even, got)] for i in range(4)]
    (mine, other), *rest = parts
    return [mine.astype(F32) + other.astype(F32)] + [plus(mine, other) for mine, other in rest]


def team_start(terms, *others):
    own, near_b, near_a, far = terms
    rows = far.shape[0] // 2
    near_b, near_a, far = after((near_b, near_a, far), *others)
    via_a, via_b = swap_a(far[:rows]), swap_b(far[rows:])
    from_a, from_b = swap_a(near_a[:rows]), swap_b(near_b[rows:])
    return own, near_b[:rows], near_a[rows:], via_a, via_b, from_a, from_b


def team_end(started, *others):
    own, near_b, near_a, via_a, via_b, from_a, from_b = started
    via_a, via_b = after((via_a, via_b), *others)
    late_a = swap_a(plus(near_a, via_b))
    late_b = swap_b(plus(near_b, via_a))
    sums = jnp.concatenate(
        [
            from_a.astype(F32) + late_b.astype(F32),
            late_a.astype(F32) + from_b.astype(F32),
        ],
        axis=0,
    )
    return own + sums


def team_exchange(v):
    return lax.all_to_all(v, TEAM, 0, 0, tiled=True)


def matmul(left, right):
    return jnp.dot(left, right, preferred_element_type=F32)


def weight_grad(left, right):
    return jnp.einsum("ra,rb->ab", left, right, preferred_element_type=F32)


def back_grad(grad, weight):
    return jnp.einsum("rb,ab->ra", grad, weight, preferred_element_type=F32)


def rms_unit(value):
    scale = lax.rsqrt(jnp.mean(value * value, axis=-1, keepdims=True) + EPS)
    return value * scale, scale


def rms_pull(unit, scale, gain, grad):
    inner = grad * gain
    return scale * (inner - unit * jnp.mean(inner * unit, axis=-1, keepdims=True))


def gather_small(v, groups):
    both = v[None]
    for axis, swap in (("c", swap_c), ("b", swap_b), ("a", swap_a)):
        other = swap(both)
        mine = lax.axis_index(axis) == 0
        both = jnp.concatenate(
            [jnp.where(mine, both, other), jnp.where(mine, other, both)], axis=0
        )
    me = lax.axis_index("g")
    whole = jnp.zeros((groups,) + both.shape, both.dtype)
    whole = lax.dynamic_update_index_in_dim(whole, both, me, 0)
    for step in range(1, groups):
        got = lax.ppermute(both, "g", [(j, (j + step) % groups) for j in range(groups)])
        whole = lax.dynamic_update_index_in_dim(whole, got, (me - step) % groups, 0)
    return whole.reshape(-1, v.shape[0])


def group_sum_small(v, groups):
    me = lax.axis_index("g")
    total = lax.dynamic_index_in_dim(v, me, 0, False)
    for step in range(1, groups):
        send = lax.dynamic_index_in_dim(v, (me + step) % groups, 0, False).astype(BF)
        got = lax.ppermute(send, "g", [(j, (j + step) % groups) for j in range(groups)])
        total = total + got.astype(F32)
    return total


def group_scatter(v):
    return lax.psum_scatter(v, "g", scatter_dimension=0, tiled=True)


def group_gather(v):
    return lax.all_gather(v, "g", axis=0, tiled=False)


def on_device(
    tokens, group_ids, seq_weights, cotangent, attn_gain, w_query, w_key, w_value, w_gate, w_beta,
    conv_query, conv_key, conv_value, head_gain, w_out, mlp_gain, w_ffgate, w_ffup, w_ffdown,
):
    groups = lax.axis_size("g")
    team = 8
    devices = groups * team
    seqs, length, width = tokens.shape
    span = attn_gain.shape[0]
    taps = conv_query.shape[0]
    heads = w_beta.shape[1]
    size = head_gain.shape[0] * devices
    ff = w_ffgate.shape[1]
    cols = width // team
    own_heads = heads // team
    ff_rows = w_ffdown.shape[0]
    member = lax.axis_index(TEAM)
    first = ff_rows * groups // 2 // 128 * 128
    first = (first + 128 if first * 2 < ff_rows * groups else first) // groups
    ff_parts = [(0, first), (first, ff_rows)]

    mixer_w = jnp.concatenate(
        [w.reshape(span, team, cols) for w in (w_query, w_key, w_value, w_gate)], axis=2
    ).transpose(1, 0, 2)
    mixer_sent = team_exchange(mixer_w).reshape(team * span, 4 * cols)
    mixer_all = group_gather(
        jnp.concatenate([mixer_sent, w_out.reshape(-1, 4 * cols)], axis=0)
    )

    small = jnp.concatenate(
        [
            attn_gain, mlp_gain,
            conv_query.reshape(-1), conv_key.reshape(-1), conv_value.reshape(-1),
            head_gain, w_beta.reshape(-1),
            group_ids.astype(BF), seq_weights.astype(BF),
        ]
    )
    small = jnp.pad(small, (0, -small.shape[0] % 128))
    small = gather_small(after(small, mixer_sent), groups)

    x_own = tokens.reshape(length, width)
    x_pieces = team_pieces(near_pieces(after(x_own, mixer_sent)))
    at = 0

    def take(count):
        nonlocal at
        part = small[:, at : at + count]
        at += count
        return part

    gain_one = take(span).reshape(-1).astype(F32)
    gain_two = take(span).reshape(-1).astype(F32)
    all_taps = [
        take(taps * span).reshape(devices, taps, span).transpose(1, 0, 2).reshape(taps, width)
        for _ in range(3)
    ]
    gain_head = take(head_gain.shape[0]).reshape(-1).astype(F32)
    beta_w = take(span * heads).reshape(width, heads)
    ids = take(1).reshape(-1)
    own_taps = lax.dynamic_slice_in_dim(
        jnp.concatenate(all_taps, axis=0).astype(F32), member * cols, cols, 1
    )
    own_taps = jnp.pad(own_taps, ((0, 16 - 3 * taps), (0, 0)))
    head_rows = jnp.pad(gain_head[None], ((0, 7), (0, 0)))
    beta_w = jnp.pad(
        lax.dynamic_slice_in_dim(beta_w, member * own_heads, own_heads, 1),
        ((0, 0), (0, 128 - own_heads)),
    )
    count = jnp.sum((ids.astype(F32) == group_ids.astype(F32)[0]).astype(jnp.int32)) * length
    factor = (
        seq_weights.astype(F32)[0] * (devices * seqs * length) / (GROUPS * count.astype(F32))
    )

    ff_own = []
    gates = [w.reshape(span, groups, team, ff_rows) for w in (w_ffgate, w_ffup)]
    sent = (small, x_pieces[6])
    for low, high in ff_parts:
        part = (high - low) * groups
        main = part // 128 * 128
        own = [
            w[..., low:high].transpose(2, 0, 1, 3).reshape(team, span, part) for w in gates
        ]
        own = [w[..., :main] for w in own] + [w[..., main:] for w in own]
        own = after(jnp.concatenate(own, axis=2), *sent)
        own = team_exchange(own).reshape(team * span, 2 * part)
        sent = (own,)
        ff_own.append(own)
    d_final = cotangent.reshape(length, width).astype(F32) * factor
    d_near = near_pieces(after(d_final.astype(BF), x_pieces[6]))
    x_pieces, d_near, ff_own = after((x_pieces, d_near, ff_own))
    ff_gu = [group_gather(ff_own[0])]
    down_w = group_gather(after(w_ffdown, ff_own[0]))
    ff_gu.append(group_gather(ff_own[1]))
    ff_gu = [v.reshape(width, -1) for v in ff_gu]
    ff_down = [down_w[:, low:high].reshape(-1, width) for low, high in ff_parts]

    gain_rows = jnp.pad(gain_one[None], ((0, 7), (0, 0)))
    normed, pre, beta_pre = project(x_pieces, gain_rows, mixer_all, beta_w)
    place = member.astype(jnp.int32).reshape(1)
    out_near = near_pieces(mixer_all[:, team * span :].reshape(groups * span, width))
    pre, out_near = after((pre, out_near))
    gated, inverse = delta_forward(
        place, pre, beta_pre, own_taps, head_rows, team, own_heads, size
    )
    d_down = team_pieces(after(d_near, out_near))
    gated, d_down[6], out_near = after((gated, d_down[6], out_near))
    gated, out_far = after((team_exchange(gated), far_piece(out_near)))
    out_pieces = [v.reshape(groups, span, width) for v in team_pieces(out_near, out_far)]
    gated = gated.transpose(1, 0, 2).reshape(length, width)
    out_full = assemble(place, out_pieces).reshape(width, width)
    inputs = x_own.astype(F32)
    resid = inputs + matmul(gated, out_full)

    unit_two, scale_two = rms_unit(resid)
    normed_two = team_pieces(near_pieces((unit_two * gain_two).astype(BF)))
    normed_two, d_down, hidden, d_gu, *sums = feed_forward(
        ff_gu[0], ff_down[0], normed_two, d_down
    )
    grad_gu = weight_grad(normed_two, d_gu).astype(BF)
    hidden_more, d_gu_more, dn_even, dn_odd, out_even, out_odd = feed_forward(
        ff_gu[1], ff_down[1], more=(normed_two, d_down) + tuple(after(sums, grad_gu))
    )
    ff_grads = [group_scatter(grad_gu)]
    terms = team_terms(dn_even, dn_odd)
    hidden, hidden_more = after((hidden, hidden_more), *terms)
    grad_gu = weight_grad(normed_two, d_gu_more).astype(BF)
    ff_grads.append(group_scatter(grad_gu))
    grad_down = jnp.concatenate(
        [
            weight_grad(v, d_down).astype(BF).reshape(groups, -1, width)
            for v in after((hidden, hidden_more), grad_gu)
        ],
        axis=1,
    )
    final_terms = team_terms(*after((out_even, out_odd), *terms))
    started = team_start(terms)
    started, grad_down, ff_grads[0] = after((started, grad_down, ff_grads[0]))
    grad_ffdown = group_scatter(grad_down.reshape(-1, width)).astype(F32)
    d_normed_two = team_end(started)
    gu_home_first = team_exchange(after(ff_grads[0], d_normed_two))
    mlp_part = jnp.sum(d_normed_two * unit_two, axis=0)
    d_resid = d_final + rms_pull(unit_two, scale_two, gain_two, d_normed_two)

    d_branch = d_resid.astype(BF)
    d_gated = back_grad(d_branch, out_full).astype(BF)
    d_gated_sent = d_gated.reshape(length, team, cols).transpose(1, 0, 2)
    d_gated_sent, gu_home_first = after((d_gated_sent, gu_home_first))
    d_gated = team_exchange(d_gated_sent)
    final_started = team_start(final_terms, d_gated)
    gated_rows = gated.reshape(length, groups, team, span)
    gated_rows = [
        lax.dynamic_index_in_dim(gated_rows, jnp.bitwise_xor(member, i), 2, False).reshape(
            length, groups * span
        )
        for i in range(team)
    ]
    out_terms = team_terms(
        *[
            weight_grad(jnp.concatenate(gated_rows[i::2], axis=1), d_branch).astype(BF)
            for i in range(2)
        ]
    )
    d_pre, d_beta, d_taps, d_head = delta_backward(
        place, pre, beta_pre, own_taps, head_rows, inverse, after(d_gated, *out_terms), team,
        own_heads, size
    )
    d_pre, final_started = after((d_pre, final_started))
    final_sum = team_end(final_started)
    grads = weight_grad(normed, d_pre).astype(BF)
    mixer_grads = group_scatter(grads)
    d_pre, grads, final_sum, ff_grads[1] = after((d_pre, grads, final_sum, ff_grads[1]))
    out_started = team_start(out_terms, final_sum)
    grad_beta = weight_grad(normed, d_beta)[:, :own_heads]
    dn_even, dn_odd, attn_part = pull_projections(
        d_pre, d_beta, x_pieces, mixer_all, beta_w
    )
    dn_even, dn_odd, out_started, grad_ffdown = after((dn_even, dn_odd, out_started, grad_ffdown))
    grad_out = team_end(out_started)
    in_terms = team_terms(dn_even, dn_odd)
    grad_out_home = group_sum_small(grad_out.reshape(groups, span, width), groups)
    mixed = (resid + final_sum).astype(BF).reshape(seqs, length, width)
    in_terms, mixer_grads = after((in_terms, mixer_grads))
    in_started = team_start(in_terms, out_started)
    gu_home = [gu_home_first, team_exchange(after(ff_grads[1], *in_terms[1:]))]

    ff_home = [[], []]
    for gu, (low, high) in zip(gu_home, ff_parts):
        part = (high - low) * groups
        main = part // 128 * 128
        gu = after(gu, mixer_grads).reshape(team, span, 2 * part)
        gate = jnp.concatenate([gu[..., :main], gu[..., 2 * main : part + main]], axis=2)
        up = jnp.concatenate([gu[..., main : 2 * main], gu[..., part + main :]], axis=2)
        for home, v in zip(ff_home, (gate, up)):
            home.append(v.reshape(team, span, groups, high - low).transpose(1, 2, 0, 3))
    grad_ffgate, grad_ffup = [
        jnp.concatenate(home, axis=3).reshape(span, ff).astype(F32) for home in ff_home
    ]
    mixer_grads = team_exchange(mixer_grads)
    mixer_grads = mixer_grads.reshape(team, span, 4, cols).transpose(2, 1, 0, 3)
    mixer_grads = mixer_grads.reshape(4, span, width).astype(F32)

    tap_rows = lax.dynamic_update_slice_in_dim(
        jnp.zeros((3 * taps, width), F32), d_taps[: 3 * taps], member * cols, 1
    )
    head_part = jnp.pad(
        d_head[0].reshape(devices, -1), ((0, 0), (0, span - head_gain.shape[0]))
    )
    extra = jnp.concatenate(
        [
            grad_beta, jnp.sum(attn_part, axis=0)[:, None], tap_rows.T,
            head_part.reshape(-1)[:, None], mlp_part[:, None],
        ],
        axis=1,
    )
    kinds = extra.shape[1]
    extra = extra.reshape(groups, team, span * kinds)
    extra = jnp.pad(extra, ((0, 0), (0, 0), (0, -extra.shape[2] % 128)))
    extra = team_exchange(group_sum_small(extra, groups))
    extra = extra[:, : span * kinds].reshape(team, span, kinds)
    grad_beta = extra[:, :, :own_heads].transpose(1, 0, 2).reshape(span, heads)
    rest = jnp.sum(extra[:, :, own_heads:], axis=0)
    grad_attn = rest[:, 0]
    grad_taps = rest[:, 1 : 1 + 3 * taps].T.reshape(3, taps, span)
    grad_head = rest[: head_gain.shape[0], 1 + 3 * taps]
    grad_mlp = rest[:, 2 + 3 * taps]

    d_normed = team_end(in_started)
    unit_one, scale_one = rms_unit(inputs)
    input_grad = d_resid + rms_pull(unit_one, scale_one, gain_one, d_normed)
    return (
        mixed,
        input_grad.reshape(seqs, length, width),
        grad_attn,
        mixer_grads[0],
        mixer_grads[1],
        mixer_grads[2],
        mixer_grads[3],
        grad_beta,
        grad_taps[0],
        grad_taps[1],
        grad_taps[2],
        grad_head,
        grad_out_home,
        grad_mlp,
        grad_ffgate,
        grad_ffup,
        grad_ffdown,
    )


def solution(mesh):
    dp, fsdp = mesh.shape["dp"], mesh.shape["fsdp"]
    finer = jax.sharding.Mesh(mesh.devices.reshape(dp // 2, 2, fsdp // 2, 2), AXES)
    one, rows, last = P(AXES), P(AXES, None), P(None, AXES)
    seq = P(AXES, None, None)
    return jax.shard_map(
        on_device,
        mesh=finer,
        in_specs=(
            seq, one, one, seq, one, rows, rows, rows, rows, rows, last, last, last, one, rows,
            one, rows, rows, rows,
        ),
        out_specs=(
            seq, seq, one, rows, rows, rows, rows, rows, last, last, last, one, rows, one, rows,
            rows, rows,
        ),
        check_vma=False,
    )
```

time: 969 us -> 758 us (0.78)
  matrix products: 216 us -> 72.1 us
  waiting for transfers between devices: 231 us -> 171 us
  blocking collectives: 59.3 us -> 0 us
  Pallas kernels: 122 us -> 168 us
  starting transfers between devices: 97.3 us -> 114 us
  other arithmetic: 89.7 us -> 78.7 us
    dot_general x6 -> x1, matrix products: 89.7 us -> 7.36 us  [back_grad(): return jnp.einsum('rb,ab->ra', grad, weight, preferred_element_type=F32)]
    all_to_all x3 -> x0, blocking collectives: 59.3 us -> none  [team_exchange(): return lax.all_to_all(v, TEAM, 0, 0, tiled=True)]
    dot_general x6 -> x1, matrix products: 62.9 us -> 6.23 us  [matmul(): return jnp.dot(left, right, preferred_element_type=F32)]
    pallas_call x2 -> x7, Pallas kernels: 122 us -> 168 us  [the longest x2 68.5 us: feed_forward(): pl.pallas_call(ff_first_kernel if more is None else ff_more_kernel, grid=...]
    all_to_all x5 -> x9, waiting for transfers between devices: 61.7 us -> 28.3 us  [team_exchange(): return lax.all_to_all(v, TEAM, 0, 0, tiled=True)]
    unnamed x17 -> x2, other arithmetic: 31.7 us -> 0.01 us
    slice x11 -> x30, local copies, waits for them, and re-layouts: 14.4 us -> 38.3 us  [the longest x4 7.3 us: team_start(): via_a, via_b = (swap_a(far[:rows]), swap_b(far[rows:]))]
    ppermute x4 -> x0, waiting for transfers between devices: 22.6 us -> none  [team_sum(): from_ab = lax.ppermute(own[3].astype(BF), ('a', 'b'), CROSS)]
  transfers between devices with their start and end apart: 83 -> 89, of which waited for: 26 -> 29; matrix products, arithmetic and copies ran while one was open for 41% -> 34% of each run, Pallas kernels for 13% -> 23%
where the time goes in v2:
time: 758 us; the launch traced here: 746 us
  waiting for transfers between devices  171 us (23%)
  Pallas kernels  168 us (22%)
  local copies, waits for them, and re-layouts  124 us (16%)
  starting transfers between devices  114 us (15%)
  other arithmetic  78.7 us (10%)
  matrix products  72.1 us (10%)
  between operations  17.9 us (2%)
    pallas_call x2, Pallas kernels, feed_forward(): pl.pallas_call(ff_first_kernel if more is None else ff_more_kernel, grid=...  68.5 us
    ppermute x21, waiting for transfers between devices, swap_b(): return lax.ppermute(v, 'b', SWAP)  65.1 us
    dot_general x8, matrix products, weight_grad(): return jnp.einsum('ra,rb->ab', left, right, preferred_element_type=F32)  58.5 us
    ppermute x21, waiting for transfers between devices, swap_a(): return lax.ppermute(v, 'a', SWAP)  52.7 us
    all_to_all x9, starting transfers between devices, team_exchange(): return lax.all_to_all(v, TEAM, 0, 0, tiled=True)  48.2 us
    convert_element_type x12, other arithmetic, plus(): return (left.astype(F32) + right.astype(F32)).astype(BF)  37.8 us
    pallas_call x1, Pallas kernels, delta_backward(): pl.pallas_call(functools.partial(bwd_kernel, heads=heads, size=size, leng...  30.9 us
    all_to_all x9, waiting for transfers between devices, team_exchange(): return lax.all_to_all(v, TEAM, 0, 0, tiled=True)  28.3 us
  transfers between devices with their start and end apart: 89, of which 29 were waited for; matrix products, arithmetic and copies ran while one was open for 34% of the time, Pallas kernels for 23%

profile of v2, /device:TPU:11, one launch (start us, length us, event | category | flops | bytes accessed | tf_op | source)
XLA Modules:
  0.0 745.8 jit_solution(15551817006809742650)
XLA Ops:
  17.6 12.5 %all-to-all-done = bf16[8,64,1024]{2,1,0:T(8,128)(2,1)S(1)} async-done(((bf16[8,64,1024]{2,1,0:T(8,128)(2,1)}), bf16[8,64,1024]{2,1,0:T(8,128)(2,1)S(1)}, u32[]{:S(2)}, u32[]{:S(2)}) %all-to-all-start) | async-done | bytes 1048608 | tf_op jit(solution)/shard_map/all_to_all | solution.py:644
  56.3 14.0 %collective-permute-done.9.refs_4_ = bf16[256,2048]{1,0:T(8,128)(2,1)} collective-permute-done((bf16[256,2048]{1,0:T(8,128)(2,1)S(1)}, bf16[256,2048]{1,0:T(8,128)(2,1)}, u32[]{:S(2)}, u32[]{:S(2)}) %collective-permute-start.9) | collective-permute-done | bytes 1048608 | tf_op jit(solution)/shard_map/ppermute | solution.py:573
  76.5 7.9 %collective-permute-done.11 = bf16[128,2048]{1,0:T(8,128)(2,1)} collective-permute-done((bf16[128,2048]{1,0:T(8,128)(2,1)}, bf16[128,2048]{1,0:T(8,128)(2,1)}, u32[]{:S(2)}, u32[]{:S(2)}) %collective-permute-start.11) | collective-permute-done | bytes 524320 | tf_op jit(solution)/shard_map/ppermute | solution.py:577
  114.4 13.8 %collective-permute-done.14.refs_10_ = bf16[256,2048]{1,0:T(8,128)(2,1)} collective-permute-done((bf16[256,2048]{1,0:T(8,128)(2,1)}, bf16[256,2048]{1,0:T(8,128)(2,1)}, u32[]{:S(2)}, u32[]{:S(2)}) %collective-permute-start.14) | collective-permute-done | bytes 1048608 | tf_op jit(solution)/shard_map/ppermute | solution.py:577
  142.3 18.1 %project.1 = (bf16[2048,2048]{1,0:T(8,128)(2,1)}, f32[2048,1024]{1,0:T(8,128)}, f32[2048,128]{1,0:T(8,128)S(1)}) custom-call(f32[8,2048]{1,0:T(8,128)S(1)} %pad_convert_fusion.gain_ref, bf16[4,640,1024]{2,1,0:T(8,128)(2,1)} %bitcast.186, bf16[2048,128]{1,0:T(8,128)(2,1)S(1)} %pad.35.beta_ref, bf16[256,2048]{1,0:T(8,128)(2,1)S(1)} %bitcast.181, ...), custom_call_target="tpu_custom_call" | custom-call | flops 1073741824 | bytes 4194304 | tf_op jit(solution)/shard_map/project/pallas_call | solution.py:541
  170.0 22.1 %delta_forward.1 = (bf16[8,256,256]{2,1,0:T(8,128)(2,1)S(1)}, f32[8,2,2,128,128]{4,3,2,1,0:T(8,128)S(1)}) custom-call(s32[1]{0:T(128)} %bitcast.1.place_ref, f32[2048,1024]{1,0:T(8,128)} %get-tuple-element.158.pre_ref, f32[2048,128]{1,0:T(8,128)S(1)} %copy-done.5, f32[16,256]{1,0:T(8,128)S(1)} %pad.36.taps_ref, f32[8,128]{1,0:T(8,128)S(1)} %pad_convert_fusion.1.gain_ref), custom_call_target="tpu_custom_call" | custom-call | flops 1600000000 | bytes 2097152 | tf_op jit(solution)/shard_map/delta_forward/pallas_call | solution.py:266
  197.6 7.0 all-to-all-start.3
  211.1 18.3 %collective-permute-done.20 = bf16[128,2048]{1,0:T(8,128)(2,1)} collective-permute-done((bf16[128,2048]{1,0:T(8,128)(2,1)S(1)}, bf16[128,2048]{1,0:T(8,128)(2,1)}, u32[]{:S(2)}, u32[]{:S(2)}) %collective-permute-start.20) | collective-permute-done | bytes 524320 | tf_op jit(solution)/shard_map/ppermute | solution.py:577
  235.2 9.0 %assemble.1 = bf16[4,8,64,2048]{3,2,1,0:T(8,128)(2,1)} custom-call(s32[1]{0:T(128)} %bitcast.1.place_ref, bf16[4,64,2048]{2,1,0:T(8,128)(2,1)} %bitcast.24.refs_0_, bf16[4,64,2048]{2,1,0:T(8,128)(2,1)} %bitcast.25.refs_1_, bf16[4,64,2048]{2,1,0:T(8,128)(2,1)} %bitcast.26.refs_2_, bf16[4,64,2048]{2,1,0:T(8,128)(2,1)} %bitcast.27.refs_3_, ...), custom_call_target="tpu_custom_call" | custom-call | bytes 16777216 | tf_op jit(solution)/shard_map/assemble/pallas_call | solution.py:365
  253.7 21.6 %collective-permute-done.29.refs_4_ = bf16[256,2048]{1,0:T(8,128)(2,1)} collective-permute-done((bf16[256,2048]{1,0:T(8,128)(2,1)S(1)}, bf16[256,2048]{1,0:T(8,128)(2,1)}, u32[]{:S(2)}, u32[]{:S(2)}) %collective-permute-start.29) | collective-permute-done | bytes 1048608 | tf_op jit(solution)/shard_map/ppermute | solution.py:573
  280.6 9.1 %collective-permute-done.31 = bf16[128,2048]{1,0:T(8,128)(2,1)} collective-permute-done((bf16[128,2048]{1,0:T(8,128)(2,1)}, bf16[128,2048]{1,0:T(8,128)(2,1)}, u32[]{:S(2)}, u32[]{:S(2)}) %collective-permute-start.31) | collective-permute-done | bytes 524320 | tf_op jit(solution)/shard_map/ppermute | solution.py:577
  301.2 33.8 %feed_forward.2 = (bf16[2048,2048]{1,0:T(8,128)(2,1)}, bf16[2048,2048]{1,0:T(8,128)(2,1)}, bf16[2048,384]{1,0:T(8,128)(2,1)}, bf16[2048,768]{1,0:T(8,128)(2,1)},...) custom-call(bf16[2048,768]{1,0:T(8,128)(2,1)} %all-gather.15.cloned.1.call-done.gu_ref, ...), custom_call_target="tpu_custom_call" | custom-call | flops 1610612736 | bytes 8388608 | tf_op jit(solution)/shard_map/feed_forward/pallas_call | solution.py:455
  335.0 11.4 %convolution_convert_fusion.3 = bf16[2048,768]{1,0:T(8,128)(2,1)} fusion(bf16[2048,2048]{1,0:T(8,128)(2,1)} %get-tuple-element.181.n_ref, bf16[2048,768]{1,0:T(8,128)(2,1)} %get-tuple-element.185), kind=kOutput, calls=%fused_computation.3 | convolution fusion | flops 6444023808 | bytes 14680064 | tf_op jit(solution)/shard_map/ra,rb->ab/dot_general | solution.py:652
  349.2 34.8 %feed_forward.3 = (bf16[2048,320]{1,0:T(8,128)(2,1)}, bf16[2048,640]{1,0:T(8,128)(2,1)}, bf16[1024,2048]{1,0:T(8,128)(2,1)}, bf16[1024,2048]{1,0:T(8,128)(2,1)},...) custom-call(bf16[2048,640]{1,0:T(8,128)(2,1)} %all-gather.11.cloned.1.call-done.gu_ref, ...), custom_call_target="tpu_custom_call" | custom-call | flops 1342177280 | bytes 8388608 | tf_op jit(solution)/shard_map/feed_forward/pallas_call | solution.py:455
  384.2 11.1 %convolution_convert_fusion.4 = bf16[2048,640]{1,0:T(8,128)(2,1)} fusion(bf16[2048,2048]{1,0:T(8,128)(2,1)} %get-tuple-element.181.n_ref, bf16[2048,640]{1,0:T(8,128)(2,1)} %get-tuple-element.197), kind=kOutput, calls=%fused_computation.4 | convolution fusion | flops 5370019840 | bytes 13631488 | tf_op jit(solution)/shard_map/ra,rb->ab/dot_general | solution.py:652
  402.6 7.1 convolution_convert_fusion.5
  424.1 10.2 %collective-permute-done.41 = bf16[128,2048]{1,0:T(8,128)(2,1)} collective-permute-done((bf16[128,2048]{1,0:T(8,128)(2,1)S(1)}, bf16[128,2048]{1,0:T(8,128)(2,1)}, u32[]{:S(2)}, u32[]{:S(2)}) %collective-permute-start.41) | collective-permute-done | bytes 524320 | tf_op jit(solution)/shard_map/ppermute | solution.py:573
  464.5 7.4 convolution_convert_fusion.7
  507.0 30.9 %delta_backward.1 = (bf16[2048,1024]{1,0:T(8,128)(2,1)}, bf16[2048,128]{1,0:T(8,128)(2,1)S(1)}, f32[16,256]{1,0:T(8,128)S(1)}, f32[8,128]{1,0:T(8,128)S(1)}) custom-call(s32[1]{0:T(128)} %bitcast.1.place_ref, f32[2048,1024]{1,0:T(8,128)} %get-tuple-element.158.pre_ref, f32[2048,128]{1,0:T(8,128)S(1)} %copy-done.6, f32[16,256]{1,0:T(8,128)S(1)} %pad.36.taps_ref, ...), custom_call_target="tpu_custom_call" | custom-call | flops 1600000000 | bytes 2097152 | tf_op jit(solution)/shard_map/delta_backward/pallas_call | solution.py:298
  544.1 12.7 %convolution_convert_fusion.2 = bf16[2048,1024]{1,0:T(8,128)(2,1)} fusion(bf16[2048,2048]{1,0:T(8,128)(2,1)S(1)} %bitcast.189, bf16[2048,1024]{1,0:T(8,128)(2,1)} %get-tuple-element.233.dpre_ref), kind=kOutput, calls=%fused_computation.2 | convolution fusion | flops 8592031744 | bytes 16777216 | tf_op jit(solution)/shard_map/ra,rb->ab/dot_general | solution.py:652
  572.0 19.2 %pull_projections.1 = (bf16[1024,2048]{1,0:T(8,128)(2,1)}, bf16[1024,2048]{1,0:T(8,128)(2,1)}, f32[8,2048]{1,0:T(8,128)S(1)}) custom-call(bf16[2048,1024]{1,0:T(8,128)(2,1)} %get-tuple-element.233.dpre_ref, bf16[2048,128]{1,0:T(8,128)(2,1)S(1)} %get-tuple-element.234.dbeta_ref, bf16[4,640,1024]{2,1,0:T(8,128)(2,1)} %bitcast.187, ...), custom_call_target="tpu_custom_call" | custom-call | flops 1073741824 | bytes 4194304 | tf_op jit(solution)/shard_map/pull_projections/pallas_call | solution.py:497
  627.1 7.2 collective-permute-done.67
  654.8 8.5 %collective-permute-done.70 = bf16[64,2048]{1,0:T(8,128)(2,1)} collective-permute-done((bf16[64,2048]{1,0:T(8,128)(2,1)}, bf16[64,2048]{1,0:T(8,128)(2,1)}, u32[]{:S(2)}, u32[]{:S(2)}) %collective-permute-start.70) | collective-permute-done | bytes 262176 | tf_op jit(solution)/shard_map/ppermute | solution.py:691
  715.1 8.2 %all-to-all-done.7 = bf16[8,64,1024]{2,1,0:T(8,128)(2,1)S(1)} async-done(((bf16[8,64,1024]{2,1,0:T(8,128)(2,1)}), bf16[8,64,1024]{2,1,0:T(8,128)(2,1)S(1)}, u32[]{:S(2)}, u32[]{:S(2)}) %all-to-all-start.7) | async-done | bytes 1048608 | tf_op jit(solution)/shard_map/all_to_all | solution.py:644
  (492 shorter events, 371.9 us)
Async XLA Ops:
  17.5 116.9 %all-gather.9.cloned.1.call-start = ((), (), s32[]{:S(2)}) async-start(), calls=%async_computation.17 | async-start | bytes 6553600 | tf_op jit(solution)/shard_map/all_gather | solution.py:701
  47.5 52.0 %collective-permute-start.6 = (bf16[256,2048]{1,0:T(8,128)(2,1)S(1)}, bf16[256,2048]{1,0:T(8,128)(2,1)S(1)}, u32[]{:S(2)}, u32[]{:S(2)}) collective-permute-start(bf16[256,2048]{1,0:T(8,128)(2,1)S(1)} %bitcast.180), channel_id=1, source_target_pairs={{0,1},{1,0},{2,3},{3,2},{4,5},{5,4},{6,7},{7,6},{8,9},{9,8},{10,11... | collective-permute-start | bytes 3145736 | tf_op jit(solution)/shard_map/ppermute | solution.py:581
  114.1 181.4 %all-gather.13.cloned.1.call-start = ((), (), s32[]{:S(2)}) async-start(), calls=%async_computation.19 | async-start | bytes 3604480 | tf_op jit(solution)/shard_map/all_gather | solution.py:701
  204.6 93.8 %all-gather.15.cloned.1.call-start = ((), (), s32[]{:S(2)}) async-start(), calls=%async_computation.20 | async-start | bytes 3932160 | tf_op jit(solution)/shard_map/all_gather | solution.py:701
  209.2 140.1 %all-gather.11.cloned.1.call-start = ((), (), s32[]{:S(2)}) async-start(), calls=%async_computation.18 | async-start | bytes 3276800 | tf_op jit(solution)/shard_map/all_gather | solution.py:701
  252.3 42.4 %collective-permute-start.34 = (bf16[256,2048]{1,0:T(8,128)(2,1)}, bf16[256,2048]{1,0:T(8,128)(2,1)}, u32[]{:S(2)}, u32[]{:S(2)}) collective-permute-start(bf16[256,2048]{1,0:T(8,128)(2,1)} %bitcast_convert_fusion.refs_8_), channel_id=1, source_target_pairs={{0,1},{1,0},{2,3},{3,2},{4,5},{5,4},{6,7},{7,6},{8,9},{9,8},{10,11... | collective-permute-start | bytes 3145736 | tf_op jit(solution)/shard_map/ppermute | solution.py:581
  253.2 41.8 %collective-permute-start.35 = (bf16[256,2048]{1,0:T(8,128)(2,1)}, bf16[256,2048]{1,0:T(8,128)(2,1)}, u32[]{:S(2)}, u32[]{:S(2)}) collective-permute-start(bf16[256,2048]{1,0:T(8,128)(2,1)} %collective-permute-done.14.refs_10_), channel_id=1, source_target_pairs={{0,1},{1,0},{2,3},{3,2},{4,5},{5,4},{6,7},{7,6},{8,9},{9,8},{10,11... | collective-permute-start | bytes 3145736 | tf_op jit(solution)/shard_map/ppermute | solution.py:581
  253.2 42.0 %collective-permute-start.36 = (bf16[256,2048]{1,0:T(8,128)(2,1)}, bf16[256,2048]{1,0:T(8,128)(2,1)}, u32[]{:S(2)}, u32[]{:S(2)}) collective-permute-start(bf16[256,2048]{1,0:T(8,128)(2,1)} %collective-permute-done.15.refs_12_), channel_id=1, source_target_pairs={{0,1},{1,0},{2,3},{3,2},{4,5},{5,4},{6,7},{7,6},{8,9},{9,8},{10,11... | collective-permute-start | bytes 3145736 | tf_op jit(solution)/shard_map/ppermute | solution.py:581
  280.6 154.8 %reduce-scatter.5.cloned.1.call-start = ((), (), s32[]{:S(2)}) async-start(), calls=%async_computation.13 | async-start | bytes 3932160 | tf_op jit(solution)/shard_map/reduce_scatter | solution.py:697
  346.5 219.9 %reduce-scatter.7.cloned.1.call-start = ((), (), s32[]{:S(2)}) async-start(), calls=%async_computation.14 | async-start | bytes 3276800 | tf_op jit(solution)/shard_map/reduce_scatter | solution.py:697
  395.4 216.4 %reduce-scatter.9.cloned.1.call-start = ((), (), s32[]{:S(2)}) async-start(), calls=%async_computation.15 | async-start | bytes 3604480 | tf_op jit(solution)/shard_map/reduce_scatter | solution.py:697
  440.6 45.4 %collective-permute-start.46 = (bf16[1024,2048]{1,0:T(8,128)(2,1)}, bf16[1024,2048]{1,0:T(8,128)(2,1)}, u32[]{:S(2)}, u32[]{:S(2)}) collective-permute-start(bf16[1024,2048]{1,0:T(8,128)(2,1)} %get-tuple-element.217), channel_id=1, source_target_pairs={{0,1},{1,0},{2,3},{3,2},{4,5},{5,4},{6,7},{7,6},{8,9},{9,8},{10,11... | collective-permute-start | bytes 12582920 | tf_op jit(solution)/shard_map/ppermute | solution.py:581
  456.9 43.8 %collective-permute-start.45 = (bf16[1024,2048]{1,0:T(8,128)(2,1)}, bf16[1024,2048]{1,0:T(8,128)(2,1)}, u32[]{:S(2)}, u32[]{:S(2)}) collective-permute-start(bf16[1024,2048]{1,0:T(8,128)(2,1)} %convolution_convert_fusion), channel_id=1, source_target_pairs={{0,1},{1,0},{2,3},{3,2},{4,5},{5,4},{6,7},{7,6},{8,9},{9,8},{10,11... | collective-permute-start | bytes 12582920 | tf_op jit(solution)/shard_map/ppermute | solution.py:581
  480.7 171.1 %reduce-scatter.11.cloned.1.call-start = ((), (), s32[]{:S(2)}) async-start(), calls=%async_computation.16 | async-start | bytes 5242880 | tf_op jit(solution)/shard_map/reduce_scatter | solution.py:697
  495.8 42.2 %collective-permute-start.47 = (bf16[128,2048]{1,0:T(8,128)(2,1)}, bf16[128,2048]{1,0:T(8,128)(2,1)}, u32[]{:S(2)}, u32[]{:S(2)}) collective-permute-start(bf16[128,2048]{1,0:T(8,128)(2,1)} %get-tuple-element.363), channel_id=1, source_target_pairs={{0,4},{4,0},{1,5},{5,1},{2,6},{6,2},{3,7},{7,3},{8,12},{12,8},{9,1... | collective-permute-start | bytes 1572872 | tf_op jit(solution)/shard_map/ppermute | solution.py:573
  496.9 41.0 %collective-permute-start.48 = (bf16[128,2048]{1,0:T(8,128)(2,1)}, bf16[128,2048]{1,0:T(8,128)(2,1)}, u32[]{:S(2)}, u32[]{:S(2)}) collective-permute-start(bf16[128,2048]{1,0:T(8,128)(2,1)} %get-tuple-element.362), channel_id=1, source_target_pairs={{0,2},{2,0},{1,3},{3,1},{4,6},{6,4},{5,7},{7,5},{8,10},{10,8},{9,1... | collective-permute-start | bytes 1572872 | tf_op jit(solution)/shard_map/ppermute | solution.py:577
  499.0 38.9 %collective-permute-start.49 = (bf16[128,2048]{1,0:T(8,128)(2,1)}, bf16[128,2048]{1,0:T(8,128)(2,1)}, u32[]{:S(2)}, u32[]{:S(2)}) collective-permute-start(bf16[128,2048]{1,0:T(8,128)(2,1)} %get-tuple-element.360), channel_id=1, source_target_pairs={{0,4},{4,0},{1,5},{5,1},{2,6},{6,2},{3,7},{7,3},{8,12},{12,8},{9,1... | collective-permute-start | bytes 1572872 | tf_op jit(solution)/shard_map/ppermute | solution.py:573
  568.8 45.4 %collective-permute-start.53 = (bf16[128,2048]{1,0:T(8,128)(2,1)}, bf16[128,2048]{1,0:T(8,128)(2,1)}, u32[]{:S(2)}, u32[]{:S(2)}) collective-permute-start(bf16[128,2048]{1,0:T(8,128)(2,1)} %get-tuple-element.357), channel_id=1, source_target_pairs={{0,4},{4,0},{1,5},{5,1},{2,6},{6,2},{3,7},{7,3},{8,12},{12,8},{9,1... | collective-permute-start | bytes 1572872 | tf_op jit(solution)/shard_map/ppermute | solution.py:573
  569.1 45.1 %collective-permute-start.54 = (bf16[128,2048]{1,0:T(8,128)(2,1)}, bf16[128,2048]{1,0:T(8,128)(2,1)}, u32[]{:S(2)}, u32[]{:S(2)}) collective-permute-start(bf16[128,2048]{1,0:T(8,128)(2,1)} %get-tuple-element.356), channel_id=1, source_target_pairs={{0,2},{2,0},{1,3},{3,1},{4,6},{6,4},{5,7},{7,5},{8,10},{10,8},{9,1... | collective-permute-start | bytes 1572872 | tf_op jit(solution)/shard_map/ppermute | solution.py:577
  570.9 43.3 %collective-permute-start.55 = (bf16[128,2048]{1,0:T(8,128)(2,1)}, bf16[128,2048]{1,0:T(8,128)(2,1)}, u32[]{:S(2)}, u32[]{:S(2)}) collective-permute-start(bf16[128,2048]{1,0:T(8,128)(2,1)} %get-tuple-element.354), channel_id=1, source_target_pairs={{0,4},{4,0},{1,5},{5,1},{2,6},{6,2},{3,7},{7,3},{8,12},{12,8},{9,1... | collective-permute-start | bytes 1572872 | tf_op jit(solution)/shard_map/ppermute | solution.py:573
  685.8 46.3 %collective-permute-start.58 = (bf16[128,2048]{1,0:T(8,128)(2,1)}, bf16[128,2048]{1,0:T(8,128)(2,1)}, u32[]{:S(2)}, u32[]{:S(2)}) collective-permute-start(bf16[128,2048]{1,0:T(8,128)(2,1)} %slice.402), channel_id=1, source_target_pairs={{0,4},{4,0},{1,5},{5,1},{2,6},{6,2},{3,7},{7,3},{8,12},{12,8},{9,1... | collective-permute-start | bytes 1572872 | tf_op jit(solution)/shard_map/ppermute | solution.py:573
  686.7 46.8 %collective-permute-start.63 = (bf16[128,2048]{1,0:T(8,128)(2,1)}, bf16[128,2048]{1,0:T(8,128)(2,1)}, u32[]{:S(2)}, u32[]{:S(2)}) collective-permute-start(bf16[128,2048]{1,0:T(8,128)(2,1)} %slice.407), channel_id=1, source_target_pairs={{0,2},{2,0},{1,3},{3,1},{4,6},{6,4},{5,7},{7,5},{8,10},{10,8},{9,1... | collective-permute-start | bytes 1572872 | tf_op jit(solution)/shard_map/ppermute | solution.py:577
  690.1 42.0 %collective-permute-start.61 = (bf16[128,2048]{1,0:T(8,128)(2,1)}, bf16[128,2048]{1,0:T(8,128)(2,1)}, u32[]{:S(2)}, u32[]{:S(2)}) collective-permute-start(bf16[128,2048]{1,0:T(8,128)(2,1)} %add_convert_fusion.16), channel_id=1, source_target_pairs={{0,2},{2,0},{1,3},{3,1},{4,6},{6,4},{5,7},{7,5},{8,10},{10,8},{9,1... | collective-permute-start | bytes 1572872 | tf_op jit(solution)/shard_map/ppermute | solution.py:577
  692.1 41.4 %collective-permute-start.62 = (bf16[128,2048]{1,0:T(8,128)(2,1)}, bf16[128,2048]{1,0:T(8,128)(2,1)}, u32[]{:S(2)}, u32[]{:S(2)}) collective-permute-start(bf16[128,2048]{1,0:T(8,128)(2,1)} %add_convert_fusion.15), channel_id=1, source_target_pairs={{0,4},{4,0},{1,5},{5,1},{2,6},{6,2},{3,7},{7,3},{8,12},{12,8},{9,1... | collective-permute-start | bytes 1572872 | tf_op jit(solution)/shard_map/ppermute | solution.py:573
  (124 other events, 1632.4 us)
Sparse Core Ops, SparseCore 0:
  31.4 98.6 all-gather.8
  134.5 58.0 all-gather.12
  209.3 61.5 all-gather.14
  280.7 54.0 all-gather.10
  346.6 60.3 reduce-scatter.4
  409.2 51.6 reduce-scatter.6
  463.1 56.1 reduce-scatter.8
  557.0 80.4 reduce-scatter.10

commit v3 on v2

--- a/solution.py
+++ b/solution.py
@@ -806,8 +806,8 @@
         place, pre, beta_pre, own_taps, head_rows, team, own_heads, size
     )
     d_down = team_pieces(after(d_near, out_near))
-    gated, d_down[6], out_near = after((gated, d_down[6], out_near))
-    gated, out_far = after((team_exchange(gated), far_piece(out_near)))
+    gated, d_down[6], out_far = after((gated, d_down[6], far_piece(out_near)))
+    gated, out_near, out_far = after((team_exchange(gated), out_near, out_far))
     out_pieces = [v.reshape(groups, span, width) for v in team_pieces(out_near, out_far)]
     gated = gated.transpose(1, 0, 2).reshape(length, width)
     out_full = assemble(place, out_pieces).reshape(width, width)
@@ -871,20 +871,24 @@
     final_sum = team_end(final_started)
     grads = weight_grad(normed, d_pre).astype(BF)
     mixer_grads = group_scatter(grads)
-    d_pre, grads, final_sum, ff_grads[1] = after((d_pre, grads, final_sum, ff_grads[1]))
+    d_pre, grads, final_sum, ff_grads[1], grad_ffdown = after(
+        (d_pre, grads, final_sum, ff_grads[1], grad_ffdown)
+    )
     out_started = team_start(out_terms, final_sum)
     grad_beta = weight_grad(normed, d_beta)[:, :own_heads]
     dn_even, dn_odd, attn_part = pull_projections(
         d_pre, d_beta, x_pieces, mixer_all, beta_w
     )
-    dn_even, dn_odd, out_started, grad_ffdown = after((dn_even, dn_odd, out_started, grad_ffdown))
+    dn_even, dn_odd, out_started = after((dn_even, dn_odd, out_started))
     grad_out = team_end(out_started)
     in_terms = team_terms(dn_even, dn_odd)
+    mixed = (resid + final_sum).astype(BF).reshape(seqs, length, width)
+    gu_home = [gu_home_first, team_exchange(after(ff_grads[1], out_started))]
+    in_terms, gu_home = after((in_terms, gu_home))
+    in_started = team_start(in_terms)
+    in_started, mixer_grads, grad_out = after((in_started, mixer_grads, grad_out))
+
     grad_out_home = group_sum_small(grad_out.reshape(groups, span, width), groups)
-    mixed = (resid + final_sum).astype(BF).reshape(seqs, length, width)
-    in_terms, mixer_grads = after((in_terms, mixer_grads))
-    in_started = team_start(in_terms, out_started)
-    gu_home = [gu_home_first, team_exchange(after(ff_grads[1], *in_terms[1:]))]
 
     ff_home = [[], []]
     for gu, (low, high) in zip(gu_home, ff_parts):
@@ -916,6 +920,7 @@
         axis=1,
     )
     kinds = extra.shape[1]
+    extra = after(extra, *in_terms[1:])
     extra = extra.reshape(groups, team, span * kinds)
     extra = jnp.pad(extra, ((0, 0), (0, 0), (0, -extra.shape[2] % 128)))
     extra = team_exchange(group_sum_small(extra, groups))

time: 758 us -> 752 us (level)
    reduce_scatter x4, waiting for transfers between devices: 0.01 us -> 16.5 us  [group_scatter(): return lax.psum_scatter(v, 'g', scatter_dimension=0, tiled=True)]
    ppermute x21, waiting for transfers between devices: 65.1 us -> 51.2 us  [swap_b(): return lax.ppermute(v, 'b', SWAP)]
    all_to_all x9, waiting for transfers between devices: 28.3 us -> 38.4 us  [team_exchange(): return lax.all_to_all(v, TEAM, 0, 0, tiled=True)]
    unnamed x134 -> x138, local copies, waits for them, and re-layouts: 25.4 us -> 23.6 us
  transfers between devices with their start and end apart: 89 -> 89, of which waited for: 29 -> 29; matrix products, arithmetic and copies ran while one was open for 34% -> 29% of each run, Pallas kernels for 23% -> 18%
where the time goes in v3:
time: 752 us; the launch traced here: 739 us
  waiting for transfers between devices  176 us (23%)
  Pallas kernels  168 us (22%)
  local copies, waits for them, and re-layouts  117 us (16%)
  starting transfers between devices  115 us (15%)
  other arithmetic  73.6 us (10%)
  matrix products  72.5 us (10%)
  between operations  17.8 us (2%)
    pallas_call x2, Pallas kernels, feed_forward(): pl.pallas_call(ff_first_kernel if more is None else ff_more_kernel, grid=...  68.5 us
    dot_general x8, matrix products, weight_grad(): return jnp.einsum('ra,rb->ab', left, right, preferred_element_type=F32)  58.9 us
    ppermute x21, waiting for transfers between devices, swap_b(): return lax.ppermute(v, 'b', SWAP)  51.2 us
    all_to_all x9, starting transfers between devices, team_exchange(): return lax.all_to_all(v, TEAM, 0, 0, tiled=True)  49.3 us
    ppermute x21, waiting for transfers between devices, swap_a(): return lax.ppermute(v, 'a', SWAP)  46.8 us
    all_to_all x9, waiting for transfers between devices, team_exchange(): return lax.all_to_all(v, TEAM, 0, 0, tiled=True)  38.4 us
    convert_element_type x12, other arithmetic, plus(): return (left.astype(F32) + right.astype(F32)).astype(BF)  36 us
    pallas_call x1, Pallas kernels, delta_backward(): pl.pallas_call(functools.partial(bwd_kernel, heads=heads, size=size, leng...  30.9 us
  transfers between devices with their start and end apart: 89, of which 29 were waited for; matrix products, arithmetic and copies ran while one was open for 29% of the time, Pallas kernels for 18%

profile of v3, /device:TPU:11, one launch (start us, length us, event | category | flops | bytes accessed | tf_op | source)
XLA Modules:
  0.0 738.9 jit_solution(6025721387207544524)
XLA Ops:
  17.6 12.5 %all-to-all-done = bf16[8,64,1024]{2,1,0:T(8,128)(2,1)S(1)} async-done(((bf16[8,64,1024]{2,1,0:T(8,128)(2,1)}), bf16[8,64,1024]{2,1,0:T(8,128)(2,1)S(1)}, u32[]{:S(2)}, u32[]{:S(2)}) %all-to-all-start) | async-done | bytes 1048608 | tf_op jit(solution)/shard_map/all_to_all | solution.py:644
  56.3 14.0 %collective-permute-done.9.refs_4_ = bf16[256,2048]{1,0:T(8,128)(2,1)} collective-permute-done((bf16[256,2048]{1,0:T(8,128)(2,1)S(1)}, bf16[256,2048]{1,0:T(8,128)(2,1)}, u32[]{:S(2)}, u32[]{:S(2)}) %collective-permute-start.9) | collective-permute-done | bytes 1048608 | tf_op jit(solution)/shard_map/ppermute | solution.py:573
  76.5 7.9 %collective-permute-done.11 = bf16[128,2048]{1,0:T(8,128)(2,1)} collective-permute-done((bf16[128,2048]{1,0:T(8,128)(2,1)}, bf16[128,2048]{1,0:T(8,128)(2,1)}, u32[]{:S(2)}, u32[]{:S(2)}) %collective-permute-start.11) | collective-permute-done | bytes 524320 | tf_op jit(solution)/shard_map/ppermute | solution.py:577
  114.3 13.9 %collective-permute-done.14.refs_10_ = bf16[256,2048]{1,0:T(8,128)(2,1)} collective-permute-done((bf16[256,2048]{1,0:T(8,128)(2,1)}, bf16[256,2048]{1,0:T(8,128)(2,1)}, u32[]{:S(2)}, u32[]{:S(2)}) %collective-permute-start.14) | collective-permute-done | bytes 1048608 | tf_op jit(solution)/shard_map/ppermute | solution.py:577
  142.2 18.1 %project.1 = (bf16[2048,2048]{1,0:T(8,128)(2,1)}, f32[2048,1024]{1,0:T(8,128)}, f32[2048,128]{1,0:T(8,128)S(1)}) custom-call(f32[8,2048]{1,0:T(8,128)S(1)} %pad_convert_fusion.gain_ref, bf16[4,640,1024]{2,1,0:T(8,128)(2,1)} %bitcast.186, bf16[2048,128]{1,0:T(8,128)(2,1)S(1)} %pad.35.beta_ref, bf16[256,2048]{1,0:T(8,128)(2,1)S(1)} %bitcast.181, ...), custom_call_target="tpu_custom_call" | custom-call | flops 1073741824 | bytes 4194304 | tf_op jit(solution)/shard_map/project/pallas_call | solution.py:541
  172.5 22.1 %delta_forward.1 = (bf16[8,256,256]{2,1,0:T(8,128)(2,1)S(1)}, f32[8,2,2,128,128]{4,3,2,1,0:T(8,128)S(1)}) custom-call(s32[1]{0:T(128)} %bitcast.1.place_ref, f32[2048,1024]{1,0:T(8,128)} %get-tuple-element.170.pre_ref, f32[2048,128]{1,0:T(8,128)S(1)} %copy-done.5, f32[16,256]{1,0:T(8,128)S(1)} %pad.36.taps_ref, f32[8,128]{1,0:T(8,128)S(1)} %pad_convert_fusion.1.gain_ref), custom_call_target="tpu_custom_call" | custom-call | flops 1600000000 | bytes 2097152 | tf_op jit(solution)/shard_map/delta_forward/pallas_call | solution.py:266
  199.9 8.4 %all-to-all-start.3 = ((bf16[8,256,256]{2,1,0:T(8,128)(2,1)}), bf16[8,256,256]{2,1,0:T(8,128)(2,1)}, u32[]{:S(2)}, u32[]{:S(2)}) async-start(bf16[8,256,256]{2,1,0:T(8,128)(2,1)} %copy-done.9), calls=%async_computation.3 | async-start | bytes 2097152 | tf_op jit(solution)/shard_map/all_to_all | solution.py:644
  209.1 11.9 %all-to-all-done.3 = bf16[8,256,256]{2,1,0:T(8,128)(2,1)} async-done(((bf16[8,256,256]{2,1,0:T(8,128)(2,1)}), bf16[8,256,256]{2,1,0:T(8,128)(2,1)}, u32[]{:S(2)}, u32[]{:S(2)}) %all-to-all-start.3) | async-done | bytes 1048608 | tf_op jit(solution)/shard_map/all_to_all | solution.py:644
  229.9 9.0 %assemble.1 = bf16[4,8,64,2048]{3,2,1,0:T(8,128)(2,1)} custom-call(s32[1]{0:T(128)} %bitcast.1.place_ref, bf16[4,64,2048]{2,1,0:T(8,128)(2,1)} %bitcast.24.refs_0_, bf16[4,64,2048]{2,1,0:T(8,128)(2,1)} %bitcast.25.refs_1_, bf16[4,64,2048]{2,1,0:T(8,128)(2,1)} %bitcast.26.refs_2_, bf16[4,64,2048]{2,1,0:T(8,128)(2,1)} %bitcast.27.refs_3_, ...), custom_call_target="tpu_custom_call" | custom-call | bytes 16777216 | tf_op jit(solution)/shard_map/assemble/pallas_call | solution.py:365
  248.4 21.5 %collective-permute-done.29.refs_4_ = bf16[256,2048]{1,0:T(8,128)(2,1)} collective-permute-done((bf16[256,2048]{1,0:T(8,128)(2,1)S(1)}, bf16[256,2048]{1,0:T(8,128)(2,1)}, u32[]{:S(2)}, u32[]{:S(2)}) %collective-permute-start.29) | collective-permute-done | bytes 1048608 | tf_op jit(solution)/shard_map/ppermute | solution.py:573
  275.5 8.8 %collective-permute-done.31 = bf16[128,2048]{1,0:T(8,128)(2,1)} collective-permute-done((bf16[128,2048]{1,0:T(8,128)(2,1)}, bf16[128,2048]{1,0:T(8,128)(2,1)}, u32[]{:S(2)}, u32[]{:S(2)}) %collective-permute-start.31) | collective-permute-done | bytes 524320 | tf_op jit(solution)/shard_map/ppermute | solution.py:577
  295.8 33.8 %feed_forward.2 = (bf16[2048,2048]{1,0:T(8,128)(2,1)}, bf16[2048,2048]{1,0:T(8,128)(2,1)}, bf16[2048,384]{1,0:T(8,128)(2,1)}, bf16[2048,768]{1,0:T(8,128)(2,1)},...) custom-call(bf16[2048,768]{1,0:T(8,128)(2,1)} %all-gather.15.cloned.1.call-done.gu_ref, ...), custom_call_target="tpu_custom_call" | custom-call | flops 1610612736 | bytes 8388608 | tf_op jit(solution)/shard_map/feed_forward/pallas_call | solution.py:455
  329.6 11.4 %convolution_convert_fusion.3 = bf16[2048,768]{1,0:T(8,128)(2,1)} fusion(bf16[2048,2048]{1,0:T(8,128)(2,1)} %get-tuple-element.194.n_ref, bf16[2048,768]{1,0:T(8,128)(2,1)} %get-tuple-element.198), kind=kOutput, calls=%fused_computation.3 | convolution fusion | flops 6444023808 | bytes 14680064 | tf_op jit(solution)/shard_map/ra,rb->ab/dot_general | solution.py:652
  341.0 34.7 %feed_forward.3 = (bf16[2048,320]{1,0:T(8,128)(2,1)}, bf16[2048,640]{1,0:T(8,128)(2,1)}, bf16[1024,2048]{1,0:T(8,128)(2,1)}, bf16[1024,2048]{1,0:T(8,128)(2,1)},...) custom-call(bf16[2048,640]{1,0:T(8,128)(2,1)} %all-gather.11.cloned.1.call-done.gu_ref, ...), custom_call_target="tpu_custom_call" | custom-call | flops 1342177280 | bytes 8388608 | tf_op jit(solution)/shard_map/feed_forward/pallas_call | solution.py:455
  376.6 11.1 %convolution_convert_fusion.4 = bf16[2048,640]{1,0:T(8,128)(2,1)} fusion(bf16[2048,2048]{1,0:T(8,128)(2,1)} %get-tuple-element.194.n_ref, bf16[2048,640]{1,0:T(8,128)(2,1)} %get-tuple-element.210), kind=kOutput, calls=%fused_computation.4 | convolution fusion | flops 5370019840 | bytes 13631488 | tf_op jit(solution)/shard_map/ra,rb->ab/dot_general | solution.py:652
  398.6 7.2 convolution_convert_fusion.5
  410.6 8.8 %collective-permute-done.41 = bf16[128,2048]{1,0:T(8,128)(2,1)} collective-permute-done((bf16[128,2048]{1,0:T(8,128)(2,1)S(1)}, bf16[128,2048]{1,0:T(8,128)(2,1)}, u32[]{:S(2)}, u32[]{:S(2)}) %collective-permute-start.41) | collective-permute-done | bytes 524320 | tf_op jit(solution)/shard_map/ppermute | solution.py:573
  420.1 16.5 %reduce-scatter.5.cloned.1.call-done = bf16[512,768]{1,0:T(8,128)(2,1)} async-done(((bf16[2048,768]{1,0:T(8,128)(2,1)}), bf16[512,768]{1,0:T(8,128)(2,1)}) %reduce-scatter.5.cloned.1.call-update) | async-done | bytes 786448 | tf_op jit(solution)/shard_map/reduce_scatter | solution.py:697
  443.1 8.2 %collective-permute-done.43 = bf16[128,2048]{1,0:T(8,128)(2,1)S(1)} collective-permute-done((bf16[128,2048]{1,0:T(8,128)(2,1)S(1)}, bf16[128,2048]{1,0:T(8,128)(2,1)S(1)}, u32[]{:S(2)}, u32[]{:S(2)}) %collective-permute-start.43) | collective-permute-done | bytes 524320 | tf_op jit(solution)/shard_map/ppermute | solution.py:577
  465.2 7.4 %convolution_convert_fusion.7 = bf16[256,2048]{1,0:T(8,128)(2,1)} fusion(bf16[2048,2048]{1,0:T(8,128)(2,1)} %bitcast.184, f32[256,2048]{1,0:T(8,128)} %copy-done.13), kind=kOutput, calls=%fused_computation.11 | convolution fusion | flops 2148532224 | bytes 11534336 | tf_op jit(solution)/shard_map/rb,ab->ra/dot_general | solution.py:656
  507.5 30.9 %delta_backward.1 = (bf16[2048,1024]{1,0:T(8,128)(2,1)}, bf16[2048,128]{1,0:T(8,128)(2,1)S(1)}, f32[16,256]{1,0:T(8,128)S(1)}, f32[8,128]{1,0:T(8,128)S(1)}) custom-call(s32[1]{0:T(128)} %bitcast.1.place_ref, f32[2048,1024]{1,0:T(8,128)} %get-tuple-element.170.pre_ref, f32[2048,128]{1,0:T(8,128)S(1)} %copy-done.6, f32[16,256]{1,0:T(8,128)S(1)} %pad.36.taps_ref, ...), custom_call_target="tpu_custom_call" | custom-call | flops 1600000000 | bytes 2097152 | tf_op jit(solution)/shard_map/delta_backward/pallas_call | solution.py:298
  544.6 13.0 %convolution_convert_fusion.2 = bf16[2048,1024]{1,0:T(8,128)(2,1)} fusion(bf16[2048,2048]{1,0:T(8,128)(2,1)S(1)} %bitcast.189, bf16[2048,1024]{1,0:T(8,128)(2,1)} %get-tuple-element.247.dpre_ref), kind=kOutput, calls=%fused_computation.2 | convolution fusion | flops 8592031744 | bytes 16777216 | tf_op jit(solution)/shard_map/ra,rb->ab/dot_general | solution.py:652
  573.5 19.2 %pull_projections.1 = (bf16[1024,2048]{1,0:T(8,128)(2,1)}, bf16[1024,2048]{1,0:T(8,128)(2,1)}, f32[8,2048]{1,0:T(8,128)S(1)}) custom-call(bf16[2048,1024]{1,0:T(8,128)(2,1)} %get-tuple-element.247.dpre_ref, bf16[2048,128]{1,0:T(8,128)(2,1)S(1)} %get-tuple-element.248.dbeta_ref, bf16[4,640,1024]{2,1,0:T(8,128)(2,1)} %bitcast.187, ...), custom_call_target="tpu_custom_call" | custom-call | flops 1073741824 | bytes 4194304 | tf_op jit(solution)/shard_map/pull_projections/pallas_call | solution.py:497
  697.5 8.3 %collective-permute-done.70 = bf16[64,2048]{1,0:T(8,128)(2,1)} collective-permute-done((bf16[64,2048]{1,0:T(8,128)(2,1)}, bf16[64,2048]{1,0:T(8,128)(2,1)}, u32[]{:S(2)}, u32[]{:S(2)}) %collective-permute-start.70) | collective-permute-done | bytes 262176 | tf_op jit(solution)/shard_map/ppermute | solution.py:691
  (496 shorter events, 362.4 us)
Async XLA Ops:
  17.5 116.9 %all-gather.9.cloned.1.call-start = ((), (), s32[]{:S(2)}) async-start(), calls=%async_computation.17 | async-start | bytes 6553600 | tf_op jit(solution)/shard_map/all_gather | solution.py:701
  47.5 52.0 %collective-permute-start.6 = (bf16[256,2048]{1,0:T(8,128)(2,1)S(1)}, bf16[256,2048]{1,0:T(8,128)(2,1)S(1)}, u32[]{:S(2)}, u32[]{:S(2)}) collective-permute-start(bf16[256,2048]{1,0:T(8,128)(2,1)S(1)} %bitcast.180), channel_id=1, source_target_pairs={{0,1},{1,0},{2,3},{3,2},{4,5},{5,4},{6,7},{7,6},{8,9},{9,8},{10,11... | collective-permute-start | bytes 3145736 | tf_op jit(solution)/shard_map/ppermute | solution.py:581
  98.1 30.1 %collective-permute-start.14 = (bf16[256,2048]{1,0:T(8,128)(2,1)}, bf16[256,2048]{1,0:T(8,128)(2,1)}, u32[]{:S(2)}, u32[]{:S(2)}) collective-permute-start(bf16[256,2048]{1,0:T(8,128)(2,1)} %bitcast_convert_fusion.refs_8_), channel_id=1, source_target_pairs={{0,2},{2,0},{1,3},{3,1},{4,6},{6,4},{5,7},{7,5},{8,10},{10,8},{9,1... | collective-permute-start | bytes 3145736 | tf_op jit(solution)/shard_map/ppermute | solution.py:577
  114.1 176.1 %all-gather.13.cloned.1.call-start = ((), (), s32[]{:S(2)}) async-start(), calls=%async_computation.19 | async-start | bytes 3604480 | tf_op jit(solution)/shard_map/all_gather | solution.py:701
  164.5 30.2 %collective-permute-start.18 = (bf16[128,2048]{1,0:T(8,128)(2,1)}, bf16[128,2048]{1,0:T(8,128)(2,1)}, u32[]{:S(2)}, u32[]{:S(2)}) collective-permute-start(bf16[128,2048]{1,0:T(8,128)(2,1)} %slice.343), channel_id=1, source_target_pairs={{0,2},{2,0},{1,3},{3,1},{4,6},{6,4},{5,7},{7,5},{8,10},{10,8},{9,1... | collective-permute-start | bytes 1572872 | tf_op jit(solution)/shard_map/ppermute | solution.py:577
  167.3 29.6 %collective-permute-start.19 = (bf16[128,2048]{1,0:T(8,128)(2,1)}, bf16[128,2048]{1,0:T(8,128)(2,1)}, u32[]{:S(2)}, u32[]{:S(2)}) collective-permute-start(bf16[128,2048]{1,0:T(8,128)(2,1)} %slice.344), channel_id=1, source_target_pairs={{0,4},{4,0},{1,5},{5,1},{2,6},{6,2},{3,7},{7,3},{8,12},{12,8},{9,1... | collective-permute-start | bytes 1572872 | tf_op jit(solution)/shard_map/ppermute | solution.py:573
  208.4 87.2 %all-gather.15.cloned.1.call-start = ((), (), s32[]{:S(2)}) async-start(), calls=%async_computation.20 | async-start | bytes 3932160 | tf_op jit(solution)/shard_map/all_gather | solution.py:701
  209.1 131.9 %all-gather.11.cloned.1.call-start = ((), (), s32[]{:S(2)}) async-start(), calls=%async_computation.18 | async-start | bytes 3276800 | tf_op jit(solution)/shard_map/all_gather | solution.py:701
  246.9 42.6 %collective-permute-start.34 = (bf16[256,2048]{1,0:T(8,128)(2,1)}, bf16[256,2048]{1,0:T(8,128)(2,1)}, u32[]{:S(2)}, u32[]{:S(2)}) collective-permute-start(bf16[256,2048]{1,0:T(8,128)(2,1)} %bitcast_convert_fusion.refs_8_), channel_id=1, source_target_pairs={{0,1},{1,0},{2,3},{3,2},{4,5},{5,4},{6,7},{7,6},{8,9},{9,8},{10,11... | collective-permute-start | bytes 3145736 | tf_op jit(solution)/shard_map/ppermute | solution.py:581
  247.9 41.8 %collective-permute-start.35 = (bf16[256,2048]{1,0:T(8,128)(2,1)}, bf16[256,2048]{1,0:T(8,128)(2,1)}, u32[]{:S(2)}, u32[]{:S(2)}) collective-permute-start(bf16[256,2048]{1,0:T(8,128)(2,1)} %collective-permute-done.14.refs_10_), channel_id=1, source_target_pairs={{0,1},{1,0},{2,3},{3,2},{4,5},{5,4},{6,7},{7,6},{8,9},{9,8},{10,11... | collective-permute-start | bytes 3145736 | tf_op jit(solution)/shard_map/ppermute | solution.py:581
  247.9 42.1 %collective-permute-start.36 = (bf16[256,2048]{1,0:T(8,128)(2,1)}, bf16[256,2048]{1,0:T(8,128)(2,1)}, u32[]{:S(2)}, u32[]{:S(2)}) collective-permute-start(bf16[256,2048]{1,0:T(8,128)(2,1)} %collective-permute-done.15.refs_12_), channel_id=1, source_target_pairs={{0,1},{1,0},{2,3},{3,2},{4,5},{5,4},{6,7},{7,6},{8,9},{9,8},{10,11... | collective-permute-start | bytes 3145736 | tf_op jit(solution)/shard_map/ppermute | solution.py:581
  275.2 161.4 %reduce-scatter.5.cloned.1.call-start = ((), (), s32[]{:S(2)}) async-start(), calls=%async_computation.13 | async-start | bytes 3932160 | tf_op jit(solution)/shard_map/reduce_scatter | solution.py:697
  376.2 185.9 %reduce-scatter.9.cloned.1.call-start = ((), (), s32[]{:S(2)}) async-start(), calls=%async_computation.15 | async-start | bytes 3604480 | tf_op jit(solution)/shard_map/reduce_scatter | solution.py:697
  436.6 127.9 %reduce-scatter.7.cloned.1.call-start = ((), (), s32[]{:S(2)}) async-start(), calls=%async_computation.14 | async-start | bytes 3276800 | tf_op jit(solution)/shard_map/reduce_scatter | solution.py:697
  441.9 44.8 %collective-permute-start.46 = (bf16[1024,2048]{1,0:T(8,128)(2,1)}, bf16[1024,2048]{1,0:T(8,128)(2,1)}, u32[]{:S(2)}, u32[]{:S(2)}) collective-permute-start(bf16[1024,2048]{1,0:T(8,128)(2,1)} %get-tuple-element.230), channel_id=1, source_target_pairs={{0,1},{1,0},{2,3},{3,2},{4,5},{5,4},{6,7},{7,6},{8,9},{9,8},{10,11... | collective-permute-start | bytes 12582920 | tf_op jit(solution)/shard_map/ppermute | solution.py:581
  459.8 41.6 %collective-permute-start.45 = (bf16[1024,2048]{1,0:T(8,128)(2,1)}, bf16[1024,2048]{1,0:T(8,128)(2,1)}, u32[]{:S(2)}, u32[]{:S(2)}) collective-permute-start(bf16[1024,2048]{1,0:T(8,128)(2,1)} %convolution_convert_fusion), channel_id=1, source_target_pairs={{0,1},{1,0},{2,3},{3,2},{4,5},{5,4},{6,7},{7,6},{8,9},{9,8},{10,11... | collective-permute-start | bytes 12582920 | tf_op jit(solution)/shard_map/ppermute | solution.py:581
  481.4 180.0 %reduce-scatter.11.cloned.1.call-start = ((), (), s32[]{:S(2)}) async-start(), calls=%async_computation.16 | async-start | bytes 5242880 | tf_op jit(solution)/shard_map/reduce_scatter | solution.py:697
  496.5 41.9 %collective-permute-start.47 = (bf16[128,2048]{1,0:T(8,128)(2,1)}, bf16[128,2048]{1,0:T(8,128)(2,1)}, u32[]{:S(2)}, u32[]{:S(2)}) collective-permute-start(bf16[128,2048]{1,0:T(8,128)(2,1)} %get-tuple-element.391), channel_id=1, source_target_pairs={{0,4},{4,0},{1,5},{5,1},{2,6},{6,2},{3,7},{7,3},{8,12},{12,8},{9,1... | collective-permute-start | bytes 1572872 | tf_op jit(solution)/shard_map/ppermute | solution.py:573
  497.6 40.8 %collective-permute-start.48 = (bf16[128,2048]{1,0:T(8,128)(2,1)}, bf16[128,2048]{1,0:T(8,128)(2,1)}, u32[]{:S(2)}, u32[]{:S(2)}) collective-permute-start(bf16[128,2048]{1,0:T(8,128)(2,1)} %get-tuple-element.390), channel_id=1, source_target_pairs={{0,2},{2,0},{1,3},{3,1},{4,6},{6,4},{5,7},{7,5},{8,10},{10,8},{9,1... | collective-permute-start | bytes 1572872 | tf_op jit(solution)/shard_map/ppermute | solution.py:577
  499.6 38.8 %collective-permute-start.49 = (bf16[128,2048]{1,0:T(8,128)(2,1)}, bf16[128,2048]{1,0:T(8,128)(2,1)}, u32[]{:S(2)}, u32[]{:S(2)}) collective-permute-start(bf16[128,2048]{1,0:T(8,128)(2,1)} %get-tuple-element.388), channel_id=1, source_target_pairs={{0,4},{4,0},{1,5},{5,1},{2,6},{6,2},{3,7},{7,3},{8,12},{12,8},{9,1... | collective-permute-start | bytes 1572872 | tf_op jit(solution)/shard_map/ppermute | solution.py:573
  501.0 37.4 %collective-permute-start.50 = (bf16[128,2048]{1,0:T(8,128)(2,1)}, bf16[128,2048]{1,0:T(8,128)(2,1)}, u32[]{:S(2)}, u32[]{:S(2)}) collective-permute-start(bf16[128,2048]{1,0:T(8,128)(2,1)} %get-tuple-element.386), channel_id=1, source_target_pairs={{0,2},{2,0},{1,3},{3,1},{4,6},{6,4},{5,7},{7,5},{8,10},{10,8},{9,1... | collective-permute-start | bytes 1572872 | tf_op jit(solution)/shard_map/ppermute | solution.py:577
  629.7 30.4 %collective-permute-start.58 = (bf16[128,2048]{1,0:T(8,128)(2,1)}, bf16[128,2048]{1,0:T(8,128)(2,1)}, u32[]{:S(2)}, u32[]{:S(2)}) collective-permute-start(bf16[128,2048]{1,0:T(8,128)(2,1)} %get-tuple-element.379), channel_id=1, source_target_pairs={{0,4},{4,0},{1,5},{5,1},{2,6},{6,2},{3,7},{7,3},{8,12},{12,8},{9,1... | collective-permute-start | bytes 1572872 | tf_op jit(solution)/shard_map/ppermute | solution.py:573
  630.5 29.7 %collective-permute-start.59 = (bf16[128,2048]{1,0:T(8,128)(2,1)}, bf16[128,2048]{1,0:T(8,128)(2,1)}, u32[]{:S(2)}, u32[]{:S(2)}) collective-permute-start(bf16[128,2048]{1,0:T(8,128)(2,1)} %get-tuple-element.378), channel_id=1, source_target_pairs={{0,2},{2,0},{1,3},{3,1},{4,6},{6,4},{5,7},{7,5},{8,10},{10,8},{9,1... | collective-permute-start | bytes 1572872 | tf_op jit(solution)/shard_map/ppermute | solution.py:577
  687.4 35.7 %all-to-all-start.8 = ((bf16[8,64,1024]{2,1,0:T(8,128)(2,1)}), bf16[8,64,1024]{2,1,0:T(8,128)(2,1)S(1)}, u32[]{:S(2)}, u32[]{:S(2)}) async-start(bf16[8,64,1024]{2,1,0:T(8,128)(2,1)} %bitcast.217), calls=%async_computation.12 | async-start | bytes 2097152 | tf_op jit(solution)/shard_map/all_to_all | solution.py:644
  (126 other events, 1564.3 us)
Sparse Core Ops, SparseCore 0:
  31.4 98.6 all-gather.8
  134.5 58.0 all-gather.12
  210.8 61.8 all-gather.14
  275.3 54.0 all-gather.10
  376.3 60.2 reduce-scatter.4
  438.8 56.0 reduce-scatter.8
  497.1 51.6 reduce-scatter.6
  572.1 81.6 reduce-scatter.10

commit v4 on v3

--- a/solution.py
+++ b/solution.py
@@ -884,9 +884,9 @@
     in_terms = team_terms(dn_even, dn_odd)
     mixed = (resid + final_sum).astype(BF).reshape(seqs, length, width)
     gu_home = [gu_home_first, team_exchange(after(ff_grads[1], out_started))]
-    in_terms, gu_home = after((in_terms, gu_home))
+    in_terms, gu_home, mixer_grads = after((in_terms, gu_home, mixer_grads))
     in_started = team_start(in_terms)
-    in_started, mixer_grads, grad_out = after((in_started, mixer_grads, grad_out))
+    in_started, gu_home, grad_out = after((in_started, gu_home, grad_out))
 
     grad_out_home = group_sum_small(grad_out.reshape(groups, span, width), groups)
 
@@ -894,7 +894,7 @@
     for gu, (low, high) in zip(gu_home, ff_parts):
         part = (high - low) * groups
         main = part // 128 * 128
-        gu = after(gu, mixer_grads).reshape(team, span, 2 * part)
+        gu = gu.reshape(team, span, 2 * part)
         gate = jnp.concatenate([gu[..., :main], gu[..., 2 * main : part + main]], axis=2)
         up = jnp.concatenate([gu[..., main : 2 * main], gu[..., part + main :]], axis=2)
         for home, v in zip(ff_home, (gate, up)):

time: 752 us -> 758 us (level)
    reduce_scatter x4, waiting for transfers between devices: 16.5 us -> 24.6 us  [group_scatter(): return lax.psum_scatter(v, 'g', scatter_dimension=0, tiled=True)]
    ppermute x21, waiting for transfers between devices: 51.2 us -> 43.6 us  [swap_b(): return lax.ppermute(v, 'b', SWAP)]
    unnamed x138 -> x144, local copies, waits for them, and re-layouts: 23.6 us -> 24.4 us
  transfers between devices with their start and end apart: 89 -> 89, of which waited for: 29 -> 28; matrix products, arithmetic and copies ran while one was open for 29% -> 33% of each run, Pallas kernels for 18% -> 18%
where the time goes in v4:
time: 758 us; the launch traced here: 747 us
  waiting for transfers between devices  183 us (24%)
  Pallas kernels  168 us (22%)
  local copies, waits for them, and re-layouts  119 us (16%)
  starting transfers between devices  112 us (15%)
  other arithmetic  74.3 us (10%)
  matrix products  72.6 us (10%)
  between operations  17.8 us (2%)
    pallas_call x2, Pallas kernels, feed_forward(): pl.pallas_call(ff_first_kernel if more is None else ff_more_kernel, grid=...  68.5 us
    dot_general x8, matrix products, weight_grad(): return jnp.einsum('ra,rb->ab', left, right, preferred_element_type=F32)  58.9 us
    all_to_all x9, starting transfers between devices, team_exchange(): return lax.all_to_all(v, TEAM, 0, 0, tiled=True)  48.3 us
    ppermute x21, waiting for transfers between devices, swap_a(): return lax.ppermute(v, 'a', SWAP)  47 us
    ppermute x21, waiting for transfers between devices, swap_b(): return lax.ppermute(v, 'b', SWAP)  43.6 us
    all_to_all x9, waiting for transfers between devices, team_exchange(): return lax.all_to_all(v, TEAM, 0, 0, tiled=True)  40.5 us
    convert_element_type x12, other arithmetic, plus(): return (left.astype(F32) + right.astype(F32)).astype(BF)  35.8 us
    pallas_call x1, Pallas kernels, delta_backward(): pl.pallas_call(functools.partial(bwd_kernel, heads=heads, size=size, leng...  30.9 us
  transfers between devices with their start and end apart: 89, of which 28 were waited for; matrix products, arithmetic and copies ran while one was open for 33% of the time, Pallas kernels for 18%

profile of v4, /device:TPU:11, one launch (start us, length us, event | category | flops | bytes accessed | tf_op | source)
XLA Modules:
  0.0 747.3 jit_solution(5024946303686389910)
XLA Ops:
  17.6 12.5 %all-to-all-done = bf16[8,64,1024]{2,1,0:T(8,128)(2,1)S(1)} async-done(((bf16[8,64,1024]{2,1,0:T(8,128)(2,1)}), bf16[8,64,1024]{2,1,0:T(8,128)(2,1)S(1)}, u32[]{:S(2)}, u32[]{:S(2)}) %all-to-all-start) | async-done | bytes 1048608 | tf_op jit(solution)/shard_map/all_to_all | solution.py:644
  56.3 14.0 %collective-permute-done.9.refs_4_ = bf16[256,2048]{1,0:T(8,128)(2,1)} collective-permute-done((bf16[256,2048]{1,0:T(8,128)(2,1)S(1)}, bf16[256,2048]{1,0:T(8,128)(2,1)}, u32[]{:S(2)}, u32[]{:S(2)}) %collective-permute-start.9) | collective-permute-done | bytes 1048608 | tf_op jit(solution)/shard_map/ppermute | solution.py:573
  76.5 7.9 %collective-permute-done.11 = bf16[128,2048]{1,0:T(8,128)(2,1)} collective-permute-done((bf16[128,2048]{1,0:T(8,128)(2,1)}, bf16[128,2048]{1,0:T(8,128)(2,1)}, u32[]{:S(2)}, u32[]{:S(2)}) %collective-permute-start.11) | collective-permute-done | bytes 524320 | tf_op jit(solution)/shard_map/ppermute | solution.py:577
  114.3 13.9 %collective-permute-done.14.refs_10_ = bf16[256,2048]{1,0:T(8,128)(2,1)} collective-permute-done((bf16[256,2048]{1,0:T(8,128)(2,1)}, bf16[256,2048]{1,0:T(8,128)(2,1)}, u32[]{:S(2)}, u32[]{:S(2)}) %collective-permute-start.14) | collective-permute-done | bytes 1048608 | tf_op jit(solution)/shard_map/ppermute | solution.py:577
  142.2 18.1 %project.1 = (bf16[2048,2048]{1,0:T(8,128)(2,1)}, f32[2048,1024]{1,0:T(8,128)}, f32[2048,128]{1,0:T(8,128)S(1)}) custom-call(f32[8,2048]{1,0:T(8,128)S(1)} %pad_convert_fusion.gain_ref, bf16[4,640,1024]{2,1,0:T(8,128)(2,1)} %bitcast.186, bf16[2048,128]{1,0:T(8,128)(2,1)S(1)} %pad.35.beta_ref, bf16[256,2048]{1,0:T(8,128)(2,1)S(1)} %bitcast.181, ...), custom_call_target="tpu_custom_call" | custom-call | flops 1073741824 | bytes 4194304 | tf_op jit(solution)/shard_map/project/pallas_call | solution.py:541
  172.5 22.1 %delta_forward.1 = (bf16[8,256,256]{2,1,0:T(8,128)(2,1)S(1)}, f32[8,2,2,128,128]{4,3,2,1,0:T(8,128)S(1)}) custom-call(s32[1]{0:T(128)} %bitcast.1.place_ref, f32[2048,1024]{1,0:T(8,128)} %get-tuple-element.170.pre_ref, f32[2048,128]{1,0:T(8,128)S(1)} %copy-done.5, f32[16,256]{1,0:T(8,128)S(1)} %pad.36.taps_ref, f32[8,128]{1,0:T(8,128)S(1)} %pad_convert_fusion.1.gain_ref), custom_call_target="tpu_custom_call" | custom-call | flops 1600000000 | bytes 2097152 | tf_op jit(solution)/shard_map/delta_forward/pallas_call | solution.py:266
  199.9 8.4 %all-to-all-start.3 = ((bf16[8,256,256]{2,1,0:T(8,128)(2,1)}), bf16[8,256,256]{2,1,0:T(8,128)(2,1)}, u32[]{:S(2)}, u32[]{:S(2)}) async-start(bf16[8,256,256]{2,1,0:T(8,128)(2,1)} %copy-done.9), calls=%async_computation.3 | async-start | bytes 2097152 | tf_op jit(solution)/shard_map/all_to_all | solution.py:644
  209.1 11.9 %all-to-all-done.3 = bf16[8,256,256]{2,1,0:T(8,128)(2,1)} async-done(((bf16[8,256,256]{2,1,0:T(8,128)(2,1)}), bf16[8,256,256]{2,1,0:T(8,128)(2,1)}, u32[]{:S(2)}, u32[]{:S(2)}) %all-to-all-start.3) | async-done | bytes 1048608 | tf_op jit(solution)/shard_map/all_to_all | solution.py:644
  229.9 9.0 %assemble.1 = bf16[4,8,64,2048]{3,2,1,0:T(8,128)(2,1)} custom-call(s32[1]{0:T(128)} %bitcast.1.place_ref, bf16[4,64,2048]{2,1,0:T(8,128)(2,1)} %bitcast.24.refs_0_, bf16[4,64,2048]{2,1,0:T(8,128)(2,1)} %bitcast.25.refs_1_, bf16[4,64,2048]{2,1,0:T(8,128)(2,1)} %bitcast.26.refs_2_, bf16[4,64,2048]{2,1,0:T(8,128)(2,1)} %bitcast.27.refs_3_, ...), custom_call_target="tpu_custom_call" | custom-call | bytes 16777216 | tf_op jit(solution)/shard_map/assemble/pallas_call | solution.py:365
  248.4 21.5 %collective-permute-done.29.refs_4_ = bf16[256,2048]{1,0:T(8,128)(2,1)} collective-permute-done((bf16[256,2048]{1,0:T(8,128)(2,1)S(1)}, bf16[256,2048]{1,0:T(8,128)(2,1)}, u32[]{:S(2)}, u32[]{:S(2)}) %collective-permute-start.29) | collective-permute-done | bytes 1048608 | tf_op jit(solution)/shard_map/ppermute | solution.py:573
  275.4 8.9 %collective-permute-done.31 = bf16[128,2048]{1,0:T(8,128)(2,1)} collective-permute-done((bf16[128,2048]{1,0:T(8,128)(2,1)}, bf16[128,2048]{1,0:T(8,128)(2,1)}, u32[]{:S(2)}, u32[]{:S(2)}) %collective-permute-start.31) | collective-permute-done | bytes 524320 | tf_op jit(solution)/shard_map/ppermute | solution.py:577
  295.8 33.8 %feed_forward.2 = (bf16[2048,2048]{1,0:T(8,128)(2,1)}, bf16[2048,2048]{1,0:T(8,128)(2,1)}, bf16[2048,384]{1,0:T(8,128)(2,1)}, bf16[2048,768]{1,0:T(8,128)(2,1)},...) custom-call(bf16[2048,768]{1,0:T(8,128)(2,1)} %all-gather.15.cloned.1.call-done.gu_ref, ...), custom_call_target="tpu_custom_call" | custom-call | flops 1610612736 | bytes 8388608 | tf_op jit(solution)/shard_map/feed_forward/pallas_call | solution.py:455
  329.6 11.4 %convolution_convert_fusion.3 = bf16[2048,768]{1,0:T(8,128)(2,1)} fusion(bf16[2048,2048]{1,0:T(8,128)(2,1)} %get-tuple-element.194.n_ref, bf16[2048,768]{1,0:T(8,128)(2,1)} %get-tuple-element.198), kind=kOutput, calls=%fused_computation.3 | convolution fusion | flops 6444023808 | bytes 14680064 | tf_op jit(solution)/shard_map/ra,rb->ab/dot_general | solution.py:652
  341.0 34.7 %feed_forward.3 = (bf16[2048,320]{1,0:T(8,128)(2,1)}, bf16[2048,640]{1,0:T(8,128)(2,1)}, bf16[1024,2048]{1,0:T(8,128)(2,1)}, bf16[1024,2048]{1,0:T(8,128)(2,1)},...) custom-call(bf16[2048,640]{1,0:T(8,128)(2,1)} %all-gather.11.cloned.1.call-done.gu_ref, ...), custom_call_target="tpu_custom_call" | custom-call | flops 1342177280 | bytes 8388608 | tf_op jit(solution)/shard_map/feed_forward/pallas_call | solution.py:455
  376.6 11.1 %convolution_convert_fusion.4 = bf16[2048,640]{1,0:T(8,128)(2,1)} fusion(bf16[2048,2048]{1,0:T(8,128)(2,1)} %get-tuple-element.194.n_ref, bf16[2048,640]{1,0:T(8,128)(2,1)} %get-tuple-element.210), kind=kOutput, calls=%fused_computation.4 | convolution fusion | flops 5370019840 | bytes 13631488 | tf_op jit(solution)/shard_map/ra,rb->ab/dot_general | solution.py:652
  410.4 8.7 %collective-permute-done.41 = bf16[128,2048]{1,0:T(8,128)(2,1)} collective-permute-done((bf16[128,2048]{1,0:T(8,128)(2,1)S(1)}, bf16[128,2048]{1,0:T(8,128)(2,1)}, u32[]{:S(2)}, u32[]{:S(2)}) %collective-permute-start.41) | collective-permute-done | bytes 524320 | tf_op jit(solution)/shard_map/ppermute | solution.py:573
  420.0 16.6 %reduce-scatter.5.cloned.1.call-done = bf16[512,768]{1,0:T(8,128)(2,1)} async-done(((bf16[2048,768]{1,0:T(8,128)(2,1)}), bf16[512,768]{1,0:T(8,128)(2,1)}) %reduce-scatter.5.cloned.1.call-update) | async-done | bytes 786448 | tf_op jit(solution)/shard_map/reduce_scatter | solution.py:697
  443.1 8.2 %collective-permute-done.43 = bf16[128,2048]{1,0:T(8,128)(2,1)S(1)} collective-permute-done((bf16[128,2048]{1,0:T(8,128)(2,1)S(1)}, bf16[128,2048]{1,0:T(8,128)(2,1)S(1)}, u32[]{:S(2)}, u32[]{:S(2)}) %collective-permute-start.43) | collective-permute-done | bytes 524320 | tf_op jit(solution)/shard_map/ppermute | solution.py:577
  507.5 30.9 %delta_backward.1 = (bf16[2048,1024]{1,0:T(8,128)(2,1)}, bf16[2048,128]{1,0:T(8,128)(2,1)S(1)}, f32[16,256]{1,0:T(8,128)S(1)}, f32[8,128]{1,0:T(8,128)S(1)}) custom-call(s32[1]{0:T(128)} %bitcast.1.place_ref, f32[2048,1024]{1,0:T(8,128)} %get-tuple-element.170.pre_ref, f32[2048,128]{1,0:T(8,128)S(1)} %copy-done.6, f32[16,256]{1,0:T(8,128)S(1)} %pad.36.taps_ref, ...), custom_call_target="tpu_custom_call" | custom-call | flops 1600000000 | bytes 2097152 | tf_op jit(solution)/shard_map/delta_backward/pallas_call | solution.py:298
  544.6 13.0 %convolution_convert_fusion.2 = bf16[2048,1024]{1,0:T(8,128)(2,1)} fusion(bf16[2048,2048]{1,0:T(8,128)(2,1)S(1)} %bitcast.189, bf16[2048,1024]{1,0:T(8,128)(2,1)} %get-tuple-element.247.dpre_ref), kind=kOutput, calls=%fused_computation.2 | convolution fusion | flops 8592031744 | bytes 16777216 | tf_op jit(solution)/shard_map/ra,rb->ab/dot_general | solution.py:652
  573.5 19.3 %pull_projections.1 = (bf16[1024,2048]{1,0:T(8,128)(2,1)}, bf16[1024,2048]{1,0:T(8,128)(2,1)}, f32[8,2048]{1,0:T(8,128)S(1)}) custom-call(bf16[2048,1024]{1,0:T(8,128)(2,1)} %get-tuple-element.247.dpre_ref, bf16[2048,128]{1,0:T(8,128)(2,1)S(1)} %get-tuple-element.248.dbeta_ref, bf16[4,640,1024]{2,1,0:T(8,128)(2,1)} %bitcast.187, ...), custom_call_target="tpu_custom_call" | custom-call | flops 1073741824 | bytes 4194304 | tf_op jit(solution)/shard_map/pull_projections/pallas_call | solution.py:497
  628.7 7.9 %reduce-scatter.11.cloned.1.call-done = bf16[512,1024]{1,0:T(8,128)(2,1)} async-done(((bf16[2048,1024]{1,0:T(8,128)(2,1)}), bf16[512,1024]{1,0:T(8,128)(2,1)}) %reduce-scatter.11.cloned.1.call-update) | async-done | bytes 1048592 | tf_op jit(solution)/shard_map/reduce_scatter | solution.py:697
  655.4 8.6 %all-to-all-done.7 = f32[8,1,1152]{2,1,0:T(1,128)S(1)} async-done(((f32[8,1,1152]{2,1,0:T(1,128)}), f32[8,1,1152]{2,1,0:T(1,128)S(1)}, u32[]{:S(2)}, u32[]{:S(2)}) %all-to-all-start.7) | async-done | bytes 36896 | tf_op jit(solution)/shard_map/all_to_all | solution.py:644
  704.6 16.4 %collective-permute-done.70 = bf16[64,2048]{1,0:T(8,128)(2,1)S(1)} collective-permute-done((bf16[64,2048]{1,0:T(8,128)(2,1)S(1)}, bf16[64,2048]{1,0:T(8,128)(2,1)S(1)}, u32[]{:S(2)}, u32[]{:S(2)}) %collective-permute-start.70) | collective-permute-done | bytes 262176 | tf_op jit(solution)/shard_map/ppermute | solution.py:691
  (502 shorter events, 360.5 us)
Async XLA Ops:
  17.5 116.9 %all-gather.9.cloned.1.call-start = ((), (), s32[]{:S(2)}) async-start(), calls=%async_computation.17 | async-start | bytes 6553600 | tf_op jit(solution)/shard_map/all_gather | solution.py:701
  47.6 52.0 %collective-permute-start.6 = (bf16[256,2048]{1,0:T(8,128)(2,1)S(1)}, bf16[256,2048]{1,0:T(8,128)(2,1)S(1)}, u32[]{:S(2)}, u32[]{:S(2)}) collective-permute-start(bf16[256,2048]{1,0:T(8,128)(2,1)S(1)} %bitcast.180), channel_id=1, source_target_pairs={{0,1},{1,0},{2,3},{3,2},{4,5},{5,4},{6,7},{7,6},{8,9},{9,8},{10,11... | collective-permute-start | bytes 3145736 | tf_op jit(solution)/shard_map/ppermute | solution.py:581
  114.1 176.1 %all-gather.13.cloned.1.call-start = ((), (), s32[]{:S(2)}) async-start(), calls=%async_computation.19 | async-start | bytes 3604480 | tf_op jit(solution)/shard_map/all_gather | solution.py:701
  164.5 30.2 %collective-permute-start.18 = (bf16[128,2048]{1,0:T(8,128)(2,1)}, bf16[128,2048]{1,0:T(8,128)(2,1)}, u32[]{:S(2)}, u32[]{:S(2)}) collective-permute-start(bf16[128,2048]{1,0:T(8,128)(2,1)} %slice.343), channel_id=1, source_target_pairs={{0,2},{2,0},{1,3},{3,1},{4,6},{6,4},{5,7},{7,5},{8,10},{10,8},{9,1... | collective-permute-start | bytes 1572872 | tf_op jit(solution)/shard_map/ppermute | solution.py:577
  208.4 87.1 %all-gather.15.cloned.1.call-start = ((), (), s32[]{:S(2)}) async-start(), calls=%async_computation.20 | async-start | bytes 3932160 | tf_op jit(solution)/shard_map/all_gather | solution.py:701
  209.1 132.0 %all-gather.11.cloned.1.call-start = ((), (), s32[]{:S(2)}) async-start(), calls=%async_computation.18 | async-start | bytes 3276800 | tf_op jit(solution)/shard_map/all_gather | solution.py:701
  246.9 42.5 %collective-permute-start.34 = (bf16[256,2048]{1,0:T(8,128)(2,1)}, bf16[256,2048]{1,0:T(8,128)(2,1)}, u32[]{:S(2)}, u32[]{:S(2)}) collective-permute-start(bf16[256,2048]{1,0:T(8,128)(2,1)} %bitcast_convert_fusion.refs_8_), channel_id=1, source_target_pairs={{0,1},{1,0},{2,3},{3,2},{4,5},{5,4},{6,7},{7,6},{8,9},{9,8},{10,11... | collective-permute-start | bytes 3145736 | tf_op jit(solution)/shard_map/ppermute | solution.py:581
  247.9 41.8 %collective-permute-start.35 = (bf16[256,2048]{1,0:T(8,128)(2,1)}, bf16[256,2048]{1,0:T(8,128)(2,1)}, u32[]{:S(2)}, u32[]{:S(2)}) collective-permute-start(bf16[256,2048]{1,0:T(8,128)(2,1)} %collective-permute-done.14.refs_10_), channel_id=1, source_target_pairs={{0,1},{1,0},{2,3},{3,2},{4,5},{5,4},{6,7},{7,6},{8,9},{9,8},{10,11... | collective-permute-start | bytes 3145736 | tf_op jit(solution)/shard_map/ppermute | solution.py:581
  247.9 42.0 %collective-permute-start.36 = (bf16[256,2048]{1,0:T(8,128)(2,1)}, bf16[256,2048]{1,0:T(8,128)(2,1)}, u32[]{:S(2)}, u32[]{:S(2)}) collective-permute-start(bf16[256,2048]{1,0:T(8,128)(2,1)} %collective-permute-done.15.refs_12_), channel_id=1, source_target_pairs={{0,1},{1,0},{2,3},{3,2},{4,5},{5,4},{6,7},{7,6},{8,9},{9,8},{10,11... | collective-permute-start | bytes 3145736 | tf_op jit(solution)/shard_map/ppermute | solution.py:581
  275.2 161.4 %reduce-scatter.5.cloned.1.call-start = ((), (), s32[]{:S(2)}) async-start(), calls=%async_computation.13 | async-start | bytes 3932160 | tf_op jit(solution)/shard_map/reduce_scatter | solution.py:697
  376.1 186.0 %reduce-scatter.9.cloned.1.call-start = ((), (), s32[]{:S(2)}) async-start(), calls=%async_computation.15 | async-start | bytes 3604480 | tf_op jit(solution)/shard_map/reduce_scatter | solution.py:697
  436.6 127.9 %reduce-scatter.7.cloned.1.call-start = ((), (), s32[]{:S(2)}) async-start(), calls=%async_computation.14 | async-start | bytes 3276800 | tf_op jit(solution)/shard_map/reduce_scatter | solution.py:697
  442.0 44.8 %collective-permute-start.46 = (bf16[1024,2048]{1,0:T(8,128)(2,1)}, bf16[1024,2048]{1,0:T(8,128)(2,1)}, u32[]{:S(2)}, u32[]{:S(2)}) collective-permute-start(bf16[1024,2048]{1,0:T(8,128)(2,1)} %get-tuple-element.230), channel_id=1, source_target_pairs={{0,1},{1,0},{2,3},{3,2},{4,5},{5,4},{6,7},{7,6},{8,9},{9,8},{10,11... | collective-permute-start | bytes 12582920 | tf_op jit(solution)/shard_map/ppermute | solution.py:581
  459.8 41.7 %collective-permute-start.45 = (bf16[1024,2048]{1,0:T(8,128)(2,1)}, bf16[1024,2048]{1,0:T(8,128)(2,1)}, u32[]{:S(2)}, u32[]{:S(2)}) collective-permute-start(bf16[1024,2048]{1,0:T(8,128)(2,1)} %convolution_convert_fusion), channel_id=1, source_target_pairs={{0,1},{1,0},{2,3},{3,2},{4,5},{5,4},{6,7},{7,6},{8,9},{9,8},{10,11... | collective-permute-start | bytes 12582920 | tf_op jit(solution)/shard_map/ppermute | solution.py:581
  481.4 155.2 %reduce-scatter.11.cloned.1.call-start = ((), (), s32[]{:S(2)}) async-start(), calls=%async_computation.16 | async-start | bytes 5242880 | tf_op jit(solution)/shard_map/reduce_scatter | solution.py:697
  496.6 41.8 %collective-permute-start.47 = (bf16[128,2048]{1,0:T(8,128)(2,1)}, bf16[128,2048]{1,0:T(8,128)(2,1)}, u32[]{:S(2)}, u32[]{:S(2)}) collective-permute-start(bf16[128,2048]{1,0:T(8,128)(2,1)} %get-tuple-element.391), channel_id=1, source_target_pairs={{0,4},{4,0},{1,5},{5,1},{2,6},{6,2},{3,7},{7,3},{8,12},{12,8},{9,1... | collective-permute-start | bytes 1572872 | tf_op jit(solution)/shard_map/ppermute | solution.py:573
  497.6 40.8 %collective-permute-start.48 = (bf16[128,2048]{1,0:T(8,128)(2,1)}, bf16[128,2048]{1,0:T(8,128)(2,1)}, u32[]{:S(2)}, u32[]{:S(2)}) collective-permute-start(bf16[128,2048]{1,0:T(8,128)(2,1)} %get-tuple-element.390), channel_id=1, source_target_pairs={{0,2},{2,0},{1,3},{3,1},{4,6},{6,4},{5,7},{7,5},{8,10},{10,8},{9,1... | collective-permute-start | bytes 1572872 | tf_op jit(solution)/shard_map/ppermute | solution.py:577
  499.7 38.7 %collective-permute-start.49 = (bf16[128,2048]{1,0:T(8,128)(2,1)}, bf16[128,2048]{1,0:T(8,128)(2,1)}, u32[]{:S(2)}, u32[]{:S(2)}) collective-permute-start(bf16[128,2048]{1,0:T(8,128)(2,1)} %get-tuple-element.388), channel_id=1, source_target_pairs={{0,4},{4,0},{1,5},{5,1},{2,6},{6,2},{3,7},{7,3},{8,12},{12,8},{9,1... | collective-permute-start | bytes 1572872 | tf_op jit(solution)/shard_map/ppermute | solution.py:573
  501.0 37.4 %collective-permute-start.50 = (bf16[128,2048]{1,0:T(8,128)(2,1)}, bf16[128,2048]{1,0:T(8,128)(2,1)}, u32[]{:S(2)}, u32[]{:S(2)}) collective-permute-start(bf16[128,2048]{1,0:T(8,128)(2,1)} %get-tuple-element.386), channel_id=1, source_target_pairs={{0,2},{2,0},{1,3},{3,1},{4,6},{6,4},{5,7},{7,5},{8,10},{10,8},{9,1... | collective-permute-start | bytes 1572872 | tf_op jit(solution)/shard_map/ppermute | solution.py:577
  637.7 35.6 %collective-permute-start.58 = (bf16[128,2048]{1,0:T(8,128)(2,1)}, bf16[128,2048]{1,0:T(8,128)(2,1)}, u32[]{:S(2)}, u32[]{:S(2)}) collective-permute-start(bf16[128,2048]{1,0:T(8,128)(2,1)} %get-tuple-element.379), channel_id=1, source_target_pairs={{0,4},{4,0},{1,5},{5,1},{2,6},{6,2},{3,7},{7,3},{8,12},{12,8},{9,1... | collective-permute-start | bytes 1572872 | tf_op jit(solution)/shard_map/ppermute | solution.py:573
  638.0 35.3 %collective-permute-start.59 = (bf16[128,2048]{1,0:T(8,128)(2,1)}, bf16[128,2048]{1,0:T(8,128)(2,1)}, u32[]{:S(2)}, u32[]{:S(2)}) collective-permute-start(bf16[128,2048]{1,0:T(8,128)(2,1)} %get-tuple-element.378), channel_id=1, source_target_pairs={{0,2},{2,0},{1,3},{3,1},{4,6},{6,4},{5,7},{7,5},{8,10},{10,8},{9,1... | collective-permute-start | bytes 1572872 | tf_op jit(solution)/shard_map/ppermute | solution.py:577
  664.1 60.9 %all-to-all-start.8 = ((bf16[8,64,1024]{2,1,0:T(8,128)(2,1)}), bf16[8,64,1024]{2,1,0:T(8,128)(2,1)S(1)}, u32[]{:S(2)}, u32[]{:S(2)}) async-start(bf16[8,64,1024]{2,1,0:T(8,128)(2,1)} %bitcast.217), calls=%async_computation.12 | async-start | bytes 2097152 | tf_op jit(solution)/shard_map/all_to_all | solution.py:644
  701.3 32.6 %collective-permute-start.64 = (bf16[128,2048]{1,0:T(8,128)(2,1)S(1)}, bf16[128,2048]{1,0:T(8,128)(2,1)}, u32[]{:S(2)}, u32[]{:S(2)}) collective-permute-start(bf16[128,2048]{1,0:T(8,128)(2,1)S(1)} %add_convert_fusion.14), channel_id=1, source_target_pairs={{0,2},{2,0},{1,3},{3,1},{4,6},{6,4},{5,7},{7,5},{8,10},{10,8},{9,1... | collective-permute-start | bytes 1572872 | tf_op jit(solution)/shard_map/ppermute | solution.py:577
  703.8 31.6 %collective-permute-start.65 = (bf16[128,2048]{1,0:T(8,128)(2,1)S(1)}, bf16[128,2048]{1,0:T(8,128)(2,1)}, u32[]{:S(2)}, u32[]{:S(2)}) collective-permute-start(bf16[128,2048]{1,0:T(8,128)(2,1)S(1)} %add_convert_fusion.13), channel_id=1, source_target_pairs={{0,4},{4,0},{1,5},{5,1},{2,6},{6,2},{3,7},{7,3},{8,12},{12,8},{9,1... | collective-permute-start | bytes 1572872 | tf_op jit(solution)/shard_map/ppermute | solution.py:573
  (129 other events, 1545.2 us)
Sparse Core Ops, SparseCore 0:
  31.4 98.6 all-gather.8
  134.5 58.0 all-gather.12
  210.8 61.8 all-gather.14
  275.3 54.1 all-gather.10
  376.2 60.3 reduce-scatter.4
  438.8 56.0 reduce-scatter.8
  497.1 51.6 reduce-scatter.6
  557.8 78.8 reduce-scatter.10
